TPU v7x, 32 devices: a whole 2x2x4 slice. The times are simulated.
32 devices in a mesh: dp: 4 (over y, core), seq: 8 (over z, x).
Axes of the slice: x: 2, y: 2, z: 4, core: 2. Of those that a mesh axis runs over, the one named last changes fastest.
Arguments:
- queries: bfloat16 [4, 8192, 128], P('dp', 'seq'), may hold values from -6 to 6
- key_vectors: bfloat16 [4, 8192, 128], P('dp', 'seq'), may hold values from -6 to 6
- value_vectors: bfloat16 [4, 8192, 128], P('dp', 'seq'), may hold values from -6 to 6
- out_grad: bfloat16 [4, 8192, 128], P('dp', 'seq'), may hold values from -6 to 6
- log_decay: float32 [4, 1, 8192], P('dp', None, 'seq'), may hold values from -0.8 to 0, as said below
- prev_grads: bfloat16 [4, 256, 6144], P('dp', 'seq'), may hold values from -6 to 6
Outputs:
- attn_out: bfloat16 [4, 8192, 128], P('dp', 'seq')
- grad_query: bfloat16 [4, 8192, 128], P('dp', 'seq')
- grad_key: bfloat16 [4, 8192, 128], P('dp', 'seq')
- grad_value: bfloat16 [4, 8192, 128], P('dp', 'seq')
- grad_shard: float32 [256, 6144], P('seq', 'dp')
Inputs may be any that keep to these rules, and one draw needn't show every extreme that they name: `log_decay`: every entry is negative.
All inputs are finite; a program needn't handle non-finite values.
Results may differ from a plain program's by a relative error of at most 0.012.
Values may be sent and summed in bfloat16 or wider, within the bound.
No kernel may reach another device: no remote copies, remote signals or barrier semaphores. Data moves between devices by JAX's collectives and lax.ppermute only.
A program may use at most 64 MiB of HBM per device.

v0:
```python
import jax
import jax.numpy as jnp
from jax import lax
from jax.sharding import PartitionSpec as P

BLK = 512


NORM_EPS = 1e-06
FULL_PRECISION = lax.Precision.HIGHEST


def product(left, right):
    return jnp.dot(left, right, precision=FULL_PRECISION, preferred_element_type=jnp.float32)


def decay_mask(running):
    spread = running[:, None] - running[None, :]
    lower_mask = jnp.tril(jnp.ones(spread.shape, dtype=bool))
    return jnp.where(lower_mask, jnp.exp(jnp.minimum(spread, 0.0)), 0.0)


def forward_local(query_head, key_head, value_head, decay_head):
    head_width = query_head.shape[-1]

    def advance(carried, block_inputs):
        query_block, key_block, value_block, decay_block = block_inputs
        running = jnp.cumsum(decay_block)
        scores = jnp.dot(query_block, key_block.T, preferred_element_type=jnp.float32) * decay_mask(
            running
        )
        query_wide = query_block.astype(jnp.float32)
        key_wide = key_block.astype(jnp.float32)
        value_wide = value_block.astype(jnp.float32)
        block_out = product(scores, value_wide) + jnp.exp(running)[:, None] * product(
            query_wide, carried
        )
        weights = jnp.exp(running[-1] - running)
        updated = jnp.exp(running[-1]) * carried + product(
            (key_wide * weights[:, None]).T, value_wide
        )
        return (updated, (block_out, carried))

    return lax.scan(
        advance,
        jnp.zeros((head_width, head_width), jnp.float32),
        (query_head, key_head, value_head, decay_head),
    )


def backward_local(query_head, key_head, value_head, dattn_head, decay_head, start_head):
    head_width = query_head.shape[-1]

    def retreat(later_sum, block_inputs):
        query_block, key_block, value_block, dattn_block, decay_block, carried = block_inputs
        running = jnp.cumsum(decay_block)
        decay_weights = decay_mask(running)
        scores = (
            jnp.dot(query_block, key_block.T, preferred_element_type=jnp.float32) * decay_weights
        )
        query_wide = query_block.astype(jnp.float32)
        key_wide = key_block.astype(jnp.float32)
        value_wide = value_block.astype(jnp.float32)
        dscores = product(dattn_block, value_wide.T) * decay_weights
        lead_decay = jnp.exp(running)[:, None]
        tail_decay = jnp.exp(running[-1] - running)[:, None]
        grad_q = product(dscores, key_wide) + lead_decay * product(dattn_block, carried.T)
        grad_k = product(dscores.T, query_wide) + tail_decay * product(value_wide, later_sum.T)
        grad_v = product(scores.T, dattn_block) + tail_decay * product(key_wide, later_sum)
        updated = jnp.exp(running[-1]) * later_sum + product(
            (query_wide * lead_decay).T, dattn_block
        )
        return (updated, (grad_q, grad_k, grad_v))

    return lax.scan(
        retreat,
        jnp.zeros((head_width, head_width), jnp.float32),
        (query_head, key_head, value_head, dattn_head, decay_head, start_head),
        reverse=True,
    )


def weigh_fold(block_logs, own_index, upward, running_sum, shard_part):
    summed_logs = jnp.cumsum(block_logs, axis=0)
    own_cum = lax.dynamic_index_in_dim(summed_logs, own_index, 0, keepdims=False)
    own_log = lax.dynamic_index_in_dim(block_logs, own_index, 0, keepdims=False)
    piece_count = shard_part.shape[0]
    token_offsets = jnp.arange(piece_count, dtype=jnp.int32)
    if upward:
        spread = summed_logs - block_logs - own_cum[None, :]
        usable = token_offsets > own_index
    else:
        spread = own_cum[None, :] - own_log[None, :] - summed_logs
        usable = token_offsets < own_index
    weights = jnp.where(usable[:, None], jnp.exp(jnp.minimum(spread, 0.0)), 0.0)
    return running_sum + jnp.einsum("nh,nhab->hab", weights, shard_part, precision=FULL_PRECISION)


def local(queries, key_vectors, value_vectors, out_grad, log_decay, prev_grads):
    row_count = queries.shape[1]
    head_count = log_decay.shape[1]
    head_width = queries.shape[2] // head_count
    block_count = row_count // BLK

    def by_head(tensor):
        return tensor[0].reshape(row_count, head_count, head_width).transpose(1, 0, 2)

    def by_block(tensor):
        return tensor.reshape(head_count, block_count, BLK, head_width)

    def to_rows(tensor):
        return (
            tensor.transpose(1, 0, 2)
            .reshape(1, row_count, head_count * head_width)
            .astype(jnp.bfloat16)
        )

    query_heads = by_head(queries)
    key_heads = by_head(key_vectors)
    value_heads = by_head(value_vectors)
    decay_rows = log_decay[0]
    decay_blocks = decay_rows.reshape(head_count, block_count, BLK)
    cumulative = jnp.cumsum(decay_rows, axis=1)
    log_total = cumulative[:, -1]
    local_state, (local_out, block_starts) = jax.vmap(forward_local)(
        by_block(query_heads), by_block(key_heads), by_block(value_heads), decay_blocks
    )
    identity = (
        jnp.zeros((head_count,), jnp.float32),
        jnp.zeros((head_count, head_width, head_width), jnp.float32),
    )
    own_index = lax.axis_index("seq")
    block_logs = lax.all_gather(log_total[None], "seq", axis=0, tiled=True)
    incoming = weigh_fold(
        block_logs,
        own_index,
        False,
        identity[1],
        lax.all_gather(local_state[None].astype(jnp.bfloat16), "seq", axis=0, tiled=True).astype(
            jnp.float32
        ),
    )
    query_wide = query_heads.astype(jnp.float32)
    key_wide = key_heads.astype(jnp.float32)
    value_wide = value_heads.astype(jnp.float32)
    lead_decay = jnp.exp(cumulative)[:, :, None]
    attention = local_out.reshape(head_count, row_count, head_width) + lead_decay * jnp.einsum(
        "hta,hab->htb", query_wide, incoming, precision=FULL_PRECISION
    )
    norm_ratio = lax.rsqrt(jnp.mean(attention * attention, axis=-1, keepdims=True) + NORM_EPS)
    attn_out = to_rows(attention * norm_ratio)
    cotangent = by_head(out_grad).astype(jnp.float32)
    cubed = norm_ratio * norm_ratio * norm_ratio
    dattn = (
        norm_ratio * cotangent
        - cubed / head_width * jnp.sum(cotangent * attention, axis=-1, keepdims=True) * attention
    )
    local_future, (grad_q_local, grad_k_local, grad_v_local) = jax.vmap(backward_local)(
        by_block(query_heads),
        by_block(key_heads),
        by_block(value_heads),
        by_block(dattn),
        decay_blocks,
        block_starts,
    )
    outgoing = weigh_fold(
        block_logs,
        own_index,
        True,
        identity[1],
        lax.all_gather(local_future[None].astype(jnp.bfloat16), "seq", axis=0, tiled=True).astype(
            jnp.float32
        ),
    )
    tail_decay = jnp.exp(log_total[:, None] - cumulative)[:, :, None]
    grad_query = grad_q_local.reshape(head_count, row_count, head_width) + lead_decay * jnp.einsum(
        "htb,hab->hta", dattn, incoming, precision=FULL_PRECISION
    )
    grad_key = grad_k_local.reshape(head_count, row_count, head_width) + tail_decay * jnp.einsum(
        "htb,hab->hta", value_wide, outgoing, precision=FULL_PRECISION
    )
    grad_value = grad_v_local.reshape(head_count, row_count, head_width) + tail_decay * jnp.einsum(
        "hta,hab->htb", key_wide, outgoing, precision=FULL_PRECISION
    )
    summed = lax.psum_scatter(
        prev_grads.astype(jnp.float32).astype(jnp.bfloat16), "dp", scatter_dimension=2, tiled=True
    ).astype(jnp.float32)
    return (attn_out, to_rows(grad_query), to_rows(grad_key), to_rows(grad_value), summed[0])


def solution(mesh):
    return jax.shard_map(
        local,
        mesh=mesh,
        in_specs=(
            P("dp", "seq", None),
            P("dp", "seq", None),
            P("dp", "seq", None),
            P("dp", "seq", None),
            P("dp", None, "seq"),
            P("dp", "seq", None),
        ),
        out_specs=(
            P("dp", "seq", None),
            P("dp", "seq", None),
            P("dp", "seq", None),
            P("dp", "seq", None),
            P("seq", "dp"),
        ),
        check_vma=False,
    )
```

profile of v0, /device:TPU:0, one launch (start us, length us, event | category | flops | bytes accessed | tf_op | source)
XLA Modules:
  0.0 152.5 jit_solution(18022749642854145533)
XLA Ops:
  7.2 0.7 reduce-scatter.2.cloned.1.call-update
  8.0 0.7 copy-done.6
  9.1 0.6 slice.60
  10.0 0.6 slice.61
  10.6 0.6 dynamic-slice
  12.5 0.7 bitcast_dynamic-update-slice_fusion.1
  13.2 23.1 %all-reduce = f32[8]{0:T(128)S(1)} all-reduce(f32[8]{0:T(128)S(1)} %bitcast_dynamic-update-slice_fusion.1), channel_id=1, replica_groups=mesh['dp'=4,'seq'=8] {'seq'}, use_global_device_ids=true, to_apply=%add | all-reduce | flops 8 | bytes 64
  36.3 0.7 subtract_exponential_fusion.2
  37.2 0.7 copy-done.2
  38.2 10.3 %while.36 = (s32[]{:T(128)}, f32[1,128,128]{2,1,0:T(8,128)S(1)}, f32[2,1,512,128]{3,2,1,0:T(8,128)S(1)}, f32[2,1,128,128]{3,2,1,0:T(8,128)S(1)}, f32[2,1,512]{2,...) while((s32[]{:T(128)}, f32[1,128,128]{2,1,0:T(8,128)S(1)}, ...), condition=%wide.region_3.4_spmd.clone, body=%wide.region_0.3_spmd.clone.sunk | while | flops 672809472 | bytes 4030787 | solution.py:44
  38.2 0.3 reduce-window.52
  38.5 0.6 slice.78
  39.5 0.6 slice.79
  41.5 0.3 convolution_multiply_fusion.14
  41.8 0.6 fusion.196
  42.7 0.5 fusion.195
  43.3 0.3 reduce-window.52
  43.6 0.6 slice.78
  44.7 0.6 slice.79
  46.7 0.3 convolution_multiply_fusion.14
  47.0 0.6 fusion.196
  47.9 0.5 fusion.195
  48.5 30.7 %all-gather = bf16[8,128,128]{2,1,0:T(8,128)(2,1)S(1)} all-gather(bf16[1,128,128]{2,1,0:T(8,128)(2,1)S(1)} %convert_element_type.117), channel_id=2, replica_groups=mesh['dp'=4,'seq'=8] {'seq'}, dimensions={0}, use_global_device_ids=true | all-gather | bytes 294912 | tf_op jit(solution)/shard_map/all_gather | solution.py:139
  79.4 0.6 dynamic-slice.1
  80.2 1.2 fusion.140
  81.4 1.1 fusion.112
  82.5 0.5 fusion.104
  83.2 0.8 copy.32
  84.4 22.2 %while.37 = (s32[]{:T(128)}, f32[1,128,128]{2,1,0:T(8,128)S(1)}, f32[2,1,512,128]{3,2,1,0:T(8,128)S(1)}, f32[2,1,512,128]{3,2,1,0:T(8,128)S(1)}, f32[2,1,512,128...) while((s32[]{:T(128)}, f32[1,128,128]{2,1,0:T(8,128)S(1)}, ...), condition=%wide.region_12.13_spmd.clone, body=%wide.region_9.12_spmd.clone.sunk | while | flops 2083668480 | bytes 10596742 | solution.py:75
  84.4 0.3 reduce-window.54
  84.7 0.6 slice.82
  85.5 0.8 reduce-window.55
  86.3 0.7 slice_bitcast_fusion.6
  87.0 0.7 slice.83
  89.1 0.7 convolution_multiply_fusion.15
  89.8 1.0 fusion.219
  90.8 0.6 fusion.217
  91.7 0.4 fusion.218
  92.1 0.3 fusion.220
  92.4 0.3 convolution_multiply_fusion.16
  92.7 1.8 %fusion.221 = f32[512,128]{1,0:T(8,128)S(1)} fusion(f32[512,512]{1,0:T(8,128)S(1)} %convolution_multiply_fusion.16, f32[2,1,512,128]{3,2,1,0:T(8,128)S(1)} %get-tuple-element.629, s32[]{:T(128)S(6)} %sub.232), kind=kOutput, calls=%fused_computation.59.clone.1 | convolution fusion | flops 402653184 | bytes 1572868 | tf_op jit(solution)/shard_map/vmap()/while/body/eval_jaxpr/dot_general | solution.py:14
  94.8 0.7 fusion.216
  95.6 0.3 reduce-window.54
  95.9 0.6 slice.82
  96.6 0.8 reduce-window.55
  97.4 0.7 slice_bitcast_fusion.6
  98.1 0.7 slice.83
  100.2 0.6 convolution_multiply_fusion.15
  100.9 1.0 fusion.219
  101.9 0.6 fusion.217
  102.8 0.4 fusion.218
  103.2 0.3 fusion.220
  103.5 0.3 convolution_multiply_fusion.16
  103.8 1.8 %fusion.221 = f32[512,128]{1,0:T(8,128)S(1)} fusion(f32[512,512]{1,0:T(8,128)S(1)} %convolution_multiply_fusion.16, f32[2,1,512,128]{3,2,1,0:T(8,128)S(1)} %get-tuple-element.629, s32[]{:T(128)S(6)} %sub.232), kind=kOutput, calls=%fused_computation.59.clone.1 | convolution fusion | flops 402653184 | bytes 1572868 | tf_op jit(solution)/shard_map/vmap()/while/body/eval_jaxpr/dot_general | solution.py:14
  105.9 0.7 fusion.216
  106.9 30.9 %all-gather.1 = bf16[8,128,128]{2,1,0:T(8,128)(2,1)S(1)} all-gather(bf16[1,128,128]{2,1,0:T(8,128)(2,1)S(1)} %convert_element_type.124), channel_id=3, replica_groups=mesh['dp'=4,'seq'=8] {'seq'}, dimensions={0}, use_global_device_ids=true | all-gather | bytes 294912 | tf_op jit(solution)/shard_map/all_gather | solution.py:171
  137.8 0.7 copy-done.9
  138.5 1.1 fusion.110
  139.6 0.4 fusion.100
  140.0 0.8 copy.34
  141.1 0.4 fusion.101
  141.5 0.8 copy.33
  142.3 1.7 %fusion.102 = bf16[1,1024,128]{2,1,0:T(8,128)(2,1)} fusion(f32[1024,128]{1,0:T(8,128)S(1)} %bitcast.339, f32[128,128]{1,0:T(8,128)S(1)} %bitcast.344, f32[1,1024,128]{1,2,0:T(8,128)S(1)} %fusion.103, f32[1024]{0:T(1024)S(1)} %get-tuple-element.430), kind=kOutput, calls=%fused_computation.129 | convolution fusion | flops 201719808 | bytes 1380352 | tf_op jit(solution)/shard_map/htb,hab->hta/dot_general | solution.py:176
  144.1 1.6 %bitcast_convert_fusion = f32[32,1536]{1,0:T(8,128)} fusion(bf16[1,32,1536]{2,1,0:T(8,128)(2,1)} %reduce-scatter.2.cloned.1.call-done), kind=kLoop, calls=%fused_computation.145 | loop fusion | flops 49152 | bytes 294912 | tf_op jit(solution)/shard_map/squeeze | solution.py:188
  (82 shorter events, 6.0 us)
Async XLA Ops:
  7.2 29.8 %copy-start.5 = (bf16[1,1024,128]{2,1,0:T(8,128)(2,1)S(1)}, bf16[1,1024,128]{2,1,0:T(8,128)(2,1)}, u32[]{:S(2)}) copy-start(bf16[1,1024,128]{2,1,0:T(8,128)(2,1)} %param.13) | copy-start | bytes 786436
  7.2 136.9 %reduce-scatter.2.cloned.1.call-start = ((), (), s32[]{:S(2)}) async-start(), calls=%async_computation.1 | async-start | bytes 491520 | tf_op jit(solution)/shard_map/reduce_scatter | solution.py:185
  8.0 0.7 copy-start.6
  10.0 0.7 copy-start.12
  36.3 43.7 %copy-start.10 = (f32[8]{0:T(128)}, f32[8]{0:T(128)S(1)}, u32[]{:S(2)}) copy-start(f32[8]{0:T(128)S(1)} %all-reduce) | copy-start | bytes 100
  37.0 1.0 copy-start.2
  37.1 1.0 copy-start
  37.1 1.0 copy-start.1
  48.5 30.8 %copy-start.3 = (f32[2,1,128,128]{3,2,1,0:T(8,128)}, f32[2,1,128,128]{3,2,1,0:T(8,128)S(1)}, u32[]{:S(2)}) copy-start(f32[2,1,128,128]{3,2,1,0:T(8,128)S(1)} %get-tuple-element.604) | copy-start | bytes 393220
  80.2 1.2 copy-start.8
  90.8 0.9 copy-start.4
  101.9 0.9 copy-start.4
  137.8 0.7 copy-start.9
  137.8 0.7 copy-start.11
  138.5 1.1 copy-start.7
Sparse Core Ops, SparseCore 0:
  10.5 23.5 reduce-scatter.1
where the time goes:
time: 153 us; the launch traced here: 152 us
  blocking collectives  84.8 us (55%)
  matrix products  20.8 us (14%)
  local copies, waits for them, and re-layouts  17.1 us (11%)
  between operations  15.6 us (10%)
  other arithmetic  7.76 us (5%)
  loops' own time  5.72 us (4%)
    all_gather x1, blocking collectives, local(): lax.all_gather(local_future[None].astype(jnp.bfloat16), 'seq', axis=0, ti...  30.9 us
    all_gather x1, blocking collectives, local(): lax.all_gather(local_state[None].astype(jnp.bfloat16), 'seq', axis=0, til...  30.7 us
    unnamed x1, blocking collectives  23.1 us
    dot_general x22, matrix products, product(): jnp.dot(left, right, precision=FULL_PRECISION, preferred_element_type=jnp...  14.4 us
    unnamed x33, local copies, waits for them, and re-layouts  7.15 us
    another operation x10, other arithmetic  3.56 us
  transfers between devices with their start and end apart: 1, of which 0 were waited for; matrix products, arithmetic and copies ran while one was open for 27% of the time, Pallas kernels for 0%

commit v1 on v0

v1 whole, which is shorter than its diff:
```python
import functools

import jax
import jax.numpy as jnp
from jax import lax
from jax.experimental import pallas as pl
from jax.experimental.pallas import tpu as pltpu
from jax.sharding import PartitionSpec as P

NORM_EPS = 1e-06
C = 128
F32 = jnp.float32
BF16 = jnp.bfloat16
LOGS = 16


def mm(a, b):
    return lax.dot_general(a, b, (((1,), (0,)), ((), ())), preferred_element_type=F32)


def mm_nt(a, b):
    return lax.dot_general(a, b, (((1,), (1,)), ((), ())), preferred_element_type=F32)


def split(x):
    high = x.astype(BF16)
    return high, (x - high.astype(F32)).astype(BF16)


def twice(x, axis):
    return jnp.concatenate([x, x], axis=axis)


def parts(x, axis):
    return jnp.concatenate(split(x), axis=axis)


def cut3(x):
    high = x.astype(BF16).astype(F32)
    middle = (x - high).astype(BF16).astype(F32)
    return high, middle, x - high - middle


def sums(decay):
    n = decay.shape[0]
    row = lax.broadcasted_iota(jnp.int32, (C, C), 0)
    col = lax.broadcasted_iota(jnp.int32, (C, C), 1)
    upto = (row <= col).astype(F32)
    after = (row > col).astype(F32)
    ones = jnp.concatenate([upto, after], axis=1).astype(BF16)
    pieces = jnp.concatenate(cut3(decay), axis=0).astype(BF16)
    both = mm(pieces, ones)
    both = both[:n] + both[n : 2 * n] + both[2 * n :]
    return both[:, :C], both[:, C:]


def totals(upto):
    n = upto.shape[0]
    return [jnp.broadcast_to(upto[r : r + 1, C - 1 :], (1, C)) for r in range(n)]


def before_chunks(tot):
    out = [jnp.zeros((1, C), F32)]
    for t in tot[:-1]:
        out.append(out[-1] + t)
    return out


def after_chunks(tot):
    return before_chunks(tot[::-1])[::-1]


def chunk(ref, r):
    return ref[r * C : (r + 1) * C, :]


def flipped(x):
    return x.astype(F32).T


def log_rows(total):
    high, middle, low = cut3(total)
    return jnp.concatenate([high, middle, low, jnp.zeros((LOGS - 3, C), F32)], axis=0).astype(BF16)


def read_log(ref):
    rows = ref[C:, :].astype(F32)
    return rows[0:1] + rows[1:2] + rows[2:3]


def state_kernel(k_ref, v_ref, decay_ref, out_ref):
    upto, after = sums(decay_ref[...])
    tot = totals(upto)
    later = after_chunks(tot)
    n = len(tot)
    state = jnp.zeros((C, C), F32)
    for r in range(n):
        weights = jnp.exp(after[r : r + 1] + later[r])
        kw = flipped(chunk(k_ref, r)) * weights
        state = state + mm(parts(kw, 1), twice(chunk(v_ref, r), 0))
    out_ref[:C, :] = state.astype(BF16)
    out_ref[C:, :] = log_rows(sum(tot))


def between(logs, positions, low, high):
    out = jnp.zeros((1, C), F32)
    for log, position in zip(logs, positions, strict=True):
        out = out + jnp.where((position > low) & (position < high), log, 0.0)
    return out


def place(stride, radix):
    return lax.rem(lax.div(lax.axis_index("seq"), stride), radix)


def fold_kernel(stride, radix, own_ref, *refs):
    out_ref = refs[-1]
    mine = place(stride, radix)
    positions = [mine ^ d for d in range(radix)]
    all_refs = [own_ref, *refs[:-1]]
    logs = [read_log(ref) for ref in all_refs]
    total = jnp.zeros((C, C), F32)
    for ref, position in zip(all_refs, positions, strict=True):
        weight = jnp.exp(between(logs, positions, position, radix))
        total = total + weight * ref[:C, :].astype(F32)
    out_ref[:C, :] = total.astype(BF16)
    out_ref[C:, :] = log_rows(sum(logs))


def forward_kernel(q_ref, k_ref, v_ref, decay_ref, order_ref, out_ref, cols_ref, qt_ref):
    upto, after = sums(decay_ref[...])
    tot = totals(upto)
    begin, later = before_chunks(tot), after_chunks(tot)
    n = len(tot)
    row = lax.broadcasted_iota(jnp.int32, (C, C), 0)
    col = lax.broadcasted_iota(jnp.int32, (C, C), 1)
    rows = [upto]
    rows.append(jnp.concatenate([jnp.exp(upto[r : r + 1] + begin[r]) for r in range(n)], axis=0))
    rows.append(jnp.concatenate([jnp.exp(after[r : r + 1] + later[r]) for r in range(n)], axis=0))
    rows.append(jnp.exp(upto))
    rows.append(jnp.exp(after))
    used = sum(x.shape[0] for x in rows)
    rows.append(jnp.zeros((C - used, C), F32))
    cols = jnp.concatenate(rows, axis=0).T
    cols_ref[...] = cols
    state = jnp.zeros((C, C), F32)
    for r in range(n):
        q, k, v = chunk(q_ref, r), chunk(k_ref, r), chunk(v_ref, r)
        decay = jnp.exp(jnp.minimum(cols[:, r : r + 1] - upto[r : r + 1], 0.0))
        scores = jnp.where(row >= col, mm_nt(q, k) * decay, 0.0)
        out = mm(parts(scores, 1), twice(v, 0))
        if r > 0:
            out = out + cols[:, 3 * n + r : 3 * n + r + 1] * mm(twice(q, 1), parts(state, 0))
        out_ref[r * C : (r + 1) * C, :] = out
        qt_ref[:, r * C : (r + 1) * C] = flipped(q).astype(BF16)
        if r < n - 1:
            kw = flipped(k) * jnp.exp(after[r : r + 1])
            state = jnp.exp(tot[r]) * state + mm(parts(kw, 1), twice(v, 0))


def norm_kernel(levels, count, local_ref, q_ref, qt_ref, dy_ref, cols_ref, *refs):
    received, (attn_ref, dattn_ref, incoming_ref, state_ref, weights_ref) = refs[:-5], refs[-5:]
    n = local_ref.shape[0] // C
    own, others = received[: len(levels)], received[len(levels) :]
    incoming = jnp.zeros((C, C), F32)
    ahead = jnp.zeros((1, C), F32)
    behind = jnp.zeros((1, C), F32)
    weights = []
    at = 0
    for (stride, radix), own_ref in zip(levels, own, strict=True):
        mine = place(stride, radix)
        positions = [mine ^ d for d in range(radix)]
        level = [own_ref, *others[at : at + radix - 1]]
        at += radix - 1
        logs = [read_log(ref) for ref in level]
        for ref, position in zip(level[1:], positions[1:], strict=True):
            weight = jnp.where(position < mine, jnp.exp(ahead + between(logs, positions, position, mine)), 0.0)
            incoming = incoming + weight * ref[:C, :].astype(F32)
            weights.append(
                jnp.where(position > mine, jnp.exp(behind + between(logs, positions, mine, position)), 0.0)
            )
        for position in positions:
            weights.append(jnp.exp(between(logs, positions, -1, position)))
        ahead = ahead + between(logs, positions, -1, mine)
        behind = behind + between(logs, positions, mine, radix)
    weights.append(jnp.zeros((count - len(weights), C), F32))
    weights_ref[...] = jnp.concatenate(weights, axis=0)
    incoming_ref[...] = incoming
    incoming = parts(incoming, 0)
    cols = cols_ref[...]
    state = jnp.zeros((C, C), F32)
    for r in range(n):
        lead = cols[:, n + r : n + r + 1]
        attention = chunk(local_ref, r) + lead * mm(twice(chunk(q_ref, r), 1), incoming)
        dy = chunk(dy_ref, r).astype(F32)
        ratio = lax.rsqrt(jnp.mean(attention * attention, axis=1, keepdims=True) + NORM_EPS)
        along = jnp.sum(dy * attention, axis=1, keepdims=True)
        attn_ref[r * C : (r + 1) * C, :] = (attention * ratio).astype(BF16)
        dattn = ratio * dy - (ratio * ratio * ratio / C * along) * attention
        dattn_ref[r * C : (r + 1) * C, :] = dattn
        both = mm(qt_ref[:, r * C : (r + 1) * C], parts(lead * dattn, 1))
        state = state + both[:, :C] + both[:, C:]
    state_ref[...] = state.astype(BF16)


def fold_back_kernel(first, own_ref, *refs):
    weights_ref, out_ref = refs[-2:]
    total = jnp.zeros((C, C), F32)
    for i, ref in enumerate((own_ref, *refs[:-2])):
        total = total + weights_ref[first + i : first + i + 1, :] * ref[...].astype(F32)
    out_ref[...] = total.astype(BF16)


def backward_kernel(
    q_ref, k_ref, v_ref, decay_ref, cols_ref, dattn_ref, incoming_ref, order_ref, dq_ref, dk_ref, dv_ref, starts
):
    upto, after = sums(decay_ref[...])
    tot = totals(upto)
    begin = before_chunks(tot)
    n = len(tot)
    row = lax.broadcasted_iota(jnp.int32, (C, C), 0)
    col = lax.broadcasted_iota(jnp.int32, (C, C), 1)
    cols = cols_ref[...]
    incoming = incoming_ref[...]
    state = jnp.zeros((C, C), F32)
    for r in range(n):
        starts[r] = state + jnp.exp(begin[r]) * incoming
        if r < n - 1:
            kw = flipped(chunk(k_ref, r)) * jnp.exp(after[r : r + 1])
            state = jnp.exp(tot[r]) * state + mm(parts(kw, 1), twice(chunk(v_ref, r), 0))
    future = jnp.zeros((C, C), F32)
    for r in reversed(range(n)):
        q, k, v = chunk(q_ref, r), chunk(k_ref, r), chunk(v_ref, r)
        dattn = chunk(dattn_ref, r)
        pair = parts(dattn, 1)
        up, down = upto[r : r + 1], cols[:, r : r + 1]
        lead, tail = cols[:, 3 * n + r : 3 * n + r + 1], cols[:, 4 * n + r : 4 * n + r + 1]
        lower = jnp.where(row >= col, jnp.exp(jnp.minimum(down - up, 0.0)), 0.0)
        upper = jnp.where(row <= col, jnp.exp(jnp.minimum(up - down, 0.0)), 0.0)
        v2 = twice(v, 1)
        dscores = mm_nt(pair, v2) * lower
        start = twice(starts[r].astype(BF16), 1)
        dq = mm(parts(dscores, 1), twice(k, 0)) + lead * mm_nt(pair, start)
        dq_ref[r * C : (r + 1) * C, :] = dq.astype(BF16)
        scores_t = mm_nt(k, q) * upper
        dscores_t = mm_nt(v2, pair) * upper
        high, low = split(dattn)
        s_high, s_low = split(scores_t)
        dk = mm(parts(dscores_t, 1), twice(q, 0))
        dv = mm(jnp.concatenate([s_high, s_low], 1), twice(high, 0)) + mm(s_high, low)
        if r < n - 1:
            dk = dk + tail * mm_nt(twice(v, 1), parts(future, 1))
            dv = dv + tail * mm(twice(k, 1), parts(future, 0))
        dk_ref[r * C : (r + 1) * C, :] = dk
        dv_ref[r * C : (r + 1) * C, :] = dv
        if r > 0:
            both = mm(flipped(q).astype(BF16), parts(lead * dattn, 1))
            future = jnp.exp(tot[r]) * future + both[:, :C] + both[:, C:]


def last_kernel(levels, dk_ref, dv_ref, k_ref, v_ref, cols_ref, weights_ref, *refs):
    received, (out_k_ref, out_v_ref) = refs[:-2], refs[-2:]
    n = dk_ref.shape[0] // C
    future = jnp.zeros((C, C), F32)
    at, taken = 0, 0
    for _, radix in levels:
        for d in range(radix - 1):
            future = future + weights_ref[at + d : at + d + 1, :] * received[taken + d][...].astype(F32)
        at += 2 * radix - 1
        taken += radix - 1
    cols = cols_ref[...]
    wide, tall = parts(future, 1), parts(future, 0)
    for r in range(n):
        tail = cols[:, 2 * n + r : 2 * n + r + 1]
        dk = chunk(dk_ref, r) + tail * mm_nt(twice(chunk(v_ref, r), 1), wide)
        dv = chunk(dv_ref, r) + tail * mm(twice(chunk(k_ref, r), 1), tall)
        out_k_ref[r * C : (r + 1) * C, :] = dk.astype(BF16)
        out_v_ref[r * C : (r + 1) * C, :] = dv.astype(BF16)


def call(body, shapes, name, scratch=(), flops=0, moved=1 << 20):
    return pl.pallas_call(
        body,
        out_shape=shapes,
        scratch_shapes=scratch,
        name=name,
        compiler_params=pltpu.CompilerParams(vmem_limit_bytes=32 * 1024 * 1024),
        cost_estimate=pl.CostEstimate(flops=flops, bytes_accessed=moved, transcendentals=0),
    )


def scan_levels(size):
    levels, stride = [], 1
    while stride < size:
        radix = 2 if stride == 1 else min(4, size // stride)
        levels.append((stride, radix))
        stride *= radix
    return levels


def swap(x, axis, size, stride, radix, d):
    pairs = [(i, i - i % (stride * radix) + ((i // stride % radix) ^ d) * stride + i % stride) for i in range(size)]
    return lax.ppermute(x, axis, pairs)


def local(levels, seq, dp, queries, key_vectors, value_vectors, out_grad, log_decay, prev_grads):
    q, k, v, dy = queries[0], key_vectors[0], value_vectors[0], out_grad[0]
    tokens = q.shape[0]
    n = tokens // C
    decay = log_decay.reshape(n, C)
    shape = jax.ShapeDtypeStruct
    payload = shape((C + LOGS, C), BF16)
    square = shape((C, C), F32)
    wide, narrow = shape((tokens, C), F32), shape((tokens, C), BF16)

    own = [call(state_kernel, payload, "state")(k, v, decay)]
    others = []
    for i, (stride, radix) in enumerate(levels):
        got = [swap(own[-1], "seq", seq, stride, radix, d) for d in range(1, radix)]
        others += got
        if i < len(levels) - 1:
            own.append(call(functools.partial(fold_kernel, stride, radix), payload, "fold")(own[-1], *got))
    local_out, cols, qt = call(forward_kernel, (wide, square, shape((C, tokens), BF16)), "forward")(
        q, k, v, decay, own[-1]
    )

    count = sum(2 * radix - 1 for _, radix in levels)
    count += -count % 8
    attn_out, dattn, incoming, state, weights = call(
        functools.partial(norm_kernel, levels, count),
        (narrow, wide, square, shape((C, C), BF16), shape((count, C), F32)),
        "norm",
    )(local_out, q, qt, dy, cols, *own, *others)

    received = []
    at = 0
    for i, (stride, radix) in enumerate(levels):
        got = [swap(state, "seq", seq, stride, radix, d) for d in range(1, radix)]
        received += got
        if i < len(levels) - 1:
            fold = functools.partial(fold_back_kernel, at + radix - 1)
            state = call(fold, shape((C, C), BF16), "fold_back")(state, *got, weights)
        at += 2 * radix - 1
    grad_query, dk, dv = call(
        backward_kernel, (narrow, wide, wide), "backward", scratch=[pltpu.VMEM((n, C, C), F32)]
    )(q, k, v, decay, cols, dattn, incoming, state)
    grad_key, grad_value = call(functools.partial(last_kernel, levels), (narrow, narrow), "last")(
        dk, dv, k, v, cols, weights, *received
    )

    mine = lax.axis_index("dp")
    grads = prev_grads[0]
    columns = grads.shape[1] // dp
    total = lax.dynamic_slice_in_dim(grads, mine * columns, columns, 1).astype(F32)
    for d in range(1, dp):
        away = lax.dynamic_slice_in_dim(grads, (mine ^ d) * columns, columns, 1)
        total = total + swap(away, "dp", dp, 1, dp, d).astype(F32)
    return attn_out[None], grad_query[None], grad_key[None], grad_value[None], total


def solution(mesh):
    seq, dp = mesh.shape["seq"], mesh.shape["dp"]
    return jax.shard_map(
        functools.partial(local, scan_levels(seq), seq, dp),
        mesh=mesh,
        in_specs=(
            P("dp", "seq", None),
            P("dp", "seq", None),
            P("dp", "seq", None),
            P("dp", "seq", None),
            P("dp", None, "seq"),
            P("dp", "seq", None),
        ),
        out_specs=(
            P("dp", "seq", None),
            P("dp", "seq", None),
            P("dp", "seq", None),
            P("dp", "seq", None),
            P("seq", "dp"),
        ),
        check_vma=False,
    )
```

time: 153 us -> 36.8 us (0.24)
  blocking collectives: 84.8 us -> 0 us
  matrix products: 20.8 us -> 0 us
  starting transfers between devices: 0.04 us -> 17.1 us
  between operations: 15.6 us -> 0.73 us
  local copies, waits for them, and re-layouts: 17.1 us -> 2.62 us
  Pallas kernels: 0 us -> 8.57 us
  other arithmetic: 7.76 us -> 0.73 us
  waiting for transfers between devices: 0.68 us -> 6.93 us
  loops' own time: 5.72 us -> 0 us
    all_gather x2 -> x0, blocking collectives: 61.7 us -> none  [the longest x1 30.9 us: local(): lax.all_gather(local_future[None].astype(jnp.bfloat16), 'seq', axis=0, ti...]
    unnamed x1 -> x0, blocking collectives: 23.1 us -> none
    dot_general x32 -> x0, matrix products: 20.8 us -> none  [the longest x22 14.4 us: product(): jnp.dot(left, right, precision=FULL_PRECISION, preferred_element_type=jnp...]
    ppermute x0 -> x11, starting transfers between devices: none -> 17.1 us  [swap(): return lax.ppermute(x, axis, pairs)]
    pallas_call x0 -> x7, Pallas kernels: none -> 8.57 us  [the longest x1 3.35 us: local(): call(backward_kernel, (narrow, wide, wide), 'backward', scratch=[pltpu.VM...]
    ppermute x0 -> x11, waiting for transfers between devices: none -> 6.93 us  [swap(): return lax.ppermute(x, axis, pairs)]
    slice x12 -> x0, local copies, waits for them, and re-layouts: 6.34 us -> none  [the longest x4 2.47 us: retreat(): running[-1]]
    another operation x2 -> x0, loops' own time: 5.72 us -> none  [the longest x1 2.94 us: backward_local(): lax.scan(retreat, jnp.zeros((head_width, head_width), jnp.float32), (quer...]
  transfers between devices with their start and end apart: 1 -> 11, of which waited for: 0 -> 3; matrix products, arithmetic and copies ran while one was open for 27% -> 2% of each run, Pallas kernels for 0% -> 19%
where the time goes in v1:
time: 36.8 us; the launch traced here: 36.6 us
  starting transfers between devices  17.1 us (46%)
  Pallas kernels  8.57 us (23%)
  waiting for transfers between devices  6.93 us (19%)
  local copies, waits for them, and re-layouts  2.62 us (7%)
  other arithmetic  0.73 us (2%)
  between operations  0.73 us (2%)
    ppermute x11, starting transfers between devices, swap(): return lax.ppermute(x, axis, pairs)  17.1 us
    ppermute x11, waiting for transfers between devices, swap(): return lax.ppermute(x, axis, pairs)  6.93 us
    pallas_call x1, Pallas kernels, local(): call(backward_kernel, (narrow, wide, wide), 'backward', scratch=[pltpu.VM...  3.35 us
    unnamed x16, local copies, waits for them, and re-layouts  2.6 us
    pallas_call x1, Pallas kernels, local(): call(forward_kernel, (wide, square, shape((C, tokens), BF16)), 'forward')  1.75 us
    pallas_call x1, Pallas kernels, local(): call(functools.partial(norm_kernel, levels, count), (narrow, wide, square...  1.66 us
    pallas_call x1, Pallas kernels, local(): call(functools.partial(last_kernel, levels), (narrow, narrow), 'last')  1.25 us
  transfers between devices with their start and end apart: 11, of which 3 were waited for; matrix products, arithmetic and copies ran while one was open for 2% of the time, Pallas kernels for 19%

profile of v1, /device:TPU:0, one launch (start us, length us, event | category | flops | bytes accessed | tf_op | source)
XLA Modules:
  0.0 36.6 jit_solution(15292930928145532985)
XLA Ops:
  0.6 0.0 copy-start.6
  0.6 0.7 %copy-done.6 = f32[1,1,1024]{2,1,0:T(1,128)S(1)} copy-done((f32[1,1,1024]{2,1,0:T(1,128)S(1)}, f32[1,1,1024]{2,1,0:T(1,128)}, u32[]{:S(2)}) %copy-start.6) | copy-done | bytes 4120
  1.3 0.0 copy-start
  1.3 0.9 %copy-done = bf16[1,1024,128]{2,1,0:T(8,128)(2,1)S(1)} copy-done((bf16[1,1024,128]{2,1,0:T(8,128)(2,1)S(1)}, bf16[1,1024,128]{2,1,0:T(8,128)(2,1)}, u32[]{:S(2)}) %copy-start) | copy-done | bytes 262168
  2.3 0.0 copy-start.2
  2.3 0.9 %copy-done.2 = bf16[1,1024,128]{2,1,0:T(8,128)(2,1)S(1)} copy-done((bf16[1,1024,128]{2,1,0:T(8,128)(2,1)S(1)}, bf16[1,1024,128]{2,1,0:T(8,128)(2,1)}, u32[]{:S(2)}) %copy-start.2) | copy-done | bytes 262168
  3.2 0.0 copy-start.7
  3.2 0.0 copy-start.4
  3.2 0.5 %state.1.own_ref.refs_0_ = bf16[144,128]{1,0:T(8,128)(2,1)S(1)} custom-call(bf16[1024,128]{1,0:T(8,128)(2,1)S(1)} %bitcast.18, bf16[1024,128]{1,0:T(8,128)(2,1)S(1)} %bitcast.22, f32[8,128]{1,0:T(8,128)S(1)} %bitcast.30), custom_call_target="tpu_custom_call" | custom-call | bytes 1048576 | tf_op jit(solution)/shard_map/state/pallas_call | solution.py:316
  3.7 3.0 %collective-permute-start = (bf16[144,128]{1,0:T(8,128)(2,1)S(1)}, bf16[144,128]{1,0:T(8,128)(2,1)S(1)}, u32[]{:S(2)}, u32[]{:S(2)}) collective-permute-start(bf16[144,128]{1,0:T(8,128)(2,1)S(1)} %state.1.own_ref.refs_0_), channel_id=1, source_target_pairs={{0,1},{1,0},{2,3},{3,2},{4,5},{5,4},{6,7},{7,6},{8,9},{9,8},{10,11... | collective-permute-start | bytes 110600 | tf_op jit(solution)/shard_map/ppermute | solution.py:303
  6.7 1.9 %collective-permute-done.refs_0_.refs_2_ = bf16[144,128]{1,0:T(8,128)(2,1)S(1)} collective-permute-done((bf16[144,128]{1,0:T(8,128)(2,1)S(1)}, bf16[144,128]{1,0:T(8,128)(2,1)S(1)}, u32[]{:S(2)}, u32[]{:S(2)}) %collective-permute-start) | collective-permute-done | bytes 36896 | tf_op jit(solution)/shard_map/ppermute | solution.py:303
  8.7 0.0 copy-start.1
  8.7 0.0 copy-start.3
  8.7 2.2 %collective-permute-start.1 = (bf16[144,128]{1,0:T(8,128)(2,1)S(1)}, bf16[144,128]{1,0:T(8,128)(2,1)S(1)}, u32[]{:S(2)}, u32[]{:S(2)}) collective-permute-start(bf16[144,128]{1,0:T(8,128)(2,1)S(1)} %fold.1.order_ref.refs_1_), channel_id=1, source_target_pairs={{0,2},{1,3},{2,0},{3,1},{4,6},{5,7},{6,4},{7,5},{8,10},{9,11},{10,... | collective-permute-start | bytes 110600 | tf_op jit(solution)/shard_map/ppermute | solution.py:303
  10.9 0.0 copy-done.7
  10.9 0.1 collective-permute-start.10
  11.0 1.6 %collective-permute-start.9 = (bf16[32,1536]{1,0:T(8,128)(2,1)S(1)}, bf16[32,1536]{1,0:T(8,128)(2,1)S(1)}, u32[]{:S(2)}, u32[]{:S(2)}) collective-permute-start(bf16[32,1536]{1,0:T(8,128)(2,1)S(1)} %get-tuple-element.33), channel_id=1, source_target_pairs={{0,16},{8,24},{16,0},{24,8},{1,17},{9,25},{17,1},{25,9},{2,18},{10... | collective-permute-start | bytes 294920 | tf_op jit(solution)/shard_map/ppermute | solution.py:303
  12.6 0.3 collective-permute-start.8
  12.9 2.6 %collective-permute-start.2 = (bf16[144,128]{1,0:T(8,128)(2,1)S(1)}, bf16[144,128]{1,0:T(8,128)(2,1)S(1)}, u32[]{:S(2)}, u32[]{:S(2)}) collective-permute-start(bf16[144,128]{1,0:T(8,128)(2,1)S(1)} %fold.1.order_ref.refs_1_), channel_id=1, source_target_pairs={{0,4},{1,5},{2,6},{3,7},{4,0},{5,1},{6,2},{7,3},{8,12},{9,13},{10,... | collective-permute-start | bytes 110600 | tf_op jit(solution)/shard_map/ppermute | solution.py:303
  15.5 0.0 collective-permute-done.1.refs_3_
  15.5 1.4 %collective-permute-start.3 = (bf16[144,128]{1,0:T(8,128)(2,1)S(1)}, bf16[144,128]{1,0:T(8,128)(2,1)S(1)}, u32[]{:S(2)}, u32[]{:S(2)}) collective-permute-start(bf16[144,128]{1,0:T(8,128)(2,1)S(1)} %fold.1.order_ref.refs_1_), channel_id=1, source_target_pairs={{0,6},{1,7},{2,4},{3,5},{4,2},{5,3},{6,0},{7,1},{8,14},{9,15},{10,... | collective-permute-start | bytes 110600 | tf_op jit(solution)/shard_map/ppermute | solution.py:303
  16.9 0.0 copy-done.4
  16.9 0.0 copy-done.1
  16.9 0.0 copy-done.3
  16.9 0.0 copy-start.5
  16.9 1.7 %forward.1 = (f32[1024,128]{1,0:T(8,128)S(1)}, f32[128,128]{1,0:T(8,128)S(1)}, bf16[128,1024]{1,0:T(8,128)(2,1)S(1)}) custom-call(bf16[1024,128]{1,0:T(8,128)(2,1)S(1)} %bitcast.26, bf16[1024,128]{1,0:T(8,128)(2,1)S(1)} %bitcast.19, bf16[1024,128]{1,0:T(8,128)(2,1)S(1)} %bitcast.23, f32[8,128]{1,0:T(8,128)S(1)} %bitcast.31, ...), custom_call_target="tpu_custom_call" | custom-call | bytes 1048576 | tf_op jit(solution)/shard_map/forward/pallas_call | solution.py:323
  18.7 0.0 collective-permute-done.2.refs_4_
  18.7 2.5 %collective-permute-done.3.refs_5_ = bf16[144,128]{1,0:T(8,128)(2,1)S(1)} collective-permute-done((bf16[144,128]{1,0:T(8,128)(2,1)S(1)}, bf16[144,128]{1,0:T(8,128)(2,1)S(1)}, u32[]{:S(2)}, u32[]{:S(2)}) %collective-permute-start.3) | collective-permute-done | bytes 36896 | tf_op jit(solution)/shard_map/ppermute | solution.py:303
  21.2 0.0 copy-done.5
  21.2 1.7 %norm.1 = (bf16[1024,128]{1,0:T(8,128)(2,1)}, f32[1024,128]{1,0:T(8,128)S(1)}, f32[128,128]{1,0:T(8,128)S(1)}, bf16[128,128]{1,0:T(8,128)(2,1)S(1)}, f32[16,128]{1,0:T(8,128)S(1)}) custom-call(f32[1024,128]{1,0:T(8,128)S(1)} %get-tuple-element.18.local_ref, bf16[1024,128]{1,0:T(8,128)(2,1)S(1)} %bitcast.27, bf16[128,1024]{1,0:T(8,128)(2,1)S(1)} %get-tuple-element.19.qt_ref, ...), custom_call_target="tpu_custom_call" | custom-call | bytes 1048576 | tf_op jit(solution)/shard_map/norm/pallas_call | solution.py:329
  22.9 1.5 %collective-permute-start.4 = (bf16[128,128]{1,0:T(8,128)(2,1)S(1)}, bf16[128,128]{1,0:T(8,128)(2,1)S(1)}, u32[]{:S(2)}, u32[]{:S(2)}) collective-permute-start(bf16[128,128]{1,0:T(8,128)(2,1)S(1)} %get-tuple-element.24.own_ref), channel_id=1, source_target_pairs={{0,1},{1,0},{2,3},{3,2},{4,5},{5,4},{6,7},{7,6},{8,9},{9,8},{10,11... | collective-permute-start | bytes 98312 | tf_op jit(solution)/shard_map/ppermute | solution.py:303
  24.4 2.4 %collective-permute-done.4.refs_0_ = bf16[128,128]{1,0:T(8,128)(2,1)S(1)} collective-permute-done((bf16[128,128]{1,0:T(8,128)(2,1)S(1)}, bf16[128,128]{1,0:T(8,128)(2,1)S(1)}, u32[]{:S(2)}, u32[]{:S(2)}) %collective-permute-start.4) | collective-permute-done | bytes 32800 | tf_op jit(solution)/shard_map/ppermute | solution.py:303
  26.8 0.1 collective-permute-start.5
  26.9 2.0 %collective-permute-start.6 = (bf16[128,128]{1,0:T(8,128)(2,1)S(1)}, bf16[128,128]{1,0:T(8,128)(2,1)S(1)}, u32[]{:S(2)}, u32[]{:S(2)}) collective-permute-start(bf16[128,128]{1,0:T(8,128)(2,1)S(1)} %fold_back.1.order_ref), channel_id=1, source_target_pairs={{0,4},{1,5},{2,6},{3,7},{4,0},{5,1},{6,2},{7,3},{8,12},{9,13},{10,... | collective-permute-start | bytes 98312 | tf_op jit(solution)/shard_map/ppermute | solution.py:303
  28.9 0.0 collective-permute-done.10
  28.9 2.4 %collective-permute-start.7 = (bf16[128,128]{1,0:T(8,128)(2,1)S(1)}, bf16[128,128]{1,0:T(8,128)(2,1)S(1)}, u32[]{:S(2)}, u32[]{:S(2)}) collective-permute-start(bf16[128,128]{1,0:T(8,128)(2,1)S(1)} %fold_back.1.order_ref), channel_id=1, source_target_pairs={{0,6},{1,7},{2,4},{3,5},{4,2},{5,3},{6,0},{7,1},{8,14},{9,15},{10,... | collective-permute-start | bytes 98312 | tf_op jit(solution)/shard_map/ppermute | solution.py:303
  31.3 0.0 collective-permute-done.9
  31.3 0.0 collective-permute-done.8
  31.3 0.7 %fusion.1 = f32[32,1536]{1,0:T(8,128)} fusion(bf16[32,1536]{1,0:T(8,128)(2,1)S(1)} %collective-permute-done.10, bf16[32,1536]{1,0:T(8,128)(2,1)S(1)} %collective-permute-done.9, bf16[32,1536]{1,0:T(8,128)(2,1)S(1)} %collective-permute-done.8, bf16[1,32,6144]{2,1,0:T(8,128)(2,1)S(1)} %copy-done.7, s32[]{:T(128)S(6)} %select_n.12), kind=kLoop, calls=%fused_computation.2 | loop fusion | flops 344064 | bytes 589828 | tf_op jit(solution)/shard_map/add | solution.py:357
  32.0 3.4 %backward.1 = (bf16[1024,128]{1,0:T(8,128)(2,1)}, f32[1024,128]{1,0:T(8,128)S(1)}, f32[1024,128]{1,0:T(8,128)S(1)}) custom-call(bf16[1024,128]{1,0:T(8,128)(2,1)S(1)} %bitcast.28, bf16[1024,128]{1,0:T(8,128)(2,1)S(1)} %bitcast.20, bf16[1024,128]{1,0:T(8,128)(2,1)S(1)} %bitcast.24, f32[8,128]{1,0:T(8,128)S(1)} %bitcast.32, ...), custom_call_target="tpu_custom_call" | custom-call | bytes 1048576 | tf_op jit(solution)/shard_map/backward/pallas_call | solution.py:344
  35.4 0.0 collective-permute-done.5.refs_1_
  35.4 0.0 collective-permute-done.6.refs_2_
  35.4 0.0 collective-permute-done.7.refs_3_
  35.4 1.2 %last.1 = (bf16[1024,128]{1,0:T(8,128)(2,1)}, bf16[1024,128]{1,0:T(8,128)(2,1)}) custom-call(f32[1024,128]{1,0:T(8,128)S(1)} %get-tuple-element.27.dk_ref, f32[1024,128]{1,0:T(8,128)S(1)} %get-tuple-element.28.dv_ref, bf16[1024,128]{1,0:T(8,128)(2,1)S(1)} %bitcast.21, bf16[1024,128]{1,0:T(8,128)(2,1)S(1)} %bitcast.25, ...), custom_call_target="tpu_custom_call" | custom-call | bytes 1048576 | tf_op jit(solution)/shard_map/last/pallas_call | solution.py:347
  (3 shorter events, 0.1 us)
Async XLA Ops:
  0.6 0.7 %copy-start.6 = (f32[1,1,1024]{2,1,0:T(1,128)S(1)}, f32[1,1,1024]{2,1,0:T(1,128)}, u32[]{:S(2)}) copy-start(f32[1,1,1024]{2,1,0:T(1,128)} %param.10) | copy-start | bytes 12292
  1.3 0.9 %copy-start = (bf16[1,1024,128]{2,1,0:T(8,128)(2,1)S(1)}, bf16[1,1024,128]{2,1,0:T(8,128)(2,1)}, u32[]{:S(2)}) copy-start(bf16[1,1024,128]{2,1,0:T(8,128)(2,1)} %param.7) | copy-start | bytes 786436
  2.3 0.9 %copy-start.2 = (bf16[1,1024,128]{2,1,0:T(8,128)(2,1)S(1)}, bf16[1,1024,128]{2,1,0:T(8,128)(2,1)}, u32[]{:S(2)}) copy-start(bf16[1,1024,128]{2,1,0:T(8,128)(2,1)} %param.8) | copy-start | bytes 786436
  3.2 7.7 %copy-start.7 = (bf16[1,32,6144]{2,1,0:T(8,128)(2,1)S(1)}, bf16[1,32,6144]{2,1,0:T(8,128)(2,1)}, u32[]{:S(2)}) copy-start(bf16[1,32,6144]{2,1,0:T(8,128)(2,1)} %param.11) | copy-start | bytes 1179652
  3.2 13.7 %copy-start.4 = (bf16[1,1024,128]{2,1,0:T(8,128)(2,1)S(1)}, bf16[1,1024,128]{2,1,0:T(8,128)(2,1)}, u32[]{:S(2)}) copy-start(bf16[1,1024,128]{2,1,0:T(8,128)(2,1)} %param.6) | copy-start | bytes 786436
  3.7 4.9 %collective-permute-start = (bf16[144,128]{1,0:T(8,128)(2,1)S(1)}, bf16[144,128]{1,0:T(8,128)(2,1)S(1)}, u32[]{:S(2)}, u32[]{:S(2)}) collective-permute-start(bf16[144,128]{1,0:T(8,128)(2,1)S(1)} %state.1.own_ref.refs_0_), channel_id=1, source_target_pairs={{0,1},{1,0},{2,3},{3,2},{4,5},{5,4},{6,7},{7,6},{8,9},{9,8},{10,11... | collective-permute-start | bytes 110600 | tf_op jit(solution)/shard_map/ppermute | solution.py:303
  8.7 8.2 %copy-start.1 = (bf16[1,1024,128]{2,1,0:T(8,128)(2,1)S(1)}, bf16[1,1024,128]{2,1,0:T(8,128)(2,1)}, u32[]{:S(2)}) copy-start(bf16[1,1024,128]{2,1,0:T(8,128)(2,1)} %param.7) | copy-start | bytes 786436
  8.7 8.2 %copy-start.3 = (bf16[1,1024,128]{2,1,0:T(8,128)(2,1)S(1)}, bf16[1,1024,128]{2,1,0:T(8,128)(2,1)}, u32[]{:S(2)}) copy-start(bf16[1,1024,128]{2,1,0:T(8,128)(2,1)} %param.8) | copy-start | bytes 786436
  8.7 6.7 %collective-permute-start.1 = (bf16[144,128]{1,0:T(8,128)(2,1)S(1)}, bf16[144,128]{1,0:T(8,128)(2,1)S(1)}, u32[]{:S(2)}, u32[]{:S(2)}) collective-permute-start(bf16[144,128]{1,0:T(8,128)(2,1)S(1)} %fold.1.order_ref.refs_1_), channel_id=1, source_target_pairs={{0,2},{1,3},{2,0},{3,1},{4,6},{5,7},{6,4},{7,5},{8,10},{9,11},{10,... | collective-permute-start | bytes 110600 | tf_op jit(solution)/shard_map/ppermute | solution.py:303
  10.9 17.9 %collective-permute-start.10 = (bf16[32,1536]{1,0:T(8,128)(2,1)S(1)}, bf16[32,1536]{1,0:T(8,128)(2,1)S(1)}, u32[]{:S(2)}, u32[]{:S(2)}) collective-permute-start(bf16[32,1536]{1,0:T(8,128)(2,1)S(1)} %get-tuple-element.32), channel_id=1, source_target_pairs={{0,24},{8,16},{16,8},{24,0},{1,25},{9,17},{17,9},{25,1},{2,26},{10... | collective-permute-start | bytes 294920 | tf_op jit(solution)/shard_map/ppermute | solution.py:303
  11.0 20.3 %collective-permute-start.9 = (bf16[32,1536]{1,0:T(8,128)(2,1)S(1)}, bf16[32,1536]{1,0:T(8,128)(2,1)S(1)}, u32[]{:S(2)}, u32[]{:S(2)}) collective-permute-start(bf16[32,1536]{1,0:T(8,128)(2,1)S(1)} %get-tuple-element.33), channel_id=1, source_target_pairs={{0,16},{8,24},{16,0},{24,8},{1,17},{9,25},{17,1},{25,9},{2,18},{10... | collective-permute-start | bytes 294920 | tf_op jit(solution)/shard_map/ppermute | solution.py:303
  12.6 18.7 %collective-permute-start.8 = (bf16[32,1536]{1,0:T(8,128)(2,1)S(1)}, bf16[32,1536]{1,0:T(8,128)(2,1)S(1)}, u32[]{:S(2)}, u32[]{:S(2)}) collective-permute-start(bf16[32,1536]{1,0:T(8,128)(2,1)S(1)} %get-tuple-element.31), channel_id=1, source_target_pairs={{0,8},{8,0},{16,24},{24,16},{1,9},{9,1},{17,25},{25,17},{2,10},{10... | collective-permute-start | bytes 294920 | tf_op jit(solution)/shard_map/ppermute | solution.py:303
  12.9 5.8 %collective-permute-start.2 = (bf16[144,128]{1,0:T(8,128)(2,1)S(1)}, bf16[144,128]{1,0:T(8,128)(2,1)S(1)}, u32[]{:S(2)}, u32[]{:S(2)}) collective-permute-start(bf16[144,128]{1,0:T(8,128)(2,1)S(1)} %fold.1.order_ref.refs_1_), channel_id=1, source_target_pairs={{0,4},{1,5},{2,6},{3,7},{4,0},{5,1},{6,2},{7,3},{8,12},{9,13},{10,... | collective-permute-start | bytes 110600 | tf_op jit(solution)/shard_map/ppermute | solution.py:303
  15.5 5.8 %collective-permute-start.3 = (bf16[144,128]{1,0:T(8,128)(2,1)S(1)}, bf16[144,128]{1,0:T(8,128)(2,1)S(1)}, u32[]{:S(2)}, u32[]{:S(2)}) collective-permute-start(bf16[144,128]{1,0:T(8,128)(2,1)S(1)} %fold.1.order_ref.refs_1_), channel_id=1, source_target_pairs={{0,6},{1,7},{2,4},{3,5},{4,2},{5,3},{6,0},{7,1},{8,14},{9,15},{10,... | collective-permute-start | bytes 110600 | tf_op jit(solution)/shard_map/ppermute | solution.py:303
  16.9 4.3 %copy-start.5 = (bf16[1,1024,128]{2,1,0:T(8,128)(2,1)S(1)}, bf16[1,1024,128]{2,1,0:T(8,128)(2,1)}, u32[]{:S(2)}) copy-start(bf16[1,1024,128]{2,1,0:T(8,128)(2,1)} %param.9) | copy-start | bytes 786436
  22.9 3.9 %collective-permute-start.4 = (bf16[128,128]{1,0:T(8,128)(2,1)S(1)}, bf16[128,128]{1,0:T(8,128)(2,1)S(1)}, u32[]{:S(2)}, u32[]{:S(2)}) collective-permute-start(bf16[128,128]{1,0:T(8,128)(2,1)S(1)} %get-tuple-element.24.own_ref), channel_id=1, source_target_pairs={{0,1},{1,0},{2,3},{3,2},{4,5},{5,4},{6,7},{7,6},{8,9},{9,8},{10,11... | collective-permute-start | bytes 98312 | tf_op jit(solution)/shard_map/ppermute | solution.py:303
  26.8 8.5 %collective-permute-start.5 = (bf16[128,128]{1,0:T(8,128)(2,1)S(1)}, bf16[128,128]{1,0:T(8,128)(2,1)S(1)}, u32[]{:S(2)}, u32[]{:S(2)}) collective-permute-start(bf16[128,128]{1,0:T(8,128)(2,1)S(1)} %fold_back.1.order_ref), channel_id=1, source_target_pairs={{0,2},{1,3},{2,0},{3,1},{4,6},{5,7},{6,4},{7,5},{8,10},{9,11},{10,... | collective-permute-start | bytes 98312 | tf_op jit(solution)/shard_map/ppermute | solution.py:303
  26.9 8.5 %collective-permute-start.6 = (bf16[128,128]{1,0:T(8,128)(2,1)S(1)}, bf16[128,128]{1,0:T(8,128)(2,1)S(1)}, u32[]{:S(2)}, u32[]{:S(2)}) collective-permute-start(bf16[128,128]{1,0:T(8,128)(2,1)S(1)} %fold_back.1.order_ref), channel_id=1, source_target_pairs={{0,4},{1,5},{2,6},{3,7},{4,0},{5,1},{6,2},{7,3},{8,12},{9,13},{10,... | collective-permute-start | bytes 98312 | tf_op jit(solution)/shard_map/ppermute | solution.py:303
  28.9 6.5 %collective-permute-start.7 = (bf16[128,128]{1,0:T(8,128)(2,1)S(1)}, bf16[128,128]{1,0:T(8,128)(2,1)S(1)}, u32[]{:S(2)}, u32[]{:S(2)}) collective-permute-start(bf16[128,128]{1,0:T(8,128)(2,1)S(1)} %fold_back.1.order_ref), channel_id=1, source_target_pairs={{0,6},{1,7},{2,4},{3,5},{4,2},{5,3},{6,0},{7,1},{8,14},{9,15},{10,... | collective-permute-start | bytes 98312 | tf_op jit(solution)/shard_map/ppermute | solution.py:303

commit v2 on v1

--- a/solution.py
+++ b/solution.py
@@ -11,7 +11,7 @@
 C = 128
 F32 = jnp.float32
 BF16 = jnp.bfloat16
-LOGS = 16
+LOGS = 8
 
 
 def mm(a, b):
@@ -88,15 +88,21 @@
     return rows[0:1] + rows[1:2] + rows[2:3]
 
 
-def state_kernel(k_ref, v_ref, decay_ref, out_ref):
+def state_kernel(k_hbm, v_hbm, decay_hbm, out_ref, k_ref, v_ref, decay_ref, sems):
+    pairs = ((decay_hbm, decay_ref), (k_hbm, k_ref), (v_hbm, v_ref))
+    copies = [pltpu.make_async_copy(source, target, sems.at[i]) for i, (source, target) in enumerate(pairs)]
+    for copy in copies:
+        copy.start()
+    copies[0].wait()
     upto, after = sums(decay_ref[...])
     tot = totals(upto)
     later = after_chunks(tot)
-    n = len(tot)
+    weights = [jnp.exp(after[r : r + 1] + later[r]) for r in range(len(tot))]
+    copies[1].wait()
+    copies[2].wait()
     state = jnp.zeros((C, C), F32)
-    for r in range(n):
-        weights = jnp.exp(after[r : r + 1] + later[r])
-        kw = flipped(chunk(k_ref, r)) * weights
+    for r, weight in enumerate(weights):
+        kw = flipped(chunk(k_ref, r)) * weight
         state = state + mm(parts(kw, 1), twice(chunk(v_ref, r), 0))
     out_ref[:C, :] = state.astype(BF16)
     out_ref[C:, :] = log_rows(sum(tot))
@@ -117,7 +123,7 @@
     out_ref = refs[-1]
     mine = place(stride, radix)
     positions = [mine ^ d for d in range(radix)]
-    all_refs = [own_ref, *refs[:-1]]
+    all_refs = [own_ref, *refs[: radix - 1]]
     logs = [read_log(ref) for ref in all_refs]
     total = jnp.zeros((C, C), F32)
     for ref, position in zip(all_refs, positions, strict=True):
@@ -127,7 +133,9 @@
     out_ref[C:, :] = log_rows(sum(logs))
 
 
-def forward_kernel(q_ref, k_ref, v_ref, decay_ref, order_ref, out_ref, cols_ref, qt_ref):
+def forward_kernel(
+    q_ref, k_ref, v_ref, decay_ref, order_ref, out_ref, cols_ref, rows_ref, qt_ref, starts_ref, lower_ref
+):
     upto, after = sums(decay_ref[...])
     tot = totals(upto)
     begin, later = before_chunks(tot), after_chunks(tot)
@@ -143,19 +151,37 @@
     rows.append(jnp.zeros((C - used, C), F32))
     cols = jnp.concatenate(rows, axis=0).T
     cols_ref[...] = cols
+    rows_ref[:n, :] = upto
+    rows_ref[n : 2 * n, :] = jnp.concatenate([jnp.exp(x) for x in tot], axis=0)
+    rows_ref[2 * n :, :] = jnp.concatenate([jnp.exp(x) for x in begin], axis=0)
     state = jnp.zeros((C, C), F32)
     for r in range(n):
         q, k, v = chunk(q_ref, r), chunk(k_ref, r), chunk(v_ref, r)
         decay = jnp.exp(jnp.minimum(cols[:, r : r + 1] - upto[r : r + 1], 0.0))
-        scores = jnp.where(row >= col, mm_nt(q, k) * decay, 0.0)
+        lower = jnp.where(row >= col, decay, 0.0)
+        lower_ref[r * C : (r + 1) * C, :] = lower
+        scores = mm_nt(q, k) * lower
         out = mm(parts(scores, 1), twice(v, 0))
         if r > 0:
             out = out + cols[:, 3 * n + r : 3 * n + r + 1] * mm(twice(q, 1), parts(state, 0))
         out_ref[r * C : (r + 1) * C, :] = out
         qt_ref[:, r * C : (r + 1) * C] = flipped(q).astype(BF16)
+        starts_ref[r * C : (r + 1) * C, :] = state
         if r < n - 1:
             kw = flipped(k) * jnp.exp(after[r : r + 1])
             state = jnp.exp(tot[r]) * state + mm(parts(kw, 1), twice(v, 0))
+
+
+def turned_kernel(q_ref, k_ref, cols_ref, rows_ref, order_ref, scores_ref, upper_ref):
+    n = rows_ref.shape[0] // 3
+    row = lax.broadcasted_iota(jnp.int32, (C, C), 0)
+    col = lax.broadcasted_iota(jnp.int32, (C, C), 1)
+    cols = cols_ref[...]
+    for r in range(n):
+        decay = jnp.exp(jnp.minimum(rows_ref[r : r + 1, :] - cols[:, r : r + 1], 0.0))
+        upper = jnp.where(row <= col, decay, 0.0)
+        upper_ref[r * C : (r + 1) * C, :] = upper
+        scores_ref[r * C : (r + 1) * C, :] = parts(mm_nt(chunk(k_ref, r), chunk(q_ref, r)) * upper, 1)
 
 
 def norm_kernel(levels, count, local_ref, q_ref, qt_ref, dy_ref, cols_ref, *refs):
@@ -203,63 +229,69 @@
     state_ref[...] = state.astype(BF16)
 
 
-def fold_back_kernel(first, own_ref, *refs):
-    weights_ref, out_ref = refs[-2:]
+def fold_back_kernel(first, radix, own_ref, *refs):
+    weights_ref, out_ref = refs[radix - 1], refs[-1]
     total = jnp.zeros((C, C), F32)
-    for i, ref in enumerate((own_ref, *refs[:-2])):
+    for i, ref in enumerate((own_ref, *refs[: radix - 1])):
         total = total + weights_ref[first + i : first + i + 1, :] * ref[...].astype(F32)
     out_ref[...] = total.astype(BF16)
 
 
-def backward_kernel(
-    q_ref, k_ref, v_ref, decay_ref, cols_ref, dattn_ref, incoming_ref, order_ref, dq_ref, dk_ref, dv_ref, starts
+def queries_kernel(
+    columns, stride, k_ref, v_ref, cols_ref, rows_ref, starts_ref, lower_ref, dattn_ref, incoming_ref, order_ref, *refs
 ):
-    upto, after = sums(decay_ref[...])
-    tot = totals(upto)
-    begin = before_chunks(tot)
-    n = len(tot)
-    row = lax.broadcasted_iota(jnp.int32, (C, C), 0)
-    col = lax.broadcasted_iota(jnp.int32, (C, C), 1)
+    attn_ref, have_ref, came_ref, attn_hbm, dq_hbm, total_hbm, done_ref, dq_ref, total_ref, sems = refs
+    n = rows_ref.shape[0] // 3
+    copies = [
+        pltpu.make_async_copy(source, target, sems.at[i])
+        for i, (source, target) in enumerate(((attn_ref, attn_hbm), (total_ref, total_hbm), (dq_ref, dq_hbm)))
+    ]
+    copies[0].start()
+    total_ref[...] = half(have_ref, columns, bit(stride), 0).astype(F32) + came_ref[...].astype(F32)
+    copies[1].start()
     cols = cols_ref[...]
     incoming = incoming_ref[...]
-    state = jnp.zeros((C, C), F32)
-    for r in range(n):
-        starts[r] = state + jnp.exp(begin[r]) * incoming
-        if r < n - 1:
-            kw = flipped(chunk(k_ref, r)) * jnp.exp(after[r : r + 1])
-            state = jnp.exp(tot[r]) * state + mm(parts(kw, 1), twice(chunk(v_ref, r), 0))
+    for r in range(n):
+        pair = parts(chunk(dattn_ref, r), 1)
+        dscores = mm_nt(pair, twice(chunk(v_ref, r), 1)) * chunk(lower_ref, r)
+        start = chunk(starts_ref, r) + rows_ref[2 * n + r : 2 * n + r + 1, :] * incoming
+        dq = mm(parts(dscores, 1), twice(chunk(k_ref, r), 0))
+        dq = dq + cols[:, 3 * n + r : 3 * n + r + 1] * mm_nt(pair, twice(start.astype(BF16), 1))
+        dq_ref[r * C : (r + 1) * C, :] = dq.astype(BF16)
+    copies[2].start()
+    done_ref[...] = rows_ref[:n, :]
+    for copy in copies:
+        copy.wait()
+
+
+def keys_kernel(
+    q_ref, k_ref, v_ref, qt_ref, cols_ref, rows_ref, scores_ref, upper_ref, dattn_ref, order_ref, dk_ref, dv_ref
+):
+    n = rows_ref.shape[0] // 3
+    cols = cols_ref[...]
     future = jnp.zeros((C, C), F32)
     for r in reversed(range(n)):
-        q, k, v = chunk(q_ref, r), chunk(k_ref, r), chunk(v_ref, r)
+        k, v = chunk(k_ref, r), chunk(v_ref, r)
         dattn = chunk(dattn_ref, r)
         pair = parts(dattn, 1)
-        up, down = upto[r : r + 1], cols[:, r : r + 1]
         lead, tail = cols[:, 3 * n + r : 3 * n + r + 1], cols[:, 4 * n + r : 4 * n + r + 1]
-        lower = jnp.where(row >= col, jnp.exp(jnp.minimum(down - up, 0.0)), 0.0)
-        upper = jnp.where(row <= col, jnp.exp(jnp.minimum(up - down, 0.0)), 0.0)
-        v2 = twice(v, 1)
-        dscores = mm_nt(pair, v2) * lower
-        start = twice(starts[r].astype(BF16), 1)
-        dq = mm(parts(dscores, 1), twice(k, 0)) + lead * mm_nt(pair, start)
-        dq_ref[r * C : (r + 1) * C, :] = dq.astype(BF16)
-        scores_t = mm_nt(k, q) * upper
-        dscores_t = mm_nt(v2, pair) * upper
-        high, low = split(dattn)
-        s_high, s_low = split(scores_t)
-        dk = mm(parts(dscores_t, 1), twice(q, 0))
-        dv = mm(jnp.concatenate([s_high, s_low], 1), twice(high, 0)) + mm(s_high, low)
+        dscores_t = mm_nt(twice(v, 1), pair) * chunk(upper_ref, r)
+        scores = chunk(scores_ref, r)
+        dk = mm(parts(dscores_t, 1), twice(chunk(q_ref, r), 0))
+        dv = mm(scores, twice(pair[:, :C], 0)) + mm(scores[:, :C], pair[:, C:])
         if r < n - 1:
             dk = dk + tail * mm_nt(twice(v, 1), parts(future, 1))
             dv = dv + tail * mm(twice(k, 1), parts(future, 0))
         dk_ref[r * C : (r + 1) * C, :] = dk
         dv_ref[r * C : (r + 1) * C, :] = dv
         if r > 0:
-            both = mm(flipped(q).astype(BF16), parts(lead * dattn, 1))
-            future = jnp.exp(tot[r]) * future + both[:, :C] + both[:, C:]
+            both = mm(qt_ref[:, r * C : (r + 1) * C], parts(lead * dattn, 1))
+            future = rows_ref[n + r : n + r + 1, :] * future + both[:, :C] + both[:, C:]
 
 
 def last_kernel(levels, dk_ref, dv_ref, k_ref, v_ref, cols_ref, weights_ref, *refs):
-    received, (out_k_ref, out_v_ref) = refs[:-2], refs[-2:]
+    received, (k_hbm, v_hbm, out_k_ref, out_v_ref, sems) = refs[:-5], refs[-5:]
+    copies = [pltpu.make_async_copy(out_k_ref, k_hbm, sems.at[0]), pltpu.make_async_copy(out_v_ref, v_hbm, sems.at[1])]
     n = dk_ref.shape[0] // C
     future = jnp.zeros((C, C), F32)
     at, taken = 0, 0
@@ -273,19 +305,52 @@
     for r in range(n):
         tail = cols[:, 2 * n + r : 2 * n + r + 1]
         dk = chunk(dk_ref, r) + tail * mm_nt(twice(chunk(v_ref, r), 1), wide)
+        out_k_ref[r * C : (r + 1) * C, :] = dk.astype(BF16)
+    copies[0].start()
+    for r in range(n):
+        tail = cols[:, 2 * n + r : 2 * n + r + 1]
         dv = chunk(dv_ref, r) + tail * mm(twice(chunk(k_ref, r), 1), tall)
-        out_k_ref[r * C : (r + 1) * C, :] = dk.astype(BF16)
         out_v_ref[r * C : (r + 1) * C, :] = dv.astype(BF16)
-
-
-def call(body, shapes, name, scratch=(), flops=0, moved=1 << 20):
+    copies[1].start()
+    for copy in copies:
+        copy.wait()
+
+
+def half(ref, columns, odd, i):
+    return ref[:, pl.ds(pl.multiple_of((2 * i + odd) * columns, C), columns)]
+
+
+def bit(stride):
+    return lax.rem(lax.div(lax.axis_index("dp"), stride), 2)
+
+
+def cut_kernel(columns, have_ref, order_ref, sent_ref):
+    for i in range(have_ref.shape[1] // columns // 2):
+        sent_ref[:, i * columns : (i + 1) * columns] = half(have_ref, columns, 1 - bit(1), i)
+
+
+def add_kernel(columns, stride, have_ref, came_ref, kept_ref, sent_ref):
+    for i in range(have_ref.shape[1] // columns // 2):
+        kept = half(have_ref, columns, bit(stride), i).astype(F32)
+        kept_ref[:, i * columns : (i + 1) * columns] = kept + came_ref[:, i * columns : (i + 1) * columns].astype(F32)
+    for i in range(kept_ref.shape[1] // columns // 2):
+        sent_ref[:, i * columns : (i + 1) * columns] = half(kept_ref, columns, 1 - bit(2 * stride), i).astype(BF16)
+
+
+def call(body, shapes, name, scratch=(), in_specs=None, out_specs=None, flops=0, moved=1024, vmem=32 << 20):
+    specs = {}
+    if in_specs is not None:
+        specs["in_specs"] = in_specs
+    if out_specs is not None:
+        specs["out_specs"] = out_specs
     return pl.pallas_call(
         body,
         out_shape=shapes,
         scratch_shapes=scratch,
         name=name,
-        compiler_params=pltpu.CompilerParams(vmem_limit_bytes=32 * 1024 * 1024),
+        compiler_params=pltpu.CompilerParams(vmem_limit_bytes=vmem),
         cost_estimate=pl.CostEstimate(flops=flops, bytes_accessed=moved, transcendentals=0),
+        **specs,
     )
 
 
@@ -313,49 +378,78 @@
     square = shape((C, C), F32)
     wide, narrow = shape((tokens, C), F32), shape((tokens, C), BF16)
 
-    own = [call(state_kernel, payload, "state")(k, v, decay)]
+    away = pl.BlockSpec(memory_space=pltpu.HBM)
+    here = pl.BlockSpec(memory_space=pltpu.VMEM)
+    whole = pltpu.VMEM((tokens, C), BF16)
+    dma = pltpu.SemaphoreType.DMA
+
+    own = [
+        call(
+            state_kernel,
+            payload,
+            "state",
+            scratch=[whole, whole, pltpu.VMEM((n, C), F32), dma((3,))],
+            in_specs=[away] * 3,
+        )(*[pltpu.with_memory_space_constraint(x, pltpu.HBM) for x in (k, v, decay)])
+    ]
+    grads = prev_grads[0]
+    lines = grads.shape[0]
+    columns = grads.shape[1] // dp
     others = []
     for i, (stride, radix) in enumerate(levels):
         got = [swap(own[-1], "seq", seq, stride, radix, d) for d in range(1, radix)]
         others += got
+        if i == 0:
+            sent = call(functools.partial(cut_kernel, columns), shape((lines, grads.shape[1] // 2), BF16), "cut")(grads, own[0])
+            came = swap(sent, "dp", dp, 1, 2, 1)
+            total, part = grads, 1
+            while 2 * part < dp:
+                kept, sent = shape((lines, total.shape[1] // 2), F32), shape((lines, total.shape[1] // 4), BF16)
+                total, sent = call(functools.partial(add_kernel, columns, part), (kept, sent), "add")(total, came)
+                part *= 2
+                came = swap(sent, "dp", dp, part, 2, 1)
         if i < len(levels) - 1:
-            own.append(call(functools.partial(fold_kernel, stride, radix), payload, "fold")(own[-1], *got))
-    local_out, cols, qt = call(forward_kernel, (wide, square, shape((C, tokens), BF16)), "forward")(
-        q, k, v, decay, own[-1]
-    )
-
+            fold = functools.partial(fold_kernel, stride, radix)
+            own.append(call(fold, payload, "fold")(own[-1], *got, *([total] if i == 0 else [])))
+    local_out, cols, rows, qt, starts, lower = call(
+        forward_kernel, (wide, square, shape((3 * n, C), F32), shape((C, tokens), BF16), wide, wide), "forward"
+    )(q, k, v, decay, own[-1])
+    scores_t, upper = call(turned_kernel, (shape((tokens, 2 * C), BF16), wide), "turned")(q, k, cols, rows, own[-1])
     count = sum(2 * radix - 1 for _, radix in levels)
     count += -count % 8
-    attn_out, dattn, incoming, state, weights = call(
+    attention, dattn, incoming, state, weights = call(
         functools.partial(norm_kernel, levels, count),
         (narrow, wide, square, shape((C, C), BF16), shape((count, C), F32)),
         "norm",
-    )(local_out, q, qt, dy, cols, *own, *others)
-
+    )(local_out, q, qt, dy, cols, *own, *others, scores_t)
+
+    attn_out, grad_query, grad_shard, done = call(
+        functools.partial(queries_kernel, columns, dp // 2),
+        (narrow, narrow, shape((lines, columns), F32), shape((n, C), F32)),
+        "queries",
+        scratch=[whole, pltpu.VMEM((lines, columns), F32), dma((3,))],
+        in_specs=[here] * 12,
+        out_specs=(away, away, away, here),
+    )(k, v, cols, rows, starts, lower, dattn, incoming, state, attention, total, came)
     received = []
     at = 0
     for i, (stride, radix) in enumerate(levels):
         got = [swap(state, "seq", seq, stride, radix, d) for d in range(1, radix)]
         received += got
         if i < len(levels) - 1:
-            fold = functools.partial(fold_back_kernel, at + radix - 1)
-            state = call(fold, shape((C, C), BF16), "fold_back")(state, *got, weights)
+            fold = functools.partial(fold_back_kernel, at + radix - 1, radix)
+            state = call(fold, shape((C, C), BF16), "fold_back")(state, *got, weights, done)
         at += 2 * radix - 1
-    grad_query, dk, dv = call(
-        backward_kernel, (narrow, wide, wide), "backward", scratch=[pltpu.VMEM((n, C, C), F32)]
-    )(q, k, v, decay, cols, dattn, incoming, state)
-    grad_key, grad_value = call(functools.partial(last_kernel, levels), (narrow, narrow), "last")(
-        dk, dv, k, v, cols, weights, *received
-    )
-
-    mine = lax.axis_index("dp")
-    grads = prev_grads[0]
-    columns = grads.shape[1] // dp
-    total = lax.dynamic_slice_in_dim(grads, mine * columns, columns, 1).astype(F32)
-    for d in range(1, dp):
-        away = lax.dynamic_slice_in_dim(grads, (mine ^ d) * columns, columns, 1)
-        total = total + swap(away, "dp", dp, 1, dp, d).astype(F32)
-    return attn_out[None], grad_query[None], grad_key[None], grad_value[None], total
+    dk, dv = call(keys_kernel, (wide, wide), "keys")(q, k, v, qt, cols, rows, scores_t, upper, dattn, state)
+    grad_key, grad_value = call(
+        functools.partial(last_kernel, levels),
+        (narrow, narrow),
+        "last",
+        scratch=[whole, whole, dma((2,))],
+        in_specs=[here] * (6 + len(received)),
+        out_specs=(away, away),
+    )(dk, dv, k, v, cols, weights, *received)
+    return attn_out[None], grad_query[None], grad_key[None], grad_value[None], grad_shard
 
 
 def solution(mesh):

time: 36.8 us -> 30 us (0.82)
  waiting for transfers between devices: 6.93 us -> 4.15 us
  local copies, waits for them, and re-layouts: 2.62 us -> 0.03 us
  starting transfers between devices: 17.1 us -> 15.4 us
  Pallas kernels: 8.57 us -> 9.48 us
  other arithmetic: 0.73 us -> 0 us
    ppermute x11 -> x10, waiting for transfers between devices: 6.93 us -> 4.15 us  [swap(): return lax.ppermute(x, axis, pairs)]
    unnamed x16 -> x12, local copies, waits for them, and re-layouts: 2.6 us -> 0.03 us
    ppermute x11 -> x10, starting transfers between devices: 17.1 us -> 15.4 us  [swap(): return lax.ppermute(x, axis, pairs)]
    pallas_call x6 -> x10, Pallas kernels: 6.91 us -> 8.37 us  [the longest x1 1.76 us: local(): call(forward_kernel, (wide, square, shape((3 * n, C), F32), shape((C, tok...]
    add x1 -> x0, other arithmetic: 0.73 us -> none  [local(): total = total + swap(away, 'dp', dp, 1, dp, d).astype(F32)]
    pallas_call x1, Pallas kernels: 1.66 us -> 1.11 us  [local(): call(functools.partial(norm_kernel, levels, count), (narrow, wide, square...]
  transfers between devices with their start and end apart: 11 -> 10, of which waited for: 3 -> 4; matrix products, arithmetic and copies ran while one was open for 2% -> 0% of each run, Pallas kernels for 19% -> 23%
where the time goes in v2:
time: 30 us; the launch traced here: 29.8 us
  starting transfers between devices  15.4 us (51%)
  Pallas kernels  9.48 us (32%)
  waiting for transfers between devices  4.15 us (14%)
  between operations  0.76 us (3%)
    ppermute x10, starting transfers between devices, swap(): return lax.ppermute(x, axis, pairs)  15.4 us
    ppermute x10, waiting for transfers between devices, swap(): return lax.ppermute(x, axis, pairs)  4.15 us
    pallas_call x1, Pallas kernels, local(): call(forward_kernel, (wide, square, shape((3 * n, C), F32), shape((C, tok...  1.76 us
    pallas_call x1, Pallas kernels, local(): call(functools.partial(queries_kernel, columns, dp // 2), (narrow, narrow...  1.74 us
    pallas_call x1, Pallas kernels, local(): call(keys_kernel, (wide, wide), 'keys')  1.72 us
    pallas_call x1, Pallas kernels, local(): call(state_kernel, payload, 'state', scratch=[whole, whole, pltpu.VMEM((n...  1.49 us
    pallas_call x1, Pallas kernels, local(): call(functools.partial(last_kernel, levels), (narrow, narrow), 'last', sc...  1.19 us
    pallas_call x1, Pallas kernels, local(): call(functools.partial(norm_kernel, levels, count), (narrow, wide, square...  1.11 us
  transfers between devices with their start and end apart: 10, of which 4 were waited for; matrix products, arithmetic and copies ran while one was open for 0% of the time, Pallas kernels for 23%

profile of v2, /device:TPU:0, one launch (start us, length us, event | category | flops | bytes accessed | tf_op | source)
XLA Modules:
  0.0 29.8 jit_solution(10354952260474340775)
XLA Ops:
  0.6 0.0 copy-start.3
  0.6 1.5 %state.1.order_ref.own_ref.refs_0_ = bf16[136,128]{1,0:T(8,128)(2,1)S(1)} custom-call(bf16[1024,128]{1,0:T(8,128)(2,1)} %bitcast.10, bf16[1024,128]{1,0:T(8,128)(2,1)} %bitcast.16, f32[8,128]{1,0:T(8,128)} %bitcast.28), custom_call_target="tpu_custom_call" | custom-call | bytes 1024 | tf_op jit(solution)/shard_map/state/pallas_call | solution.py:387
  2.1 0.0 copy-done.3
  2.2 0.5 %collective-permute-start.1 = (bf16[32,3072]{1,0:T(8,128)(2,1)S(1)}, bf16[32,3072]{1,0:T(8,128)(2,1)S(1)}, u32[]{:S(2)}, u32[]{:S(2)}) collective-permute-start(bf16[32,3072]{1,0:T(8,128)(2,1)S(1)} %cut.1), channel_id=1, source_target_pairs={{0,8},{8,0},{16,24},{24,16},{1,9},{9,1},{17,25},{25,17},{2,10},{10... | collective-permute-start | bytes 589832 | tf_op jit(solution)/shard_map/ppermute | solution.py:368
  2.7 2.6 %collective-permute-start = (bf16[136,128]{1,0:T(8,128)(2,1)S(1)}, bf16[136,128]{1,0:T(8,128)(2,1)S(1)}, u32[]{:S(2)}, u32[]{:S(2)}) collective-permute-start(bf16[136,128]{1,0:T(8,128)(2,1)S(1)} %state.1.order_ref.own_ref.refs_0_), channel_id=1, source_target_pairs={{0,1},{1,0},{2,3},{3,2},{4,5},{5,4},{6,7},{7,6},{8,9},{9,8},{10,11... | collective-permute-start | bytes 104456 | tf_op jit(solution)/shard_map/ppermute | solution.py:368
  5.3 0.0 collective-permute-done.1.came_ref
  5.3 0.0 copy-start.1
  5.3 0.0 copy-start.2
  5.3 0.1 add.1
  5.4 0.0 copy-start
  5.4 1.6 %collective-permute-start.5 = (bf16[32,1536]{1,0:T(8,128)(2,1)S(1)}, bf16[32,1536]{1,0:T(8,128)(2,1)S(1)}, u32[]{:S(2)}, u32[]{:S(2)}) collective-permute-start(bf16[32,1536]{1,0:T(8,128)(2,1)S(1)} %get-tuple-element.40), channel_id=1, source_target_pairs={{0,16},{8,24},{16,0},{24,8},{1,17},{9,25},{17,1},{25,9},{2,18},{10... | collective-permute-start | bytes 294920 | tf_op jit(solution)/shard_map/ppermute | solution.py:368
  6.9 0.3 %collective-permute-done.refs_0_.refs_2_ = bf16[136,128]{1,0:T(8,128)(2,1)S(1)} collective-permute-done((bf16[136,128]{1,0:T(8,128)(2,1)S(1)}, bf16[136,128]{1,0:T(8,128)(2,1)S(1)}, u32[]{:S(2)}, u32[]{:S(2)}) %collective-permute-start) | collective-permute-done | bytes 34848 | tf_op jit(solution)/shard_map/ppermute | solution.py:368
  7.3 0.0 copy-start.5
  7.3 4.1 %collective-permute-start.4 = (bf16[136,128]{1,0:T(8,128)(2,1)S(1)}, bf16[136,128]{1,0:T(8,128)(2,1)S(1)}, u32[]{:S(2)}, u32[]{:S(2)}) collective-permute-start(bf16[136,128]{1,0:T(8,128)(2,1)S(1)} %fold.1.order_ref.refs_1_), channel_id=1, source_target_pairs={{0,6},{1,7},{2,4},{3,5},{4,2},{5,3},{6,0},{7,1},{8,14},{9,15},{10,... | collective-permute-start | bytes 104456 | tf_op jit(solution)/shard_map/ppermute | solution.py:368
  11.4 0.0 collective-permute-start.3
  11.4 0.6 %collective-permute-start.2 = (bf16[136,128]{1,0:T(8,128)(2,1)S(1)}, bf16[136,128]{1,0:T(8,128)(2,1)S(1)}, u32[]{:S(2)}, u32[]{:S(2)}) collective-permute-start(bf16[136,128]{1,0:T(8,128)(2,1)S(1)} %fold.1.order_ref.refs_1_), channel_id=1, source_target_pairs={{0,2},{1,3},{2,0},{3,1},{4,6},{5,7},{6,4},{7,5},{8,10},{9,11},{10,... | collective-permute-start | bytes 104456 | tf_op jit(solution)/shard_map/ppermute | solution.py:368
  12.1 0.0 copy-done.1
  12.1 0.0 copy-done.2
  12.1 0.0 copy-done
  12.1 0.0 copy-done.5
  12.1 1.8 %forward.1 = (f32[1024,128]{1,0:T(8,128)S(1)}, f32[128,128]{1,0:T(8,128)S(1)}, f32[24,128]{1,0:T(8,128)S(1)}, bf16[128,1024]{1,0:T(8,128)(2,1)S(1)}, f32[1024,128]{1,0:T(8,128)S(1)}, /*index=5*/f32[1024,128]{1,0:T(8,128)S(1)}) custom-call(bf16[1024,128]{1,0:T(8,128)(2,1)S(1)} %bitcast.21, bf16[1024,128]{1,0:T(8,128)(2,1)S(1)} %bitcast.11, ...), custom_call_target="tpu_custom_call" | custom-call | bytes 1024 | tf_op jit(solution)/shard_map/forward/pallas_call | solution.py:414
  13.8 0.0 copy-start.4
  13.9 0.3 %turned.1 = (bf16[1024,256]{1,0:T(8,128)(2,1)S(1)}, f32[1024,128]{1,0:T(8,128)S(1)}) custom-call(bf16[1024,128]{1,0:T(8,128)(2,1)S(1)} %bitcast.22, bf16[1024,128]{1,0:T(8,128)(2,1)S(1)} %bitcast.12, f32[128,128]{1,0:T(8,128)S(1)} %get-tuple-element.29.cols_ref, f32[24,128]{1,0:T(8,128)S(1)} %get-tuple-element.30.rows_ref, ...), custom_call_target="tpu_custom_call" | custom-call | bytes 1024 | tf_op jit(solution)/shard_map/turned/pallas_call | solution.py:417
  14.2 0.0 collective-permute-done.4.refs_5_
  14.2 2.1 %collective-permute-done.3.refs_4_ = bf16[136,128]{1,0:T(8,128)(2,1)S(1)} collective-permute-done((bf16[136,128]{1,0:T(8,128)(2,1)S(1)}, bf16[136,128]{1,0:T(8,128)(2,1)S(1)}, u32[]{:S(2)}, u32[]{:S(2)}) %collective-permute-start.3) | collective-permute-done | bytes 34848 | tf_op jit(solution)/shard_map/ppermute | solution.py:368
  16.3 0.0 collective-permute-done.2.refs_3_
  16.3 0.0 copy-done.4
  16.3 1.1 %norm.1 = (bf16[1024,128]{1,0:T(8,128)(2,1)S(1)}, f32[1024,128]{1,0:T(8,128)S(1)}, f32[128,128]{1,0:T(8,128)S(1)}, bf16[128,128]{1,0:T(8,128)(2,1)S(1)}, f32[16,128]{1,0:T(8,128)S(1)}) custom-call(f32[1024,128]{1,0:T(8,128)S(1)} %get-tuple-element.33.local_ref, bf16[1024,128]{1,0:T(8,128)(2,1)S(1)} %bitcast.23, ...), custom_call_target="tpu_custom_call" | custom-call | bytes 1024 | tf_op jit(solution)/shard_map/norm/pallas_call | solution.py:420
  17.4 1.6 %collective-permute-start.6 = (bf16[128,128]{1,0:T(8,128)(2,1)S(1)}, bf16[128,128]{1,0:T(8,128)(2,1)S(1)}, u32[]{:S(2)}, u32[]{:S(2)}) collective-permute-start(bf16[128,128]{1,0:T(8,128)(2,1)S(1)} %get-tuple-element.38.order_ref.own_ref), channel_id=1, source_target_pairs={{0,1},{1,0},{2,3},{3,2},{4,5},{5,4},{6,7},{7,6},{8,9},{9,8},{10,11... | collective-permute-start | bytes 98312 | tf_op jit(solution)/shard_map/ppermute | solution.py:368
  18.9 0.0 collective-permute-done.5.refs_2_
  19.0 1.7 %queries.1 = (bf16[1024,128]{1,0:T(8,128)(2,1)}, bf16[1024,128]{1,0:T(8,128)(2,1)}, f32[32,1536]{1,0:T(8,128)}, f32[8,128]{1,0:T(8,128)S(1)}) custom-call(bf16[1024,128]{1,0:T(8,128)(2,1)S(1)} %bitcast.13, bf16[1024,128]{1,0:T(8,128)(2,1)S(1)} %bitcast.18, f32[128,128]{1,0:T(8,128)S(1)} %get-tuple-element.29.cols_ref, ...), custom_call_target="tpu_custom_call" | custom-call | bytes 1024 | tf_op jit(solution)/shard_map/queries/pallas_call | solution.py:426
  20.7 0.7 %collective-permute-done.6.refs_0_ = bf16[128,128]{1,0:T(8,128)(2,1)S(1)} collective-permute-done((bf16[128,128]{1,0:T(8,128)(2,1)S(1)}, bf16[128,128]{1,0:T(8,128)(2,1)S(1)}, u32[]{:S(2)}, u32[]{:S(2)}) %collective-permute-start.6) | collective-permute-done | bytes 32800 | tf_op jit(solution)/shard_map/ppermute | solution.py:368
  21.4 2.3 %collective-permute-start.9 = (bf16[128,128]{1,0:T(8,128)(2,1)S(1)}, bf16[128,128]{1,0:T(8,128)(2,1)S(1)}, u32[]{:S(2)}, u32[]{:S(2)}) collective-permute-start(bf16[128,128]{1,0:T(8,128)(2,1)S(1)} %fold_back.1.order_ref), channel_id=1, source_target_pairs={{0,6},{1,7},{2,4},{3,5},{4,2},{5,3},{6,0},{7,1},{8,14},{9,15},{10,... | collective-permute-start | bytes 98312 | tf_op jit(solution)/shard_map/ppermute | solution.py:368
  23.7 0.0 collective-permute-start.8
  23.7 2.1 %collective-permute-start.7 = (bf16[128,128]{1,0:T(8,128)(2,1)S(1)}, bf16[128,128]{1,0:T(8,128)(2,1)S(1)}, u32[]{:S(2)}, u32[]{:S(2)}) collective-permute-start(bf16[128,128]{1,0:T(8,128)(2,1)S(1)} %fold_back.1.order_ref), channel_id=1, source_target_pairs={{0,2},{1,3},{2,0},{3,1},{4,6},{5,7},{6,4},{7,5},{8,10},{9,11},{10,... | collective-permute-start | bytes 98312 | tf_op jit(solution)/shard_map/ppermute | solution.py:368
  25.8 1.7 %keys.1 = (f32[1024,128]{1,0:T(8,128)S(1)}, f32[1024,128]{1,0:T(8,128)S(1)}) custom-call(bf16[1024,128]{1,0:T(8,128)(2,1)S(1)} %bitcast.24, bf16[1024,128]{1,0:T(8,128)(2,1)S(1)} %bitcast.14, bf16[1024,128]{1,0:T(8,128)(2,1)S(1)} %bitcast.19, bf16[128,1024]{1,0:T(8,128)(2,1)S(1)} %get-tuple-element.34.qt_ref, f32[128,128]{1,0:T(8,128)S(1)} %get-tuple-element.29.cols_ref, ...), custom_call_target="tpu_custom_call" | custom-call | bytes 1024 | tf_op jit(solution)/shard_map/keys/pallas_call | solution.py:443
  27.6 0.0 collective-permute-done.9.refs_3_
  27.6 1.1 %collective-permute-done.8.refs_2_ = bf16[128,128]{1,0:T(8,128)(2,1)S(1)} collective-permute-done((bf16[128,128]{1,0:T(8,128)(2,1)S(1)}, bf16[128,128]{1,0:T(8,128)(2,1)S(1)}, u32[]{:S(2)}, u32[]{:S(2)}) %collective-permute-start.8) | collective-permute-done | bytes 32800 | tf_op jit(solution)/shard_map/ppermute | solution.py:368
  28.6 0.0 collective-permute-done.7.refs_1_
  28.6 1.2 %last.1 = (bf16[1024,128]{1,0:T(8,128)(2,1)}, bf16[1024,128]{1,0:T(8,128)(2,1)}) custom-call(f32[1024,128]{1,0:T(8,128)S(1)} %get-tuple-element.46.dk_ref, f32[1024,128]{1,0:T(8,128)S(1)} %get-tuple-element.47.dv_ref, bf16[1024,128]{1,0:T(8,128)(2,1)S(1)} %bitcast.15, bf16[1024,128]{1,0:T(8,128)(2,1)S(1)} %bitcast.20, ...), custom_call_target="tpu_custom_call" | custom-call | bytes 1024 | tf_op jit(solution)/shard_map/last/pallas_call | solution.py:444
  (3 shorter events, 0.1 us)
Async XLA Ops:
  0.6 1.5 %copy-start.3 = (bf16[1,32,6144]{2,1,0:T(8,128)(2,1)S(1)}, bf16[1,32,6144]{2,1,0:T(8,128)(2,1)}, u32[]{:S(2)}) copy-start(bf16[1,32,6144]{2,1,0:T(8,128)(2,1)} %param.11) | copy-start | bytes 1179652
  2.2 3.1 %collective-permute-start.1 = (bf16[32,3072]{1,0:T(8,128)(2,1)S(1)}, bf16[32,3072]{1,0:T(8,128)(2,1)S(1)}, u32[]{:S(2)}, u32[]{:S(2)}) collective-permute-start(bf16[32,3072]{1,0:T(8,128)(2,1)S(1)} %cut.1), channel_id=1, source_target_pairs={{0,8},{8,0},{16,24},{24,16},{1,9},{9,1},{17,25},{25,17},{2,10},{10... | collective-permute-start | bytes 589832 | tf_op jit(solution)/shard_map/ppermute | solution.py:368
  2.7 4.6 %collective-permute-start = (bf16[136,128]{1,0:T(8,128)(2,1)S(1)}, bf16[136,128]{1,0:T(8,128)(2,1)S(1)}, u32[]{:S(2)}, u32[]{:S(2)}) collective-permute-start(bf16[136,128]{1,0:T(8,128)(2,1)S(1)} %state.1.order_ref.own_ref.refs_0_), channel_id=1, source_target_pairs={{0,1},{1,0},{2,3},{3,2},{4,5},{5,4},{6,7},{7,6},{8,9},{9,8},{10,11... | collective-permute-start | bytes 104456 | tf_op jit(solution)/shard_map/ppermute | solution.py:368
  5.3 6.8 %copy-start.1 = (bf16[1,1024,128]{2,1,0:T(8,128)(2,1)S(1)}, bf16[1,1024,128]{2,1,0:T(8,128)(2,1)}, u32[]{:S(2)}) copy-start(bf16[1,1024,128]{2,1,0:T(8,128)(2,1)} %param.8) | copy-start | bytes 786436
  5.3 6.8 %copy-start.2 = (bf16[1,1024,128]{2,1,0:T(8,128)(2,1)S(1)}, bf16[1,1024,128]{2,1,0:T(8,128)(2,1)}, u32[]{:S(2)}) copy-start(bf16[1,1024,128]{2,1,0:T(8,128)(2,1)} %param.6) | copy-start | bytes 786436
  5.4 6.7 %copy-start = (bf16[1,1024,128]{2,1,0:T(8,128)(2,1)S(1)}, bf16[1,1024,128]{2,1,0:T(8,128)(2,1)}, u32[]{:S(2)}) copy-start(bf16[1,1024,128]{2,1,0:T(8,128)(2,1)} %param.7) | copy-start | bytes 786436
  5.4 13.6 %collective-permute-start.5 = (bf16[32,1536]{1,0:T(8,128)(2,1)S(1)}, bf16[32,1536]{1,0:T(8,128)(2,1)S(1)}, u32[]{:S(2)}, u32[]{:S(2)}) collective-permute-start(bf16[32,1536]{1,0:T(8,128)(2,1)S(1)} %get-tuple-element.40), channel_id=1, source_target_pairs={{0,16},{8,24},{16,0},{24,8},{1,17},{9,25},{17,1},{25,9},{2,18},{10... | collective-permute-start | bytes 294920 | tf_op jit(solution)/shard_map/ppermute | solution.py:368
  7.3 4.8 %copy-start.5 = (f32[1,1,1024]{2,1,0:T(1,128)S(1)}, f32[1,1,1024]{2,1,0:T(1,128)}, u32[]{:S(2)}) copy-start(f32[1,1,1024]{2,1,0:T(1,128)} %param.10) | copy-start | bytes 12292
  7.3 6.9 %collective-permute-start.4 = (bf16[136,128]{1,0:T(8,128)(2,1)S(1)}, bf16[136,128]{1,0:T(8,128)(2,1)S(1)}, u32[]{:S(2)}, u32[]{:S(2)}) collective-permute-start(bf16[136,128]{1,0:T(8,128)(2,1)S(1)} %fold.1.order_ref.refs_1_), channel_id=1, source_target_pairs={{0,6},{1,7},{2,4},{3,5},{4,2},{5,3},{6,0},{7,1},{8,14},{9,15},{10,... | collective-permute-start | bytes 104456 | tf_op jit(solution)/shard_map/ppermute | solution.py:368
  11.4 4.8 %collective-permute-start.3 = (bf16[136,128]{1,0:T(8,128)(2,1)S(1)}, bf16[136,128]{1,0:T(8,128)(2,1)S(1)}, u32[]{:S(2)}, u32[]{:S(2)}) collective-permute-start(bf16[136,128]{1,0:T(8,128)(2,1)S(1)} %fold.1.order_ref.refs_1_), channel_id=1, source_target_pairs={{0,4},{1,5},{2,6},{3,7},{4,0},{5,1},{6,2},{7,3},{8,12},{9,13},{10,... | collective-permute-start | bytes 104456 | tf_op jit(solution)/shard_map/ppermute | solution.py:368
  11.4 4.8 %collective-permute-start.2 = (bf16[136,128]{1,0:T(8,128)(2,1)S(1)}, bf16[136,128]{1,0:T(8,128)(2,1)S(1)}, u32[]{:S(2)}, u32[]{:S(2)}) collective-permute-start(bf16[136,128]{1,0:T(8,128)(2,1)S(1)} %fold.1.order_ref.refs_1_), channel_id=1, source_target_pairs={{0,2},{1,3},{2,0},{3,1},{4,6},{5,7},{6,4},{7,5},{8,10},{9,11},{10,... | collective-permute-start | bytes 104456 | tf_op jit(solution)/shard_map/ppermute | solution.py:368
  13.8 2.4 %copy-start.4 = (bf16[1,1024,128]{2,1,0:T(8,128)(2,1)S(1)}, bf16[1,1024,128]{2,1,0:T(8,128)(2,1)}, u32[]{:S(2)}) copy-start(bf16[1,1024,128]{2,1,0:T(8,128)(2,1)} %param.9) | copy-start | bytes 786436
  17.4 4.0 %collective-permute-start.6 = (bf16[128,128]{1,0:T(8,128)(2,1)S(1)}, bf16[128,128]{1,0:T(8,128)(2,1)S(1)}, u32[]{:S(2)}, u32[]{:S(2)}) collective-permute-start(bf16[128,128]{1,0:T(8,128)(2,1)S(1)} %get-tuple-element.38.order_ref.own_ref), channel_id=1, source_target_pairs={{0,1},{1,0},{2,3},{3,2},{4,5},{5,4},{6,7},{7,6},{8,9},{9,8},{10,11... | collective-permute-start | bytes 98312 | tf_op jit(solution)/shard_map/ppermute | solution.py:368
  21.4 6.2 %collective-permute-start.9 = (bf16[128,128]{1,0:T(8,128)(2,1)S(1)}, bf16[128,128]{1,0:T(8,128)(2,1)S(1)}, u32[]{:S(2)}, u32[]{:S(2)}) collective-permute-start(bf16[128,128]{1,0:T(8,128)(2,1)S(1)} %fold_back.1.order_ref), channel_id=1, source_target_pairs={{0,6},{1,7},{2,4},{3,5},{4,2},{5,3},{6,0},{7,1},{8,14},{9,15},{10,... | collective-permute-start | bytes 98312 | tf_op jit(solution)/shard_map/ppermute | solution.py:368
  23.7 4.9 %collective-permute-start.8 = (bf16[128,128]{1,0:T(8,128)(2,1)S(1)}, bf16[128,128]{1,0:T(8,128)(2,1)S(1)}, u32[]{:S(2)}, u32[]{:S(2)}) collective-permute-start(bf16[128,128]{1,0:T(8,128)(2,1)S(1)} %fold_back.1.order_ref), channel_id=1, source_target_pairs={{0,4},{1,5},{2,6},{3,7},{4,0},{5,1},{6,2},{7,3},{8,12},{9,13},{10,... | collective-permute-start | bytes 98312 | tf_op jit(solution)/shard_map/ppermute | solution.py:368
  23.7 4.9 %collective-permute-start.7 = (bf16[128,128]{1,0:T(8,128)(2,1)S(1)}, bf16[128,128]{1,0:T(8,128)(2,1)S(1)}, u32[]{:S(2)}, u32[]{:S(2)}) collective-permute-start(bf16[128,128]{1,0:T(8,128)(2,1)S(1)} %fold_back.1.order_ref), channel_id=1, source_target_pairs={{0,2},{1,3},{2,0},{3,1},{4,6},{5,7},{6,4},{7,5},{8,10},{9,11},{10,... | collective-permute-start | bytes 98312 | tf_op jit(solution)/shard_map/ppermute | solution.py:368

commit v3 on v2

--- a/solution.py
+++ b/solution.py
@@ -11,6 +11,7 @@
 C = 128
 F32 = jnp.float32
 BF16 = jnp.bfloat16
+FORWARD_OF_4 = ((2, 0, 3, 1), (3, 2, 1, 0), (1, 3, 0, 2))
 LOGS = 8
 
 
@@ -115,14 +116,15 @@
     return out
 
 
-def place(stride, radix):
-    return lax.rem(lax.div(lax.axis_index("seq"), stride), radix)
-
-
-def fold_kernel(stride, radix, own_ref, *refs):
+def places(stride, radix, rounds):
+    mine = lax.rem(lax.div(lax.axis_index("seq"), stride), radix)
+    senders = [sum(jnp.where(mine == to, at, 0) for at, to in enumerate(targets)) for targets in rounds]
+    return [mine, *senders]
+
+
+def fold_kernel(stride, radix, rounds, own_ref, *refs):
     out_ref = refs[-1]
-    mine = place(stride, radix)
-    positions = [mine ^ d for d in range(radix)]
+    positions = places(stride, radix, rounds)
     all_refs = [own_ref, *refs[: radix - 1]]
     logs = [read_log(ref) for ref in all_refs]
     total = jnp.zeros((C, C), F32)
@@ -134,7 +136,7 @@
 
 
 def forward_kernel(
-    q_ref, k_ref, v_ref, decay_ref, order_ref, out_ref, cols_ref, rows_ref, qt_ref, starts_ref, lower_ref
+    q_ref, k_ref, v_ref, decay_ref, order_ref, dy_ref, out_ref, cols_ref, rows_ref, qt_ref, starts_ref, lower_ref, *wide_refs
 ):
     upto, after = sums(decay_ref[...])
     tot = totals(upto)
@@ -165,6 +167,8 @@
         if r > 0:
             out = out + cols[:, 3 * n + r : 3 * n + r + 1] * mm(twice(q, 1), parts(state, 0))
         out_ref[r * C : (r + 1) * C, :] = out
+        for i, ref in enumerate(wide_refs, 1):
+            ref[r * C : (r + 1) * C, :] = jnp.broadcast_to(cols[:, i * n + r : i * n + r + 1], (C, C))
         qt_ref[:, r * C : (r + 1) * C] = flipped(q).astype(BF16)
         starts_ref[r * C : (r + 1) * C, :] = state
         if r < n - 1:
@@ -184,7 +188,7 @@
         scores_ref[r * C : (r + 1) * C, :] = parts(mm_nt(chunk(k_ref, r), chunk(q_ref, r)) * upper, 1)
 
 
-def norm_kernel(levels, count, local_ref, q_ref, qt_ref, dy_ref, cols_ref, *refs):
+def norm_kernel(levels, count, local_ref, q_ref, qt_ref, dy_ref, lead_ref, *refs):
     received, (attn_ref, dattn_ref, incoming_ref, state_ref, weights_ref) = refs[:-5], refs[-5:]
     n = local_ref.shape[0] // C
     own, others = received[: len(levels)], received[len(levels) :]
@@ -193,19 +197,21 @@
     behind = jnp.zeros((1, C), F32)
     weights = []
     at = 0
-    for (stride, radix), own_ref in zip(levels, own, strict=True):
-        mine = place(stride, radix)
-        positions = [mine ^ d for d in range(radix)]
+    for (stride, radix, rounds, back_rounds), own_ref in zip(levels, own, strict=True):
+        positions = places(stride, radix, rounds)
+        mine = positions[0]
         level = [own_ref, *others[at : at + radix - 1]]
         at += radix - 1
         logs = [read_log(ref) for ref in level]
         for ref, position in zip(level[1:], positions[1:], strict=True):
             weight = jnp.where(position < mine, jnp.exp(ahead + between(logs, positions, position, mine)), 0.0)
             incoming = incoming + weight * ref[:C, :].astype(F32)
+        senders = places(stride, radix, back_rounds)
+        for position in senders[1:]:
             weights.append(
                 jnp.where(position > mine, jnp.exp(behind + between(logs, positions, mine, position)), 0.0)
             )
-        for position in positions:
+        for position in senders:
             weights.append(jnp.exp(between(logs, positions, -1, position)))
         ahead = ahead + between(logs, positions, -1, mine)
         behind = behind + between(logs, positions, mine, radix)
@@ -213,10 +219,9 @@
     weights_ref[...] = jnp.concatenate(weights, axis=0)
     incoming_ref[...] = incoming
     incoming = parts(incoming, 0)
-    cols = cols_ref[...]
     state = jnp.zeros((C, C), F32)
     for r in range(n):
-        lead = cols[:, n + r : n + r + 1]
+        lead = chunk(lead_ref, r)
         attention = chunk(local_ref, r) + lead * mm(twice(chunk(q_ref, r), 1), incoming)
         dy = chunk(dy_ref, r).astype(F32)
         ratio = lax.rsqrt(jnp.mean(attention * attention, axis=1, keepdims=True) + NORM_EPS)
@@ -289,29 +294,29 @@
             future = rows_ref[n + r : n + r + 1, :] * future + both[:, :C] + both[:, C:]
 
 
-def last_kernel(levels, dk_ref, dv_ref, k_ref, v_ref, cols_ref, weights_ref, *refs):
+def last_kernel(levels, dk_ref, dv_ref, k_ref, v_ref, tail_ref, weights_ref, *refs):
     received, (k_hbm, v_hbm, out_k_ref, out_v_ref, sems) = refs[:-5], refs[-5:]
-    copies = [pltpu.make_async_copy(out_k_ref, k_hbm, sems.at[0]), pltpu.make_async_copy(out_v_ref, v_hbm, sems.at[1])]
     n = dk_ref.shape[0] // C
     future = jnp.zeros((C, C), F32)
     at, taken = 0, 0
-    for _, radix in levels:
+    for _, radix, _, _ in levels:
         for d in range(radix - 1):
             future = future + weights_ref[at + d : at + d + 1, :] * received[taken + d][...].astype(F32)
         at += 2 * radix - 1
         taken += radix - 1
-    cols = cols_ref[...]
     wide, tall = parts(future, 1), parts(future, 0)
+    copies = []
     for r in range(n):
-        tail = cols[:, 2 * n + r : 2 * n + r + 1]
+        tail = chunk(tail_ref, r)
         dk = chunk(dk_ref, r) + tail * mm_nt(twice(chunk(v_ref, r), 1), wide)
         out_k_ref[r * C : (r + 1) * C, :] = dk.astype(BF16)
-    copies[0].start()
-    for r in range(n):
-        tail = cols[:, 2 * n + r : 2 * n + r + 1]
         dv = chunk(dv_ref, r) + tail * mm(twice(chunk(k_ref, r), 1), tall)
         out_v_ref[r * C : (r + 1) * C, :] = dv.astype(BF16)
-    copies[1].start()
+        if (r + 1) % (n // 2) == 0:
+            rows = pl.ds((r + 1 - n // 2) * C, n // 2 * C)
+            for source, target in ((out_k_ref, k_hbm), (out_v_ref, v_hbm)):
+                copies.append(pltpu.make_async_copy(source.at[rows], target.at[rows], sems.at[len(copies)]))
+                copies[-1].start()
     for copy in copies:
         copy.wait()
 
@@ -354,17 +359,23 @@
     )
 
 
+def exchanges(radix):
+    return tuple(tuple(at ^ d for at in range(radix)) for d in range(1, radix))
+
+
 def scan_levels(size):
     levels, stride = [], 1
     while stride < size:
         radix = 2 if stride == 1 else min(4, size // stride)
-        levels.append((stride, radix))
+        pairs = exchanges(radix)
+        levels.append((stride, radix, FORWARD_OF_4 if radix == 4 else pairs, pairs))
         stride *= radix
     return levels
 
 
-def swap(x, axis, size, stride, radix, d):
-    pairs = [(i, i - i % (stride * radix) + ((i // stride % radix) ^ d) * stride + i % stride) for i in range(size)]
+def send(x, axis, size, stride, targets):
+    radix = len(targets)
+    pairs = [(i, i + (targets[i // stride % radix] - i // stride % radix) * stride) for i in range(size)]
     return lax.ppermute(x, axis, pairs)
 
 
@@ -396,32 +407,32 @@
     lines = grads.shape[0]
     columns = grads.shape[1] // dp
     others = []
-    for i, (stride, radix) in enumerate(levels):
-        got = [swap(own[-1], "seq", seq, stride, radix, d) for d in range(1, radix)]
+    for i, (stride, radix, rounds, _) in enumerate(levels):
+        got = [send(own[-1], "seq", seq, stride, targets) for targets in rounds]
         others += got
         if i == 0:
             sent = call(functools.partial(cut_kernel, columns), shape((lines, grads.shape[1] // 2), BF16), "cut")(grads, own[0])
-            came = swap(sent, "dp", dp, 1, 2, 1)
+            came = send(sent, "dp", dp, 1, (1, 0))
             total, part = grads, 1
             while 2 * part < dp:
                 kept, sent = shape((lines, total.shape[1] // 2), F32), shape((lines, total.shape[1] // 4), BF16)
                 total, sent = call(functools.partial(add_kernel, columns, part), (kept, sent), "add")(total, came)
                 part *= 2
-                came = swap(sent, "dp", dp, part, 2, 1)
+                came = send(sent, "dp", dp, part, (1, 0))
         if i < len(levels) - 1:
-            fold = functools.partial(fold_kernel, stride, radix)
+            fold = functools.partial(fold_kernel, stride, radix, rounds)
             own.append(call(fold, payload, "fold")(own[-1], *got, *([total] if i == 0 else [])))
-    local_out, cols, rows, qt, starts, lower = call(
-        forward_kernel, (wide, square, shape((3 * n, C), F32), shape((C, tokens), BF16), wide, wide), "forward"
-    )(q, k, v, decay, own[-1])
+    local_out, cols, rows, qt, starts, lower, lead, tail = call(
+        forward_kernel, (wide, square, shape((3 * n, C), F32), shape((C, tokens), BF16), wide, wide, wide, wide), "forward"
+    )(q, k, v, decay, own[-1], dy)
     scores_t, upper = call(turned_kernel, (shape((tokens, 2 * C), BF16), wide), "turned")(q, k, cols, rows, own[-1])
-    count = sum(2 * radix - 1 for _, radix in levels)
+    count = sum(2 * radix - 1 for _, radix, _, _ in levels)
     count += -count % 8
     attention, dattn, incoming, state, weights = call(
         functools.partial(norm_kernel, levels, count),
         (narrow, wide, square, shape((C, C), BF16), shape((count, C), F32)),
         "norm",
-    )(local_out, q, qt, dy, cols, *own, *others, scores_t)
+    )(local_out, q, qt, dy, lead, *own, *others, scores_t)
 
     attn_out, grad_query, grad_shard, done = call(
         functools.partial(queries_kernel, columns, dp // 2),
@@ -433,8 +444,8 @@
     )(k, v, cols, rows, starts, lower, dattn, incoming, state, attention, total, came)
     received = []
     at = 0
-    for i, (stride, radix) in enumerate(levels):
-        got = [swap(state, "seq", seq, stride, radix, d) for d in range(1, radix)]
+    for i, (stride, radix, _, rounds) in enumerate(levels):
+        got = [send(state, "seq", seq, stride, targets) for targets in rounds]
         received += got
         if i < len(levels) - 1:
             fold = functools.partial(fold_back_kernel, at + radix - 1, radix)
@@ -445,10 +456,10 @@
         functools.partial(last_kernel, levels),
         (narrow, narrow),
         "last",
-        scratch=[whole, whole, dma((2,))],
+        scratch=[whole, whole, dma((4,))],
         in_specs=[here] * (6 + len(received)),
         out_specs=(away, away),
-    )(dk, dv, k, v, cols, weights, *received)
+    )(dk, dv, k, v, tail, weights, *received)
     return attn_out[None], grad_query[None], grad_key[None], grad_value[None], grad_shard
 
 

time: 30 us -> 28.9 us (0.963)
  waiting for transfers between devices: 4.15 us -> 1.52 us
  starting transfers between devices: 15.4 us -> 16.8 us
    ppermute x10, waiting for transfers between devices: 4.15 us -> 1.52 us  [send(): return lax.ppermute(x, axis, pairs)]
    ppermute x10, starting transfers between devices: 15.4 us -> 16.8 us  [send(): return lax.ppermute(x, axis, pairs)]
    pallas_call x1, Pallas kernels: 1.76 us -> 2.17 us  [local(): call(forward_kernel, (wide, square, shape((3 * n, C), F32), shape((C, tok...]
  transfers between devices with their start and end apart: 10 -> 10, of which waited for: 4 -> 4; matrix products, arithmetic and copies ran while one was open for 0% -> 0% of each run, Pallas kernels for 23% -> 24%
where the time goes in v3:
time: 28.9 us; the launch traced here: 28.7 us
  starting transfers between devices  16.8 us (58%)
  Pallas kernels  9.62 us (33%)
  waiting for transfers between devices  1.52 us (5%)
  between operations  0.79 us (3%)
    ppermute x10, starting transfers between devices, send(): return lax.ppermute(x, axis, pairs)  16.8 us
    pallas_call x1, Pallas kernels, local(): call(forward_kernel, (wide, square, shape((3 * n, C), F32), shape((C, tok...  2.17 us
    pallas_call x1, Pallas kernels, local(): call(functools.partial(queries_kernel, columns, dp // 2), (narrow, narrow...  1.74 us
    pallas_call x1, Pallas kernels, local(): call(keys_kernel, (wide, wide), 'keys')  1.72 us
    ppermute x10, waiting for transfers between devices, send(): return lax.ppermute(x, axis, pairs)  1.52 us
    pallas_call x1, Pallas kernels, local(): call(state_kernel, payload, 'state', scratch=[whole, whole, pltpu.VMEM((n...  1.49 us
    pallas_call x1, Pallas kernels, local(): call(functools.partial(last_kernel, levels), (narrow, narrow), 'last', sc...  1.18 us
    pallas_call x1, Pallas kernels, local(): call(functools.partial(norm_kernel, levels, count), (narrow, wide, square...  0.84 us
  transfers between devices with their start and end apart: 10, of which 4 were waited for; matrix products, arithmetic and copies ran while one was open for 0% of the time, Pallas kernels for 24%

profile of v3, /device:TPU:0, one launch (start us, length us, event | category | flops | bytes accessed | tf_op | source)
XLA Modules:
  0.0 28.7 jit_solution(8951405950993246864)
XLA Ops:
  0.6 0.0 copy-start.3
  0.6 1.5 %state.1.order_ref.own_ref.refs_0_ = bf16[136,128]{1,0:T(8,128)(2,1)S(1)} custom-call(bf16[1024,128]{1,0:T(8,128)(2,1)} %bitcast.10, bf16[1024,128]{1,0:T(8,128)(2,1)} %bitcast.16, f32[8,128]{1,0:T(8,128)} %bitcast.29), custom_call_target="tpu_custom_call" | custom-call | bytes 1024 | tf_op jit(solution)/shard_map/state/pallas_call | solution.py:398
  2.1 0.0 copy-done.3
  2.2 0.5 %collective-permute-start.1 = (bf16[32,3072]{1,0:T(8,128)(2,1)S(1)}, bf16[32,3072]{1,0:T(8,128)(2,1)S(1)}, u32[]{:S(2)}, u32[]{:S(2)}) collective-permute-start(bf16[32,3072]{1,0:T(8,128)(2,1)S(1)} %cut.1), channel_id=1, source_target_pairs={{0,8},{8,0},{16,24},{24,16},{1,9},{9,1},{17,25},{25,17},{2,10},{10... | collective-permute-start | bytes 589832 | tf_op jit(solution)/shard_map/ppermute | solution.py:379
  2.7 2.6 %collective-permute-start = (bf16[136,128]{1,0:T(8,128)(2,1)S(1)}, bf16[136,128]{1,0:T(8,128)(2,1)S(1)}, u32[]{:S(2)}, u32[]{:S(2)}) collective-permute-start(bf16[136,128]{1,0:T(8,128)(2,1)S(1)} %state.1.order_ref.own_ref.refs_0_), channel_id=1, source_target_pairs={{0,1},{1,0},{2,3},{3,2},{4,5},{5,4},{6,7},{7,6},{8,9},{9,8},{10,11... | collective-permute-start | bytes 104456 | tf_op jit(solution)/shard_map/ppermute | solution.py:379
  5.3 0.0 collective-permute-done.1.came_ref
  5.3 0.0 copy-start.1
  5.3 0.0 copy-start.2
  5.3 0.0 copy-start.4
  5.3 0.1 add.1
  5.4 0.0 copy-start
  5.4 1.6 %collective-permute-start.5 = (bf16[32,1536]{1,0:T(8,128)(2,1)S(1)}, bf16[32,1536]{1,0:T(8,128)(2,1)S(1)}, u32[]{:S(2)}, u32[]{:S(2)}) collective-permute-start(bf16[32,1536]{1,0:T(8,128)(2,1)S(1)} %get-tuple-element.43), channel_id=1, source_target_pairs={{0,16},{8,24},{16,0},{24,8},{1,17},{9,25},{17,1},{25,9},{2,18},{10... | collective-permute-start | bytes 294920 | tf_op jit(solution)/shard_map/ppermute | solution.py:379
  7.0 0.3 %collective-permute-done.refs_0_.refs_2_ = bf16[136,128]{1,0:T(8,128)(2,1)S(1)} collective-permute-done((bf16[136,128]{1,0:T(8,128)(2,1)S(1)}, bf16[136,128]{1,0:T(8,128)(2,1)S(1)}, u32[]{:S(2)}, u32[]{:S(2)}) %collective-permute-start) | collective-permute-done | bytes 34848 | tf_op jit(solution)/shard_map/ppermute | solution.py:379
  7.3 0.0 copy-start.5
  7.3 2.1 %collective-permute-start.4 = (bf16[136,128]{1,0:T(8,128)(2,1)S(1)}, bf16[136,128]{1,0:T(8,128)(2,1)S(1)}, u32[]{:S(2)}, u32[]{:S(2)}) collective-permute-start(bf16[136,128]{1,0:T(8,128)(2,1)S(1)} %fold.1.order_ref.refs_1_), channel_id=1, source_target_pairs={{0,2},{1,3},{2,6},{3,7},{4,0},{5,1},{6,4},{7,5},{8,10},{9,11},{10,... | collective-permute-start | bytes 104456 | tf_op jit(solution)/shard_map/ppermute | solution.py:379
  9.4 2.5 %collective-permute-start.3 = (bf16[136,128]{1,0:T(8,128)(2,1)S(1)}, bf16[136,128]{1,0:T(8,128)(2,1)S(1)}, u32[]{:S(2)}, u32[]{:S(2)}) collective-permute-start(bf16[136,128]{1,0:T(8,128)(2,1)S(1)} %fold.1.order_ref.refs_1_), channel_id=1, source_target_pairs={{0,6},{1,7},{2,4},{3,5},{4,2},{5,3},{6,0},{7,1},{8,14},{9,15},{10,... | collective-permute-start | bytes 104456 | tf_op jit(solution)/shard_map/ppermute | solution.py:379
  11.9 1.6 %collective-permute-start.2 = (bf16[136,128]{1,0:T(8,128)(2,1)S(1)}, bf16[136,128]{1,0:T(8,128)(2,1)S(1)}, u32[]{:S(2)}, u32[]{:S(2)}) collective-permute-start(bf16[136,128]{1,0:T(8,128)(2,1)S(1)} %fold.1.order_ref.refs_1_), channel_id=1, source_target_pairs={{0,4},{1,5},{2,0},{3,1},{4,6},{5,7},{6,2},{7,3},{8,12},{9,13},{10,... | collective-permute-start | bytes 104456 | tf_op jit(solution)/shard_map/ppermute | solution.py:379
  13.4 0.0 copy-done.1
  13.4 0.0 copy-done.2
  13.4 0.0 copy-done.4
  13.4 0.0 copy-done
  13.5 0.0 copy-done.5
  13.5 2.2 %forward.1 = (f32[1024,128]{1,0:T(8,128)S(1)}, f32[128,128]{1,0:T(8,128)S(1)}, f32[24,128]{1,0:T(8,128)S(1)}, bf16[128,1024]{1,0:T(8,128)(2,1)S(1)}, f32[1024,12...) custom-call(bf16[1024,128]{1,0:T(8,128)(2,1)S(1)} %bitcast.21, ...), custom_call_target="tpu_custom_call" | custom-call | bytes 1024 | tf_op jit(solution)/shard_map/forward/pallas_call | solution.py:425
  15.6 0.3 %turned.1 = (bf16[1024,256]{1,0:T(8,128)(2,1)S(1)}, f32[1024,128]{1,0:T(8,128)S(1)}) custom-call(bf16[1024,128]{1,0:T(8,128)(2,1)S(1)} %bitcast.22, bf16[1024,128]{1,0:T(8,128)(2,1)S(1)} %bitcast.12, f32[128,128]{1,0:T(8,128)S(1)} %get-tuple-element.31.cols_ref, f32[24,128]{1,0:T(8,128)S(1)} %get-tuple-element.32.rows_ref, ...), custom_call_target="tpu_custom_call" | custom-call | bytes 1024 | tf_op jit(solution)/shard_map/turned/pallas_call | solution.py:428
  16.0 0.0 collective-permute-done.4.refs_5_
  16.0 0.0 collective-permute-done.3.refs_4_
  16.0 0.0 collective-permute-done.2.refs_3_
  16.0 0.8 %norm.1 = (bf16[1024,128]{1,0:T(8,128)(2,1)S(1)}, f32[1024,128]{1,0:T(8,128)S(1)}, f32[128,128]{1,0:T(8,128)S(1)}, bf16[128,128]{1,0:T(8,128)(2,1)S(1)}, f32[16,128]{1,0:T(8,128)S(1)}) custom-call(f32[1024,128]{1,0:T(8,128)S(1)} %get-tuple-element.35.local_ref, bf16[1024,128]{1,0:T(8,128)(2,1)S(1)} %bitcast.23, ...), custom_call_target="tpu_custom_call" | custom-call | bytes 1024 | tf_op jit(solution)/shard_map/norm/pallas_call | solution.py:431
  16.9 1.6 %collective-permute-start.6 = (bf16[128,128]{1,0:T(8,128)(2,1)S(1)}, bf16[128,128]{1,0:T(8,128)(2,1)S(1)}, u32[]{:S(2)}, u32[]{:S(2)}) collective-permute-start(bf16[128,128]{1,0:T(8,128)(2,1)S(1)} %get-tuple-element.41.order_ref.own_ref), channel_id=1, source_target_pairs={{0,1},{1,0},{2,3},{3,2},{4,5},{5,4},{6,7},{7,6},{8,9},{9,8},{10,11... | collective-permute-start | bytes 98312 | tf_op jit(solution)/shard_map/ppermute | solution.py:379
  18.4 0.0 collective-permute-done.5.refs_2_
  18.4 1.7 %queries.1 = (bf16[1024,128]{1,0:T(8,128)(2,1)}, bf16[1024,128]{1,0:T(8,128)(2,1)}, f32[32,1536]{1,0:T(8,128)}, f32[8,128]{1,0:T(8,128)S(1)}) custom-call(bf16[1024,128]{1,0:T(8,128)(2,1)S(1)} %bitcast.13, bf16[1024,128]{1,0:T(8,128)(2,1)S(1)} %bitcast.18, f32[128,128]{1,0:T(8,128)S(1)} %get-tuple-element.31.cols_ref, ...), custom_call_target="tpu_custom_call" | custom-call | bytes 1024 | tf_op jit(solution)/shard_map/queries/pallas_call | solution.py:437
  20.2 0.7 %collective-permute-done.6.refs_0_ = bf16[128,128]{1,0:T(8,128)(2,1)S(1)} collective-permute-done((bf16[128,128]{1,0:T(8,128)(2,1)S(1)}, bf16[128,128]{1,0:T(8,128)(2,1)S(1)}, u32[]{:S(2)}, u32[]{:S(2)}) %collective-permute-start.6) | collective-permute-done | bytes 32800 | tf_op jit(solution)/shard_map/ppermute | solution.py:379
  20.9 1.6 %collective-permute-start.9 = (bf16[128,128]{1,0:T(8,128)(2,1)S(1)}, bf16[128,128]{1,0:T(8,128)(2,1)S(1)}, u32[]{:S(2)}, u32[]{:S(2)}) collective-permute-start(bf16[128,128]{1,0:T(8,128)(2,1)S(1)} %fold_back.1.order_ref), channel_id=1, source_target_pairs={{0,6},{1,7},{2,4},{3,5},{4,2},{5,3},{6,0},{7,1},{8,14},{9,15},{10,... | collective-permute-start | bytes 98312 | tf_op jit(solution)/shard_map/ppermute | solution.py:379
  22.5 0.8 %collective-permute-start.8 = (bf16[128,128]{1,0:T(8,128)(2,1)S(1)}, bf16[128,128]{1,0:T(8,128)(2,1)S(1)}, u32[]{:S(2)}, u32[]{:S(2)}) collective-permute-start(bf16[128,128]{1,0:T(8,128)(2,1)S(1)} %fold_back.1.order_ref), channel_id=1, source_target_pairs={{0,4},{1,5},{2,6},{3,7},{4,0},{5,1},{6,2},{7,3},{8,12},{9,13},{10,... | collective-permute-start | bytes 98312 | tf_op jit(solution)/shard_map/ppermute | solution.py:379
  23.3 2.1 %collective-permute-start.7 = (bf16[128,128]{1,0:T(8,128)(2,1)S(1)}, bf16[128,128]{1,0:T(8,128)(2,1)S(1)}, u32[]{:S(2)}, u32[]{:S(2)}) collective-permute-start(bf16[128,128]{1,0:T(8,128)(2,1)S(1)} %fold_back.1.order_ref), channel_id=1, source_target_pairs={{0,2},{1,3},{2,0},{3,1},{4,6},{5,7},{6,4},{7,5},{8,10},{9,11},{10,... | collective-permute-start | bytes 98312 | tf_op jit(solution)/shard_map/ppermute | solution.py:379
  25.3 1.7 %keys.1 = (f32[1024,128]{1,0:T(8,128)S(1)}, f32[1024,128]{1,0:T(8,128)S(1)}) custom-call(bf16[1024,128]{1,0:T(8,128)(2,1)S(1)} %bitcast.24, bf16[1024,128]{1,0:T(8,128)(2,1)S(1)} %bitcast.14, bf16[1024,128]{1,0:T(8,128)(2,1)S(1)} %bitcast.19, bf16[128,1024]{1,0:T(8,128)(2,1)S(1)} %get-tuple-element.36.qt_ref, f32[128,128]{1,0:T(8,128)S(1)} %get-tuple-element.31.cols_ref, ...), custom_call_target="tpu_custom_call" | custom-call | bytes 1024 | tf_op jit(solution)/shard_map/keys/pallas_call | solution.py:454
  27.0 0.0 collective-permute-done.9.refs_3_
  27.0 0.4 %collective-permute-done.8.refs_2_ = bf16[128,128]{1,0:T(8,128)(2,1)S(1)} collective-permute-done((bf16[128,128]{1,0:T(8,128)(2,1)S(1)}, bf16[128,128]{1,0:T(8,128)(2,1)S(1)}, u32[]{:S(2)}, u32[]{:S(2)}) %collective-permute-start.8) | collective-permute-done | bytes 32800 | tf_op jit(solution)/shard_map/ppermute | solution.py:379
  27.4 0.1 collective-permute-done.7.refs_1_
  27.5 1.2 %last.1 = (bf16[1024,128]{1,0:T(8,128)(2,1)}, bf16[1024,128]{1,0:T(8,128)(2,1)}) custom-call(f32[1024,128]{1,0:T(8,128)S(1)} %get-tuple-element.49.dk_ref, f32[1024,128]{1,0:T(8,128)S(1)} %get-tuple-element.50.dv_ref, bf16[1024,128]{1,0:T(8,128)(2,1)S(1)} %bitcast.15, bf16[1024,128]{1,0:T(8,128)(2,1)S(1)} %bitcast.20, ...), custom_call_target="tpu_custom_call" | custom-call | bytes 1024 | tf_op jit(solution)/shard_map/last/pallas_call | solution.py:455
  (3 shorter events, 0.1 us)
Async XLA Ops:
  0.6 1.5 %copy-start.3 = (bf16[1,32,6144]{2,1,0:T(8,128)(2,1)S(1)}, bf16[1,32,6144]{2,1,0:T(8,128)(2,1)}, u32[]{:S(2)}) copy-start(bf16[1,32,6144]{2,1,0:T(8,128)(2,1)} %param.11) | copy-start | bytes 1179652
  2.2 3.1 %collective-permute-start.1 = (bf16[32,3072]{1,0:T(8,128)(2,1)S(1)}, bf16[32,3072]{1,0:T(8,128)(2,1)S(1)}, u32[]{:S(2)}, u32[]{:S(2)}) collective-permute-start(bf16[32,3072]{1,0:T(8,128)(2,1)S(1)} %cut.1), channel_id=1, source_target_pairs={{0,8},{8,0},{16,24},{24,16},{1,9},{9,1},{17,25},{25,17},{2,10},{10... | collective-permute-start | bytes 589832 | tf_op jit(solution)/shard_map/ppermute | solution.py:379
  2.7 4.6 %collective-permute-start = (bf16[136,128]{1,0:T(8,128)(2,1)S(1)}, bf16[136,128]{1,0:T(8,128)(2,1)S(1)}, u32[]{:S(2)}, u32[]{:S(2)}) collective-permute-start(bf16[136,128]{1,0:T(8,128)(2,1)S(1)} %state.1.order_ref.own_ref.refs_0_), channel_id=1, source_target_pairs={{0,1},{1,0},{2,3},{3,2},{4,5},{5,4},{6,7},{7,6},{8,9},{9,8},{10,11... | collective-permute-start | bytes 104456 | tf_op jit(solution)/shard_map/ppermute | solution.py:379
  5.3 8.2 %copy-start.1 = (bf16[1,1024,128]{2,1,0:T(8,128)(2,1)S(1)}, bf16[1,1024,128]{2,1,0:T(8,128)(2,1)}, u32[]{:S(2)}) copy-start(bf16[1,1024,128]{2,1,0:T(8,128)(2,1)} %param.8) | copy-start | bytes 786436
  5.3 8.2 %copy-start.2 = (bf16[1,1024,128]{2,1,0:T(8,128)(2,1)S(1)}, bf16[1,1024,128]{2,1,0:T(8,128)(2,1)}, u32[]{:S(2)}) copy-start(bf16[1,1024,128]{2,1,0:T(8,128)(2,1)} %param.6) | copy-start | bytes 786436
  5.3 8.2 %copy-start.4 = (bf16[1,1024,128]{2,1,0:T(8,128)(2,1)S(1)}, bf16[1,1024,128]{2,1,0:T(8,128)(2,1)}, u32[]{:S(2)}) copy-start(bf16[1,1024,128]{2,1,0:T(8,128)(2,1)} %param.9) | copy-start | bytes 786436
  5.4 8.1 %copy-start = (bf16[1,1024,128]{2,1,0:T(8,128)(2,1)S(1)}, bf16[1,1024,128]{2,1,0:T(8,128)(2,1)}, u32[]{:S(2)}) copy-start(bf16[1,1024,128]{2,1,0:T(8,128)(2,1)} %param.7) | copy-start | bytes 786436
  5.4 13.0 %collective-permute-start.5 = (bf16[32,1536]{1,0:T(8,128)(2,1)S(1)}, bf16[32,1536]{1,0:T(8,128)(2,1)S(1)}, u32[]{:S(2)}, u32[]{:S(2)}) collective-permute-start(bf16[32,1536]{1,0:T(8,128)(2,1)S(1)} %get-tuple-element.43), channel_id=1, source_target_pairs={{0,16},{8,24},{16,0},{24,8},{1,17},{9,25},{17,1},{25,9},{2,18},{10... | collective-permute-start | bytes 294920 | tf_op jit(solution)/shard_map/ppermute | solution.py:379
  7.3 6.2 %copy-start.5 = (f32[1,1,1024]{2,1,0:T(1,128)S(1)}, f32[1,1,1024]{2,1,0:T(1,128)}, u32[]{:S(2)}) copy-start(f32[1,1,1024]{2,1,0:T(1,128)} %param.10) | copy-start | bytes 12292
  7.3 8.6 %collective-permute-start.4 = (bf16[136,128]{1,0:T(8,128)(2,1)S(1)}, bf16[136,128]{1,0:T(8,128)(2,1)S(1)}, u32[]{:S(2)}, u32[]{:S(2)}) collective-permute-start(bf16[136,128]{1,0:T(8,128)(2,1)S(1)} %fold.1.order_ref.refs_1_), channel_id=1, source_target_pairs={{0,2},{1,3},{2,6},{3,7},{4,0},{5,1},{6,4},{7,5},{8,10},{9,11},{10,... | collective-permute-start | bytes 104456 | tf_op jit(solution)/shard_map/ppermute | solution.py:379
  9.4 6.6 %collective-permute-start.3 = (bf16[136,128]{1,0:T(8,128)(2,1)S(1)}, bf16[136,128]{1,0:T(8,128)(2,1)S(1)}, u32[]{:S(2)}, u32[]{:S(2)}) collective-permute-start(bf16[136,128]{1,0:T(8,128)(2,1)S(1)} %fold.1.order_ref.refs_1_), channel_id=1, source_target_pairs={{0,6},{1,7},{2,4},{3,5},{4,2},{5,3},{6,0},{7,1},{8,14},{9,15},{10,... | collective-permute-start | bytes 104456 | tf_op jit(solution)/shard_map/ppermute | solution.py:379
  11.9 4.1 %collective-permute-start.2 = (bf16[136,128]{1,0:T(8,128)(2,1)S(1)}, bf16[136,128]{1,0:T(8,128)(2,1)S(1)}, u32[]{:S(2)}, u32[]{:S(2)}) collective-permute-start(bf16[136,128]{1,0:T(8,128)(2,1)S(1)} %fold.1.order_ref.refs_1_), channel_id=1, source_target_pairs={{0,4},{1,5},{2,0},{3,1},{4,6},{5,7},{6,2},{7,3},{8,12},{9,13},{10,... | collective-permute-start | bytes 104456 | tf_op jit(solution)/shard_map/ppermute | solution.py:379
  16.9 4.0 %collective-permute-start.6 = (bf16[128,128]{1,0:T(8,128)(2,1)S(1)}, bf16[128,128]{1,0:T(8,128)(2,1)S(1)}, u32[]{:S(2)}, u32[]{:S(2)}) collective-permute-start(bf16[128,128]{1,0:T(8,128)(2,1)S(1)} %get-tuple-element.41.order_ref.own_ref), channel_id=1, source_target_pairs={{0,1},{1,0},{2,3},{3,2},{4,5},{5,4},{6,7},{7,6},{8,9},{9,8},{10,11... | collective-permute-start | bytes 98312 | tf_op jit(solution)/shard_map/ppermute | solution.py:379
  20.9 6.2 %collective-permute-start.9 = (bf16[128,128]{1,0:T(8,128)(2,1)S(1)}, bf16[128,128]{1,0:T(8,128)(2,1)S(1)}, u32[]{:S(2)}, u32[]{:S(2)}) collective-permute-start(bf16[128,128]{1,0:T(8,128)(2,1)S(1)} %fold_back.1.order_ref), channel_id=1, source_target_pairs={{0,6},{1,7},{2,4},{3,5},{4,2},{5,3},{6,0},{7,1},{8,14},{9,15},{10,... | collective-permute-start | bytes 98312 | tf_op jit(solution)/shard_map/ppermute | solution.py:379
  22.5 4.9 %collective-permute-start.8 = (bf16[128,128]{1,0:T(8,128)(2,1)S(1)}, bf16[128,128]{1,0:T(8,128)(2,1)S(1)}, u32[]{:S(2)}, u32[]{:S(2)}) collective-permute-start(bf16[128,128]{1,0:T(8,128)(2,1)S(1)} %fold_back.1.order_ref), channel_id=1, source_target_pairs={{0,4},{1,5},{2,6},{3,7},{4,0},{5,1},{6,2},{7,3},{8,12},{9,13},{10,... | collective-permute-start | bytes 98312 | tf_op jit(solution)/shard_map/ppermute | solution.py:379
  23.3 4.3 %collective-permute-start.7 = (bf16[128,128]{1,0:T(8,128)(2,1)S(1)}, bf16[128,128]{1,0:T(8,128)(2,1)S(1)}, u32[]{:S(2)}, u32[]{:S(2)}) collective-permute-start(bf16[128,128]{1,0:T(8,128)(2,1)S(1)} %fold_back.1.order_ref), channel_id=1, source_target_pairs={{0,2},{1,3},{2,0},{3,1},{4,6},{5,7},{6,4},{7,5},{8,10},{9,11},{10,... | collective-permute-start | bytes 98312 | tf_op jit(solution)/shard_map/ppermute | solution.py:379

commit v4 on v3

--- a/solution.py
+++ b/solution.py
@@ -11,7 +11,8 @@
 C = 128
 F32 = jnp.float32
 BF16 = jnp.bfloat16
-FORWARD_OF_4 = ((2, 0, 3, 1), (3, 2, 1, 0), (1, 3, 0, 2))
+FORWARD_OF_4 = ((3, 0, 1, 2), (2, 3, 0, 1), (1, 2, 3, 0))
+LAST_BACKWARD_OF_4 = ((1, 0, 3, 2), (2, 3, 0, 1), (2, 3, 1, 0))
 LOGS = 8
 
 
@@ -104,7 +105,7 @@
     state = jnp.zeros((C, C), F32)
     for r, weight in enumerate(weights):
         kw = flipped(chunk(k_ref, r)) * weight
-        state = state + mm(parts(kw, 1), twice(chunk(v_ref, r), 0))
+        state = state + mm(kw.astype(BF16), chunk(v_ref, r))
     out_ref[:C, :] = state.astype(BF16)
     out_ref[C:, :] = log_rows(sum(tot))
 
@@ -117,9 +118,9 @@
 
 
 def places(stride, radix, rounds):
-    mine = lax.rem(lax.div(lax.axis_index("seq"), stride), radix)
-    senders = [sum(jnp.where(mine == to, at, 0) for at, to in enumerate(targets)) for targets in rounds]
-    return [mine, *senders]
+    block = lax.rem(lax.axis_index("seq"), stride * radix)
+    senders = [sum(jnp.where(block == to, at // stride, 0) for at, to in enumerate(targets)) for targets in rounds]
+    return [lax.div(block, stride), *senders]
 
 
 def fold_kernel(stride, radix, rounds, own_ref, *refs):
@@ -135,8 +136,15 @@
     out_ref[C:, :] = log_rows(sum(logs))
 
 
+def spread(decay_row):
+    row = lax.broadcasted_iota(jnp.int32, (C, C), 0)
+    col = lax.broadcasted_iota(jnp.int32, (C, C), 1)
+    pieces = jnp.concatenate([jnp.where(row >= col, x, 0.0) for x in cut3(decay_row)], axis=1).astype(BF16)
+    return mm(pieces, jnp.ones((3 * C, C), BF16))
+
+
 def forward_kernel(
-    q_ref, k_ref, v_ref, decay_ref, order_ref, dy_ref, out_ref, cols_ref, rows_ref, qt_ref, starts_ref, lower_ref, *wide_refs
+    q_ref, k_ref, v_ref, decay_ref, order_ref, dy_ref, out_ref, downs_ref, rows_ref, qt_ref, starts_ref, lower_ref, lead_ref
 ):
     upto, after = sums(decay_ref[...])
     tot = totals(upto)
@@ -144,31 +152,22 @@
     n = len(tot)
     row = lax.broadcasted_iota(jnp.int32, (C, C), 0)
     col = lax.broadcasted_iota(jnp.int32, (C, C), 1)
-    rows = [upto]
-    rows.append(jnp.concatenate([jnp.exp(upto[r : r + 1] + begin[r]) for r in range(n)], axis=0))
-    rows.append(jnp.concatenate([jnp.exp(after[r : r + 1] + later[r]) for r in range(n)], axis=0))
-    rows.append(jnp.exp(upto))
-    rows.append(jnp.exp(after))
-    used = sum(x.shape[0] for x in rows)
-    rows.append(jnp.zeros((C - used, C), F32))
-    cols = jnp.concatenate(rows, axis=0).T
-    cols_ref[...] = cols
     rows_ref[:n, :] = upto
-    rows_ref[n : 2 * n, :] = jnp.concatenate([jnp.exp(x) for x in tot], axis=0)
-    rows_ref[2 * n :, :] = jnp.concatenate([jnp.exp(x) for x in begin], axis=0)
+    for i, rows in enumerate(([jnp.exp(x) for x in tot], [jnp.exp(x) for x in begin], tot, later), 1):
+        rows_ref[i * n : (i + 1) * n, :] = jnp.concatenate(rows, axis=0)
     state = jnp.zeros((C, C), F32)
     for r in range(n):
         q, k, v = chunk(q_ref, r), chunk(k_ref, r), chunk(v_ref, r)
-        decay = jnp.exp(jnp.minimum(cols[:, r : r + 1] - upto[r : r + 1], 0.0))
-        lower = jnp.where(row >= col, decay, 0.0)
+        down = spread(decay_ref[r : r + 1, :])
+        downs_ref[r * C : (r + 1) * C, :] = down
+        lead_ref[r * C : (r + 1) * C, :] = jnp.exp(down + begin[r])
+        lower = jnp.where(row >= col, jnp.exp(jnp.minimum(down - upto[r : r + 1], 0.0)), 0.0)
         lower_ref[r * C : (r + 1) * C, :] = lower
         scores = mm_nt(q, k) * lower
         out = mm(parts(scores, 1), twice(v, 0))
         if r > 0:
-            out = out + cols[:, 3 * n + r : 3 * n + r + 1] * mm(twice(q, 1), parts(state, 0))
+            out = out + jnp.exp(down) * mm(twice(q, 1), parts(state, 0))
         out_ref[r * C : (r + 1) * C, :] = out
-        for i, ref in enumerate(wide_refs, 1):
-            ref[r * C : (r + 1) * C, :] = jnp.broadcast_to(cols[:, i * n + r : i * n + r + 1], (C, C))
         qt_ref[:, r * C : (r + 1) * C] = flipped(q).astype(BF16)
         starts_ref[r * C : (r + 1) * C, :] = state
         if r < n - 1:
@@ -176,28 +175,45 @@
             state = jnp.exp(tot[r]) * state + mm(parts(kw, 1), twice(v, 0))
 
 
-def turned_kernel(q_ref, k_ref, cols_ref, rows_ref, order_ref, scores_ref, upper_ref):
-    n = rows_ref.shape[0] // 3
+def turned_kernel(q_ref, k_ref, downs_ref, rows_ref, order_ref, scores_ref, upper_ref):
+    n = rows_ref.shape[0] // 5
     row = lax.broadcasted_iota(jnp.int32, (C, C), 0)
     col = lax.broadcasted_iota(jnp.int32, (C, C), 1)
-    cols = cols_ref[...]
     for r in range(n):
-        decay = jnp.exp(jnp.minimum(rows_ref[r : r + 1, :] - cols[:, r : r + 1], 0.0))
+        decay = jnp.exp(jnp.minimum(rows_ref[r : r + 1, :] - chunk(downs_ref, r), 0.0))
         upper = jnp.where(row <= col, decay, 0.0)
         upper_ref[r * C : (r + 1) * C, :] = upper
         scores_ref[r * C : (r + 1) * C, :] = parts(mm_nt(chunk(k_ref, r), chunk(q_ref, r)) * upper, 1)
 
 
-def norm_kernel(levels, count, local_ref, q_ref, qt_ref, dy_ref, lead_ref, *refs):
-    received, (attn_ref, dattn_ref, incoming_ref, state_ref, weights_ref) = refs[:-5], refs[-5:]
+def back_weights(levels, count, payloads):
+    own, others = payloads[: len(levels)], payloads[len(levels) :]
+    behind = jnp.zeros((1, C), F32)
+    weights = []
+    at = 0
+    for (stride, radix, rounds, back_rounds), own_ref in zip(levels, own, strict=True):
+        positions, senders = places(stride, radix, rounds), places(stride, radix, back_rounds)
+        mine = positions[0]
+        logs = [read_log(ref) for ref in (own_ref, *others[at : at + radix - 1])]
+        at += radix - 1
+        for position in senders[1:]:
+            weight = jnp.exp(behind + between(logs, positions, mine, position))
+            weights.append(jnp.where(position > mine, weight, 0.0))
+        for position in senders:
+            weights.append(jnp.exp(between(logs, positions, -1, position)))
+        behind = behind + between(logs, positions, mine, radix)
+    weights.append(jnp.zeros((count - len(weights), C), F32))
+    return jnp.concatenate(weights, axis=0)
+
+
+def norm_kernel(levels, local_ref, q_ref, qt_ref, dy_ref, lead_ref, *refs):
+    received, (attn_ref, dattn_ref, incoming_ref, state_ref) = refs[:-4], refs[-4:]
     n = local_ref.shape[0] // C
     own, others = received[: len(levels)], received[len(levels) :]
     incoming = jnp.zeros((C, C), F32)
     ahead = jnp.zeros((1, C), F32)
-    behind = jnp.zeros((1, C), F32)
-    weights = []
     at = 0
-    for (stride, radix, rounds, back_rounds), own_ref in zip(levels, own, strict=True):
+    for (stride, radix, rounds, _), own_ref in zip(levels, own, strict=True):
         positions = places(stride, radix, rounds)
         mine = positions[0]
         level = [own_ref, *others[at : at + radix - 1]]
@@ -206,31 +222,20 @@
         for ref, position in zip(level[1:], positions[1:], strict=True):
             weight = jnp.where(position < mine, jnp.exp(ahead + between(logs, positions, position, mine)), 0.0)
             incoming = incoming + weight * ref[:C, :].astype(F32)
-        senders = places(stride, radix, back_rounds)
-        for position in senders[1:]:
-            weights.append(
-                jnp.where(position > mine, jnp.exp(behind + between(logs, positions, mine, position)), 0.0)
-            )
-        for position in senders:
-            weights.append(jnp.exp(between(logs, positions, -1, position)))
         ahead = ahead + between(logs, positions, -1, mine)
-        behind = behind + between(logs, positions, mine, radix)
-    weights.append(jnp.zeros((count - len(weights), C), F32))
-    weights_ref[...] = jnp.concatenate(weights, axis=0)
     incoming_ref[...] = incoming
-    incoming = parts(incoming, 0)
+    incoming = incoming.astype(BF16)
     state = jnp.zeros((C, C), F32)
     for r in range(n):
         lead = chunk(lead_ref, r)
-        attention = chunk(local_ref, r) + lead * mm(twice(chunk(q_ref, r), 1), incoming)
+        attention = chunk(local_ref, r) + lead * mm(chunk(q_ref, r), incoming)
         dy = chunk(dy_ref, r).astype(F32)
         ratio = lax.rsqrt(jnp.mean(attention * attention, axis=1, keepdims=True) + NORM_EPS)
         along = jnp.sum(dy * attention, axis=1, keepdims=True)
         attn_ref[r * C : (r + 1) * C, :] = (attention * ratio).astype(BF16)
         dattn = ratio * dy - (ratio * ratio * ratio / C * along) * attention
         dattn_ref[r * C : (r + 1) * C, :] = dattn
-        both = mm(qt_ref[:, r * C : (r + 1) * C], parts(lead * dattn, 1))
-        state = state + both[:, :C] + both[:, C:]
+        state = state + mm(qt_ref[:, r * C : (r + 1) * C], (lead * dattn).astype(BF16))
     state_ref[...] = state.astype(BF16)
 
 
@@ -243,10 +248,11 @@
 
 
 def queries_kernel(
-    columns, stride, k_ref, v_ref, cols_ref, rows_ref, starts_ref, lower_ref, dattn_ref, incoming_ref, order_ref, *refs
+    levels, count, columns, stride, k_ref, v_ref, downs_ref, rows_ref, starts_ref, lower_ref, dattn_ref, incoming_ref, order_ref, *refs
 ):
-    attn_ref, have_ref, came_ref, attn_hbm, dq_hbm, total_hbm, done_ref, dq_ref, total_ref, sems = refs
-    n = rows_ref.shape[0] // 3
+    attn_ref, have_ref, came_ref, *payloads = refs[:-7]
+    attn_hbm, dq_hbm, total_hbm, weights_ref, dq_ref, total_ref, sems = refs[-7:]
+    n = rows_ref.shape[0] // 5
     copies = [
         pltpu.make_async_copy(source, target, sems.at[i])
         for i, (source, target) in enumerate(((attn_ref, attn_hbm), (total_ref, total_hbm), (dq_ref, dq_hbm)))
@@ -254,43 +260,44 @@
     copies[0].start()
     total_ref[...] = half(have_ref, columns, bit(stride), 0).astype(F32) + came_ref[...].astype(F32)
     copies[1].start()
-    cols = cols_ref[...]
     incoming = incoming_ref[...]
     for r in range(n):
         pair = parts(chunk(dattn_ref, r), 1)
         dscores = mm_nt(pair, twice(chunk(v_ref, r), 1)) * chunk(lower_ref, r)
         start = chunk(starts_ref, r) + rows_ref[2 * n + r : 2 * n + r + 1, :] * incoming
         dq = mm(parts(dscores, 1), twice(chunk(k_ref, r), 0))
-        dq = dq + cols[:, 3 * n + r : 3 * n + r + 1] * mm_nt(pair, twice(start.astype(BF16), 1))
+        dq = dq + jnp.exp(chunk(downs_ref, r)) * mm_nt(pair, twice(start.astype(BF16), 1))
         dq_ref[r * C : (r + 1) * C, :] = dq.astype(BF16)
     copies[2].start()
-    done_ref[...] = rows_ref[:n, :]
+    weights_ref[...] = back_weights(levels, count, payloads)
     for copy in copies:
         copy.wait()
 
 
 def keys_kernel(
-    q_ref, k_ref, v_ref, qt_ref, cols_ref, rows_ref, scores_ref, upper_ref, dattn_ref, order_ref, dk_ref, dv_ref
+    q_ref, k_ref, v_ref, qt_ref, downs_ref, rows_ref, scores_ref, upper_ref, dattn_ref, order_ref, dk_ref, dv_ref, tail_ref
 ):
-    n = rows_ref.shape[0] // 3
-    cols = cols_ref[...]
+    n = rows_ref.shape[0] // 5
     future = jnp.zeros((C, C), F32)
     for r in reversed(range(n)):
         k, v = chunk(k_ref, r), chunk(v_ref, r)
         dattn = chunk(dattn_ref, r)
         pair = parts(dattn, 1)
-        lead, tail = cols[:, 3 * n + r : 3 * n + r + 1], cols[:, 4 * n + r : 4 * n + r + 1]
+        down = chunk(downs_ref, r)
+        left = jnp.minimum(rows_ref[3 * n + r : 3 * n + r + 1, :] - down, 0.0)
+        tail_ref[r * C : (r + 1) * C, :] = jnp.exp(left + rows_ref[4 * n + r : 4 * n + r + 1, :])
         dscores_t = mm_nt(twice(v, 1), pair) * chunk(upper_ref, r)
         scores = chunk(scores_ref, r)
         dk = mm(parts(dscores_t, 1), twice(chunk(q_ref, r), 0))
         dv = mm(scores, twice(pair[:, :C], 0)) + mm(scores[:, :C], pair[:, C:])
         if r < n - 1:
+            tail = jnp.exp(left)
             dk = dk + tail * mm_nt(twice(v, 1), parts(future, 1))
             dv = dv + tail * mm(twice(k, 1), parts(future, 0))
         dk_ref[r * C : (r + 1) * C, :] = dk
         dv_ref[r * C : (r + 1) * C, :] = dv
         if r > 0:
-            both = mm(qt_ref[:, r * C : (r + 1) * C], parts(lead * dattn, 1))
+            both = mm(qt_ref[:, r * C : (r + 1) * C], parts(jnp.exp(down) * dattn, 1))
             future = rows_ref[n + r : n + r + 1, :] * future + both[:, :C] + both[:, C:]
 
 
@@ -304,13 +311,13 @@
             future = future + weights_ref[at + d : at + d + 1, :] * received[taken + d][...].astype(F32)
         at += 2 * radix - 1
         taken += radix - 1
-    wide, tall = parts(future, 1), parts(future, 0)
+    future = future.astype(BF16)
     copies = []
     for r in range(n):
         tail = chunk(tail_ref, r)
-        dk = chunk(dk_ref, r) + tail * mm_nt(twice(chunk(v_ref, r), 1), wide)
+        dk = chunk(dk_ref, r) + tail * mm_nt(chunk(v_ref, r), future)
         out_k_ref[r * C : (r + 1) * C, :] = dk.astype(BF16)
-        dv = chunk(dv_ref, r) + tail * mm(twice(chunk(k_ref, r), 1), tall)
+        dv = chunk(dv_ref, r) + tail * mm(chunk(k_ref, r), future)
         out_v_ref[r * C : (r + 1) * C, :] = dv.astype(BF16)
         if (r + 1) % (n // 2) == 0:
             rows = pl.ds((r + 1 - n // 2) * C, n // 2 * C)
@@ -359,23 +366,26 @@
     )
 
 
-def exchanges(radix):
-    return tuple(tuple(at ^ d for at in range(radix)) for d in range(1, radix))
+def rounds_of(stride, places_to):
+    return tuple(
+        tuple(targets[at // stride] * stride + at % stride for at in range(stride * len(targets))) for targets in places_to
+    )
 
 
 def scan_levels(size):
     levels, stride = [], 1
     while stride < size:
         radix = 2 if stride == 1 else min(4, size // stride)
-        pairs = exchanges(radix)
-        levels.append((stride, radix, FORWARD_OF_4 if radix == 4 else pairs, pairs))
+        pairs = tuple(tuple(at ^ d for at in range(radix)) for d in range(1, radix))
+        forward = rounds_of(stride, FORWARD_OF_4 if radix == 4 else pairs)
+        backward = rounds_of(stride, LAST_BACKWARD_OF_4 if radix == 4 and 4 * stride == size else pairs)
+        levels.append((stride, radix, forward, backward))
         stride *= radix
     return levels
 
 
-def send(x, axis, size, stride, targets):
-    radix = len(targets)
-    pairs = [(i, i + (targets[i // stride % radix] - i // stride % radix) * stride) for i in range(size)]
+def send(x, axis, size, targets):
+    pairs = [(i, i - i % len(targets) + targets[i % len(targets)]) for i in range(size)]
     return lax.ppermute(x, axis, pairs)
 
 
@@ -408,50 +418,48 @@
     columns = grads.shape[1] // dp
     others = []
     for i, (stride, radix, rounds, _) in enumerate(levels):
-        got = [send(own[-1], "seq", seq, stride, targets) for targets in rounds]
+        got = [send(own[-1], "seq", seq, targets) for targets in rounds]
         others += got
         if i == 0:
             sent = call(functools.partial(cut_kernel, columns), shape((lines, grads.shape[1] // 2), BF16), "cut")(grads, own[0])
-            came = send(sent, "dp", dp, 1, (1, 0))
+            came = send(sent, "dp", dp, (1, 0))
             total, part = grads, 1
             while 2 * part < dp:
                 kept, sent = shape((lines, total.shape[1] // 2), F32), shape((lines, total.shape[1] // 4), BF16)
                 total, sent = call(functools.partial(add_kernel, columns, part), (kept, sent), "add")(total, came)
                 part *= 2
-                came = send(sent, "dp", dp, part, (1, 0))
+                came = send(sent, "dp", dp, rounds_of(part, ((1, 0),))[0])
         if i < len(levels) - 1:
             fold = functools.partial(fold_kernel, stride, radix, rounds)
             own.append(call(fold, payload, "fold")(own[-1], *got, *([total] if i == 0 else [])))
-    local_out, cols, rows, qt, starts, lower, lead, tail = call(
-        forward_kernel, (wide, square, shape((3 * n, C), F32), shape((C, tokens), BF16), wide, wide, wide, wide), "forward"
+    local_out, downs, rows, qt, starts, lower, lead = call(
+        forward_kernel, (wide, wide, shape((5 * n, C), F32), shape((C, tokens), BF16), wide, wide, wide), "forward"
     )(q, k, v, decay, own[-1], dy)
-    scores_t, upper = call(turned_kernel, (shape((tokens, 2 * C), BF16), wide), "turned")(q, k, cols, rows, own[-1])
+    scores_t, upper = call(turned_kernel, (shape((tokens, 2 * C), BF16), wide), "turned")(q, k, downs, rows, own[-1])
     count = sum(2 * radix - 1 for _, radix, _, _ in levels)
     count += -count % 8
-    attention, dattn, incoming, state, weights = call(
-        functools.partial(norm_kernel, levels, count),
-        (narrow, wide, square, shape((C, C), BF16), shape((count, C), F32)),
-        "norm",
+    attention, dattn, incoming, state = call(
+        functools.partial(norm_kernel, levels), (narrow, wide, square, shape((C, C), BF16)), "norm"
     )(local_out, q, qt, dy, lead, *own, *others, scores_t)
 
-    attn_out, grad_query, grad_shard, done = call(
-        functools.partial(queries_kernel, columns, dp // 2),
-        (narrow, narrow, shape((lines, columns), F32), shape((n, C), F32)),
+    attn_out, grad_query, grad_shard, weights = call(
+        functools.partial(queries_kernel, levels, count, columns, dp // 2),
+        (narrow, narrow, shape((lines, columns), F32), shape((count, C), F32)),
         "queries",
         scratch=[whole, pltpu.VMEM((lines, columns), F32), dma((3,))],
-        in_specs=[here] * 12,
+        in_specs=[here] * (12 + len(own) + len(others)),
         out_specs=(away, away, away, here),
-    )(k, v, cols, rows, starts, lower, dattn, incoming, state, attention, total, came)
+    )(k, v, downs, rows, starts, lower, dattn, incoming, state, attention, total, came, *own, *others)
     received = []
     at = 0
     for i, (stride, radix, _, rounds) in enumerate(levels):
-        got = [send(state, "seq", seq, stride, targets) for targets in rounds]
+        got = [send(state, "seq", seq, targets) for targets in rounds]
         received += got
         if i < len(levels) - 1:
             fold = functools.partial(fold_back_kernel, at + radix - 1, radix)
-            state = call(fold, shape((C, C), BF16), "fold_back")(state, *got, weights, done)
+            state = call(fold, shape((C, C), BF16), "fold_back")(state, *got, weights)
         at += 2 * radix - 1
-    dk, dv = call(keys_kernel, (wide, wide), "keys")(q, k, v, qt, cols, rows, scores_t, upper, dattn, state)
+    dk, dv, tail = call(keys_kernel, (wide, wide, wide), "keys")(q, k, v, qt, downs, rows, scores_t, upper, dattn, state)
     grad_key, grad_value = call(
         functools.partial(last_kernel, levels),
         (narrow, narrow),

time: 28.9 us -> 28.3 us (0.979)
  Pallas kernels: 9.62 us -> 8.9 us
  waiting for transfers between devices: 1.52 us -> 1.82 us
    pallas_call x5, Pallas kernels: 6.49 us -> 5.89 us  [the longest x1 1.74 us: local(): call(functools.partial(queries_kernel, levels, count, columns, dp // 2),...]
    ppermute x10, waiting for transfers between devices: 1.52 us -> 1.82 us  [send(): return lax.ppermute(x, axis, pairs)]
  transfers between devices with their start and end apart: 10 -> 10, of which waited for: 4 -> 4; matrix products, arithmetic and copies ran while one was open for 0% -> 0% of each run, Pallas kernels for 24% -> 22%
where the time goes in v4:
time: 28.3 us; the launch traced here: 28.2 us
  starting transfers between devices  16.6 us (59%)
  Pallas kernels  8.9 us (31%)
  waiting for transfers between devices  1.82 us (6%)
  between operations  0.78 us (3%)
    ppermute x10, starting transfers between devices, send(): return lax.ppermute(x, axis, pairs)  16.6 us
    ppermute x10, waiting for transfers between devices, send(): return lax.ppermute(x, axis, pairs)  1.82 us
    pallas_call x1, Pallas kernels, local(): call(functools.partial(queries_kernel, levels, count, columns, dp // 2),...  1.74 us
    pallas_call x1, Pallas kernels, local(): call(keys_kernel, (wide, wide, wide), 'keys')  1.71 us
    pallas_call x1, Pallas kernels, local(): call(forward_kernel, (wide, wide, shape((5 * n, C), F32), shape((C, token...  1.7 us
    pallas_call x1, Pallas kernels, local(): call(state_kernel, payload, 'state', scratch=[whole, whole, pltpu.VMEM((n...  1.43 us
    pallas_call x1, Pallas kernels, local(): call(functools.partial(last_kernel, levels), (narrow, narrow), 'last', sc...  1.12 us
    pallas_call x1, Pallas kernels, local(): call(functools.partial(norm_kernel, levels), (narrow, wide, square, shape...  0.72 us
  transfers between devices with their start and end apart: 10, of which 4 were waited for; matrix products, arithmetic and copies ran while one was open for 0% of the time, Pallas kernels for 22%

profile of v4, /device:TPU:0, one launch (start us, length us, event | category | flops | bytes accessed | tf_op | source)
XLA Modules:
  0.0 28.2 jit_solution(8102381415756460334)
XLA Ops:
  0.6 0.0 copy-start.3
  0.6 1.4 %state.1.order_ref.own_ref.refs_0_.refs_3_ = bf16[136,128]{1,0:T(8,128)(2,1)S(1)} custom-call(bf16[1024,128]{1,0:T(8,128)(2,1)} %bitcast.10, bf16[1024,128]{1,0:T(8,128)(2,1)} %bitcast.16, f32[8,128]{1,0:T(8,128)} %bitcast.29), custom_call_target="tpu_custom_call" | custom-call | bytes 1024 | tf_op jit(solution)/shard_map/state/pallas_call | solution.py:408
  2.1 0.0 copy-done.3
  2.1 0.5 %collective-permute-start.1 = (bf16[32,3072]{1,0:T(8,128)(2,1)S(1)}, bf16[32,3072]{1,0:T(8,128)(2,1)S(1)}, u32[]{:S(2)}, u32[]{:S(2)}) collective-permute-start(bf16[32,3072]{1,0:T(8,128)(2,1)S(1)} %cut.1), channel_id=1, source_target_pairs={{0,8},{8,0},{16,24},{24,16},{1,9},{9,1},{17,25},{25,17},{2,10},{10... | collective-permute-start | bytes 589832 | tf_op jit(solution)/shard_map/ppermute | solution.py:389
  2.6 2.6 %collective-permute-start = (bf16[136,128]{1,0:T(8,128)(2,1)S(1)}, bf16[136,128]{1,0:T(8,128)(2,1)S(1)}, u32[]{:S(2)}, u32[]{:S(2)}) collective-permute-start(bf16[136,128]{1,0:T(8,128)(2,1)S(1)} %state.1.order_ref.own_ref.refs_0_.refs_3_), channel_id=1, source_target_pairs={{0,1},{1,0},{2,3},{3,2},{4,5},{5,4},{6,7},{7,6},{8,9},{9,8},{10,11... | collective-permute-start | bytes 104456 | tf_op jit(solution)/shard_map/ppermute | solution.py:389
  5.2 0.0 collective-permute-done.1.came_ref
  5.2 0.0 copy-start.1
  5.2 0.0 copy-start.2
  5.2 0.0 copy-start.4
  5.2 0.1 add.1
  5.3 0.0 copy-start
  5.3 1.6 %collective-permute-start.5 = (bf16[32,1536]{1,0:T(8,128)(2,1)S(1)}, bf16[32,1536]{1,0:T(8,128)(2,1)S(1)}, u32[]{:S(2)}, u32[]{:S(2)}) collective-permute-start(bf16[32,1536]{1,0:T(8,128)(2,1)S(1)} %get-tuple-element.42), channel_id=1, source_target_pairs={{0,16},{8,24},{16,0},{24,8},{1,17},{9,25},{17,1},{25,9},{2,18},{10... | collective-permute-start | bytes 294920 | tf_op jit(solution)/shard_map/ppermute | solution.py:389
  6.9 0.3 %collective-permute-done.refs_0_.refs_2_.refs_5_ = bf16[136,128]{1,0:T(8,128)(2,1)S(1)} collective-permute-done((bf16[136,128]{1,0:T(8,128)(2,1)S(1)}, bf16[136,128]{1,0:T(8,128)(2,1)S(1)}, u32[]{:S(2)}, u32[]{:S(2)}) %collective-permute-start) | collective-permute-done | bytes 34848 | tf_op jit(solution)/shard_map/ppermute | solution.py:389
  7.2 0.0 copy-start.5
  7.3 2.0 %collective-permute-start.4 = (bf16[136,128]{1,0:T(8,128)(2,1)S(1)}, bf16[136,128]{1,0:T(8,128)(2,1)S(1)}, u32[]{:S(2)}, u32[]{:S(2)}) collective-permute-start(bf16[136,128]{1,0:T(8,128)(2,1)S(1)} %fold.1.order_ref.refs_1_.refs_4_), channel_id=1, source_target_pairs={{0,2},{1,3},{2,4},{3,5},{4,6},{5,7},{6,0},{7,1},{8,10},{9,11},{10,... | collective-permute-start | bytes 104456 | tf_op jit(solution)/shard_map/ppermute | solution.py:389
  9.3 2.6 %collective-permute-start.3 = (bf16[136,128]{1,0:T(8,128)(2,1)S(1)}, bf16[136,128]{1,0:T(8,128)(2,1)S(1)}, u32[]{:S(2)}, u32[]{:S(2)}) collective-permute-start(bf16[136,128]{1,0:T(8,128)(2,1)S(1)} %fold.1.order_ref.refs_1_.refs_4_), channel_id=1, source_target_pairs={{0,4},{1,5},{2,6},{3,7},{4,0},{5,1},{6,2},{7,3},{8,12},{9,13},{10,... | collective-permute-start | bytes 104456 | tf_op jit(solution)/shard_map/ppermute | solution.py:389
  11.9 1.3 %collective-permute-start.2 = (bf16[136,128]{1,0:T(8,128)(2,1)S(1)}, bf16[136,128]{1,0:T(8,128)(2,1)S(1)}, u32[]{:S(2)}, u32[]{:S(2)}) collective-permute-start(bf16[136,128]{1,0:T(8,128)(2,1)S(1)} %fold.1.order_ref.refs_1_.refs_4_), channel_id=1, source_target_pairs={{0,6},{1,7},{2,0},{3,1},{4,2},{5,3},{6,4},{7,5},{8,14},{9,15},{10,... | collective-permute-start | bytes 104456 | tf_op jit(solution)/shard_map/ppermute | solution.py:389
  13.3 0.0 copy-done.1
  13.3 0.0 copy-done.2
  13.3 0.0 copy-done.4
  13.3 0.0 copy-done
  13.3 0.0 copy-done.5
  13.3 1.7 %forward.1 = (f32[1024,128]{1,0:T(8,128)S(1)}, f32[1024,128]{1,0:T(8,128)S(1)}, f32[40,128]{1,0:T(8,128)S(1)}, bf16[128,1024]{1,0:T(8,128)(2,1)S(1)}, f32[1024,1...) custom-call(bf16[1024,128]{1,0:T(8,128)(2,1)S(1)} %bitcast.21, bf16[1024,128]{1,0:T(8,128)(2,1)S(1)} %bitcast.11, ...), custom_call_target="tpu_custom_call" | custom-call | bytes 1024 | tf_op jit(solution)/shard_map/forward/pallas_call | solution.py:435
  15.0 0.3 %turned.1 = (bf16[1024,256]{1,0:T(8,128)(2,1)S(1)}, f32[1024,128]{1,0:T(8,128)S(1)}) custom-call(bf16[1024,128]{1,0:T(8,128)(2,1)S(1)} %bitcast.22, bf16[1024,128]{1,0:T(8,128)(2,1)S(1)} %bitcast.12, f32[1024,128]{1,0:T(8,128)S(1)} %get-tuple-element.30.downs_ref, f32[40,128]{1,0:T(8,128)S(1)} %get-tuple-element.31.rows_ref, ...), custom_call_target="tpu_custom_call" | custom-call | bytes 1024 | tf_op jit(solution)/shard_map/turned/pallas_call | solution.py:438
  15.3 0.0 collective-permute-done.4.refs_5_.refs_8_
  15.3 0.0 collective-permute-done.3.refs_4_.refs_7_
  15.3 0.5 %collective-permute-done.2.refs_3_.refs_6_ = bf16[136,128]{1,0:T(8,128)(2,1)S(1)} collective-permute-done((bf16[136,128]{1,0:T(8,128)(2,1)S(1)}, bf16[136,128]{1,0:T(8,128)(2,1)S(1)}, u32[]{:S(2)}, u32[]{:S(2)}) %collective-permute-start.2) | collective-permute-done | bytes 34848 | tf_op jit(solution)/shard_map/ppermute | solution.py:389
  15.9 0.7 %norm.1 = (bf16[1024,128]{1,0:T(8,128)(2,1)S(1)}, f32[1024,128]{1,0:T(8,128)S(1)}, f32[128,128]{1,0:T(8,128)S(1)}, bf16[128,128]{1,0:T(8,128)(2,1)S(1)}) custom-call(f32[1024,128]{1,0:T(8,128)S(1)} %get-tuple-element.34.local_ref, bf16[1024,128]{1,0:T(8,128)(2,1)S(1)} %bitcast.23, bf16[128,1024]{1,0:T(8,128)(2,1)S(1)} %get-tuple-element.35.qt_ref, ...), custom_call_target="tpu_custom_call" | custom-call | bytes 1024 | tf_op jit(solution)/shard_map/norm/pallas_call | solution.py:441
  16.6 1.6 %collective-permute-start.6 = (bf16[128,128]{1,0:T(8,128)(2,1)S(1)}, bf16[128,128]{1,0:T(8,128)(2,1)S(1)}, u32[]{:S(2)}, u32[]{:S(2)}) collective-permute-start(bf16[128,128]{1,0:T(8,128)(2,1)S(1)} %get-tuple-element.40.order_ref.own_ref), channel_id=1, source_target_pairs={{0,1},{1,0},{2,3},{3,2},{4,5},{5,4},{6,7},{7,6},{8,9},{9,8},{10,11... | collective-permute-start | bytes 98312 | tf_op jit(solution)/shard_map/ppermute | solution.py:389
  18.1 0.0 collective-permute-done.5.refs_2_
  18.1 1.7 %queries.1 = (bf16[1024,128]{1,0:T(8,128)(2,1)}, bf16[1024,128]{1,0:T(8,128)(2,1)}, f32[32,1536]{1,0:T(8,128)}, f32[16,128]{1,0:T(8,128)S(1)}) custom-call(bf16[1024,128]{1,0:T(8,128)(2,1)S(1)} %bitcast.13, bf16[1024,128]{1,0:T(8,128)(2,1)S(1)} %bitcast.18, f32[1024,128]{1,0:T(8,128)S(1)} %get-tuple-element.30.downs_ref, ...), custom_call_target="tpu_custom_call" | custom-call | bytes 1024 | tf_op jit(solution)/shard_map/queries/pallas_call | solution.py:445
  19.9 0.7 %collective-permute-done.6.refs_0_ = bf16[128,128]{1,0:T(8,128)(2,1)S(1)} collective-permute-done((bf16[128,128]{1,0:T(8,128)(2,1)S(1)}, bf16[128,128]{1,0:T(8,128)(2,1)S(1)}, u32[]{:S(2)}, u32[]{:S(2)}) %collective-permute-start.6) | collective-permute-done | bytes 32800 | tf_op jit(solution)/shard_map/ppermute | solution.py:389
  20.6 1.0 %collective-permute-start.9 = (bf16[128,128]{1,0:T(8,128)(2,1)S(1)}, bf16[128,128]{1,0:T(8,128)(2,1)S(1)}, u32[]{:S(2)}, u32[]{:S(2)}) collective-permute-start(bf16[128,128]{1,0:T(8,128)(2,1)S(1)} %fold_back.1.order_ref), channel_id=1, source_target_pairs={{0,4},{1,5},{2,6},{3,7},{4,2},{5,3},{6,0},{7,1},{8,12},{9,13},{10,... | collective-permute-start | bytes 98312 | tf_op jit(solution)/shard_map/ppermute | solution.py:389
  21.5 0.8 %collective-permute-start.8 = (bf16[128,128]{1,0:T(8,128)(2,1)S(1)}, bf16[128,128]{1,0:T(8,128)(2,1)S(1)}, u32[]{:S(2)}, u32[]{:S(2)}) collective-permute-start(bf16[128,128]{1,0:T(8,128)(2,1)S(1)} %fold_back.1.order_ref), channel_id=1, source_target_pairs={{0,4},{1,5},{2,6},{3,7},{4,0},{5,1},{6,2},{7,3},{8,12},{9,13},{10,... | collective-permute-start | bytes 98312 | tf_op jit(solution)/shard_map/ppermute | solution.py:389
  22.4 2.7 %collective-permute-start.7 = (bf16[128,128]{1,0:T(8,128)(2,1)S(1)}, bf16[128,128]{1,0:T(8,128)(2,1)S(1)}, u32[]{:S(2)}, u32[]{:S(2)}) collective-permute-start(bf16[128,128]{1,0:T(8,128)(2,1)S(1)} %fold_back.1.order_ref), channel_id=1, source_target_pairs={{0,2},{1,3},{2,0},{3,1},{4,6},{5,7},{6,4},{7,5},{8,10},{9,11},{10,... | collective-permute-start | bytes 98312 | tf_op jit(solution)/shard_map/ppermute | solution.py:389
  25.0 1.7 %keys.1 = (f32[1024,128]{1,0:T(8,128)S(1)}, f32[1024,128]{1,0:T(8,128)S(1)}, f32[1024,128]{1,0:T(8,128)S(1)}) custom-call(bf16[1024,128]{1,0:T(8,128)(2,1)S(1)} %bitcast.24, bf16[1024,128]{1,0:T(8,128)(2,1)S(1)} %bitcast.14, bf16[1024,128]{1,0:T(8,128)(2,1)S(1)} %bitcast.19, bf16[128,1024]{1,0:T(8,128)(2,1)S(1)} %get-tuple-element.35.qt_ref, ...), custom_call_target="tpu_custom_call" | custom-call | bytes 1024 | tf_op jit(solution)/shard_map/keys/pallas_call | solution.py:462
  26.7 0.0 collective-permute-done.9.refs_3_
  26.8 0.0 collective-permute-done.8.refs_2_
  26.8 0.3 %collective-permute-done.7.refs_1_ = bf16[128,128]{1,0:T(8,128)(2,1)S(1)} collective-permute-done((bf16[128,128]{1,0:T(8,128)(2,1)S(1)}, bf16[128,128]{1,0:T(8,128)(2,1)S(1)}, u32[]{:S(2)}, u32[]{:S(2)}) %collective-permute-start.7) | collective-permute-done | bytes 32800 | tf_op jit(solution)/shard_map/ppermute | solution.py:389
  27.0 1.1 %last.1 = (bf16[1024,128]{1,0:T(8,128)(2,1)}, bf16[1024,128]{1,0:T(8,128)(2,1)}) custom-call(f32[1024,128]{1,0:T(8,128)S(1)} %get-tuple-element.47.dk_ref, f32[1024,128]{1,0:T(8,128)S(1)} %get-tuple-element.48.dv_ref, bf16[1024,128]{1,0:T(8,128)(2,1)S(1)} %bitcast.15, bf16[1024,128]{1,0:T(8,128)(2,1)S(1)} %bitcast.20, ...), custom_call_target="tpu_custom_call" | custom-call | bytes 1024 | tf_op jit(solution)/shard_map/last/pallas_call | solution.py:463
  (3 shorter events, 0.1 us)
Async XLA Ops:
  0.6 1.5 %copy-start.3 = (bf16[1,32,6144]{2,1,0:T(8,128)(2,1)S(1)}, bf16[1,32,6144]{2,1,0:T(8,128)(2,1)}, u32[]{:S(2)}) copy-start(bf16[1,32,6144]{2,1,0:T(8,128)(2,1)} %param.11) | copy-start | bytes 1179652
  2.1 3.1 %collective-permute-start.1 = (bf16[32,3072]{1,0:T(8,128)(2,1)S(1)}, bf16[32,3072]{1,0:T(8,128)(2,1)S(1)}, u32[]{:S(2)}, u32[]{:S(2)}) collective-permute-start(bf16[32,3072]{1,0:T(8,128)(2,1)S(1)} %cut.1), channel_id=1, source_target_pairs={{0,8},{8,0},{16,24},{24,16},{1,9},{9,1},{17,25},{25,17},{2,10},{10... | collective-permute-start | bytes 589832 | tf_op jit(solution)/shard_map/ppermute | solution.py:389
  2.6 4.6 %collective-permute-start = (bf16[136,128]{1,0:T(8,128)(2,1)S(1)}, bf16[136,128]{1,0:T(8,128)(2,1)S(1)}, u32[]{:S(2)}, u32[]{:S(2)}) collective-permute-start(bf16[136,128]{1,0:T(8,128)(2,1)S(1)} %state.1.order_ref.own_ref.refs_0_.refs_3_), channel_id=1, source_target_pairs={{0,1},{1,0},{2,3},{3,2},{4,5},{5,4},{6,7},{7,6},{8,9},{9,8},{10,11... | collective-permute-start | bytes 104456 | tf_op jit(solution)/shard_map/ppermute | solution.py:389
  5.2 8.1 %copy-start.1 = (bf16[1,1024,128]{2,1,0:T(8,128)(2,1)S(1)}, bf16[1,1024,128]{2,1,0:T(8,128)(2,1)}, u32[]{:S(2)}) copy-start(bf16[1,1024,128]{2,1,0:T(8,128)(2,1)} %param.8) | copy-start | bytes 786436
  5.2 8.1 %copy-start.2 = (bf16[1,1024,128]{2,1,0:T(8,128)(2,1)S(1)}, bf16[1,1024,128]{2,1,0:T(8,128)(2,1)}, u32[]{:S(2)}) copy-start(bf16[1,1024,128]{2,1,0:T(8,128)(2,1)} %param.6) | copy-start | bytes 786436
  5.2 8.1 %copy-start.4 = (bf16[1,1024,128]{2,1,0:T(8,128)(2,1)S(1)}, bf16[1,1024,128]{2,1,0:T(8,128)(2,1)}, u32[]{:S(2)}) copy-start(bf16[1,1024,128]{2,1,0:T(8,128)(2,1)} %param.9) | copy-start | bytes 786436
  5.3 8.0 %copy-start = (bf16[1,1024,128]{2,1,0:T(8,128)(2,1)S(1)}, bf16[1,1024,128]{2,1,0:T(8,128)(2,1)}, u32[]{:S(2)}) copy-start(bf16[1,1024,128]{2,1,0:T(8,128)(2,1)} %param.7) | copy-start | bytes 786436
  5.3 12.8 %collective-permute-start.5 = (bf16[32,1536]{1,0:T(8,128)(2,1)S(1)}, bf16[32,1536]{1,0:T(8,128)(2,1)S(1)}, u32[]{:S(2)}, u32[]{:S(2)}) collective-permute-start(bf16[32,1536]{1,0:T(8,128)(2,1)S(1)} %get-tuple-element.42), channel_id=1, source_target_pairs={{0,16},{8,24},{16,0},{24,8},{1,17},{9,25},{17,1},{25,9},{2,18},{10... | collective-permute-start | bytes 294920 | tf_op jit(solution)/shard_map/ppermute | solution.py:389
  7.2 6.0 %copy-start.5 = (f32[1,1,1024]{2,1,0:T(1,128)S(1)}, f32[1,1,1024]{2,1,0:T(1,128)}, u32[]{:S(2)}) copy-start(f32[1,1,1024]{2,1,0:T(1,128)} %param.10) | copy-start | bytes 12292
  7.3 8.0 %collective-permute-start.4 = (bf16[136,128]{1,0:T(8,128)(2,1)S(1)}, bf16[136,128]{1,0:T(8,128)(2,1)S(1)}, u32[]{:S(2)}, u32[]{:S(2)}) collective-permute-start(bf16[136,128]{1,0:T(8,128)(2,1)S(1)} %fold.1.order_ref.refs_1_.refs_4_), channel_id=1, source_target_pairs={{0,2},{1,3},{2,4},{3,5},{4,6},{5,7},{6,0},{7,1},{8,10},{9,11},{10,... | collective-permute-start | bytes 104456 | tf_op jit(solution)/shard_map/ppermute | solution.py:389
  9.3 6.0 %collective-permute-start.3 = (bf16[136,128]{1,0:T(8,128)(2,1)S(1)}, bf16[136,128]{1,0:T(8,128)(2,1)S(1)}, u32[]{:S(2)}, u32[]{:S(2)}) collective-permute-start(bf16[136,128]{1,0:T(8,128)(2,1)S(1)} %fold.1.order_ref.refs_1_.refs_4_), channel_id=1, source_target_pairs={{0,4},{1,5},{2,6},{3,7},{4,0},{5,1},{6,2},{7,3},{8,12},{9,13},{10,... | collective-permute-start | bytes 104456 | tf_op jit(solution)/shard_map/ppermute | solution.py:389
  11.9 3.9 %collective-permute-start.2 = (bf16[136,128]{1,0:T(8,128)(2,1)S(1)}, bf16[136,128]{1,0:T(8,128)(2,1)S(1)}, u32[]{:S(2)}, u32[]{:S(2)}) collective-permute-start(bf16[136,128]{1,0:T(8,128)(2,1)S(1)} %fold.1.order_ref.refs_1_.refs_4_), channel_id=1, source_target_pairs={{0,6},{1,7},{2,0},{3,1},{4,2},{5,3},{6,4},{7,5},{8,14},{9,15},{10,... | collective-permute-start | bytes 104456 | tf_op jit(solution)/shard_map/ppermute | solution.py:389
  16.6 4.0 %collective-permute-start.6 = (bf16[128,128]{1,0:T(8,128)(2,1)S(1)}, bf16[128,128]{1,0:T(8,128)(2,1)S(1)}, u32[]{:S(2)}, u32[]{:S(2)}) collective-permute-start(bf16[128,128]{1,0:T(8,128)(2,1)S(1)} %get-tuple-element.40.order_ref.own_ref), channel_id=1, source_target_pairs={{0,1},{1,0},{2,3},{3,2},{4,5},{5,4},{6,7},{7,6},{8,9},{9,8},{10,11... | collective-permute-start | bytes 98312 | tf_op jit(solution)/shard_map/ppermute | solution.py:389
  20.6 6.2 %collective-permute-start.9 = (bf16[128,128]{1,0:T(8,128)(2,1)S(1)}, bf16[128,128]{1,0:T(8,128)(2,1)S(1)}, u32[]{:S(2)}, u32[]{:S(2)}) collective-permute-start(bf16[128,128]{1,0:T(8,128)(2,1)S(1)} %fold_back.1.order_ref), channel_id=1, source_target_pairs={{0,4},{1,5},{2,6},{3,7},{4,2},{5,3},{6,0},{7,1},{8,12},{9,13},{10,... | collective-permute-start | bytes 98312 | tf_op jit(solution)/shard_map/ppermute | solution.py:389
  21.5 5.2 %collective-permute-start.8 = (bf16[128,128]{1,0:T(8,128)(2,1)S(1)}, bf16[128,128]{1,0:T(8,128)(2,1)S(1)}, u32[]{:S(2)}, u32[]{:S(2)}) collective-permute-start(bf16[128,128]{1,0:T(8,128)(2,1)S(1)} %fold_back.1.order_ref), channel_id=1, source_target_pairs={{0,4},{1,5},{2,6},{3,7},{4,0},{5,1},{6,2},{7,3},{8,12},{9,13},{10,... | collective-permute-start | bytes 98312 | tf_op jit(solution)/shard_map/ppermute | solution.py:389
  22.4 4.7 %collective-permute-start.7 = (bf16[128,128]{1,0:T(8,128)(2,1)S(1)}, bf16[128,128]{1,0:T(8,128)(2,1)S(1)}, u32[]{:S(2)}, u32[]{:S(2)}) collective-permute-start(bf16[128,128]{1,0:T(8,128)(2,1)S(1)} %fold_back.1.order_ref), channel_id=1, source_target_pairs={{0,2},{1,3},{2,0},{3,1},{4,6},{5,7},{6,4},{7,5},{8,10},{9,11},{10,... | collective-permute-start | bytes 98312 | tf_op jit(solution)/shard_map/ppermute | solution.py:389

commit v5 on v4

--- a/solution.py
+++ b/solution.py
@@ -13,7 +13,7 @@
 BF16 = jnp.bfloat16
 FORWARD_OF_4 = ((3, 0, 1, 2), (2, 3, 0, 1), (1, 2, 3, 0))
 LAST_BACKWARD_OF_4 = ((1, 0, 3, 2), (2, 3, 0, 1), (2, 3, 1, 0))
-LOGS = 8
+LOGS = 16
 
 
 def mm(a, b):
@@ -90,8 +90,11 @@
     return rows[0:1] + rows[1:2] + rows[2:3]
 
 
-def state_kernel(k_hbm, v_hbm, decay_hbm, out_ref, k_ref, v_ref, decay_ref, sems):
-    pairs = ((decay_hbm, decay_ref), (k_hbm, k_ref), (v_hbm, v_ref))
+def state_kernel(columns, k_hbm, v_hbm, decay_hbm, grads_hbm, out_ref, sent_ref, k_ref, v_ref, decay_ref, sems):
+    pairs = [(decay_hbm, decay_ref), (k_hbm, k_ref), (v_hbm, v_ref)]
+    for i in range(grads_hbm.shape[1] // columns // 2):
+        block = grads_hbm.at[:, pl.ds(pl.multiple_of((2 * i + 1 - bit(1)) * columns, C), columns)]
+        pairs.append((block, sent_ref.at[:, pl.ds(i * columns, columns)]))
     copies = [pltpu.make_async_copy(source, target, sems.at[i]) for i, (source, target) in enumerate(pairs)]
     for copy in copies:
         copy.start()
@@ -108,6 +111,8 @@
         state = state + mm(kw.astype(BF16), chunk(v_ref, r))
     out_ref[:C, :] = state.astype(BF16)
     out_ref[C:, :] = log_rows(sum(tot))
+    for copy in copies[3:]:
+        copy.wait()
 
 
 def between(logs, positions, low, high):
@@ -336,11 +341,6 @@
     return lax.rem(lax.div(lax.axis_index("dp"), stride), 2)
 
 
-def cut_kernel(columns, have_ref, order_ref, sent_ref):
-    for i in range(have_ref.shape[1] // columns // 2):
-        sent_ref[:, i * columns : (i + 1) * columns] = half(have_ref, columns, 1 - bit(1), i)
-
-
 def add_kernel(columns, stride, have_ref, came_ref, kept_ref, sent_ref):
     for i in range(have_ref.shape[1] // columns // 2):
         kept = half(have_ref, columns, bit(stride), i).astype(F32)
@@ -404,24 +404,22 @@
     whole = pltpu.VMEM((tokens, C), BF16)
     dma = pltpu.SemaphoreType.DMA
 
-    own = [
-        call(
-            state_kernel,
-            payload,
-            "state",
-            scratch=[whole, whole, pltpu.VMEM((n, C), F32), dma((3,))],
-            in_specs=[away] * 3,
-        )(*[pltpu.with_memory_space_constraint(x, pltpu.HBM) for x in (k, v, decay)])
-    ]
     grads = prev_grads[0]
     lines = grads.shape[0]
     columns = grads.shape[1] // dp
+    state, sent = call(
+        functools.partial(state_kernel, columns),
+        (payload, shape((lines, grads.shape[1] // 2), BF16)),
+        "state",
+        scratch=[whole, whole, pltpu.VMEM((n, C), F32), dma((3 + dp // 2,))],
+        in_specs=[away] * 4,
+    )(*[pltpu.with_memory_space_constraint(x, pltpu.HBM) for x in (k, v, decay, grads)])
+    own = [state]
     others = []
     for i, (stride, radix, rounds, _) in enumerate(levels):
         got = [send(own[-1], "seq", seq, targets) for targets in rounds]
         others += got
         if i == 0:
-            sent = call(functools.partial(cut_kernel, columns), shape((lines, grads.shape[1] // 2), BF16), "cut")(grads, own[0])
             came = send(sent, "dp", dp, (1, 0))
             total, part = grads, 1
             while 2 * part < dp:

time: 28.3 us -> 28.3 us (level)
    pallas_call x2 -> x1, Pallas kernels: 1.46 us -> 1.45 us  [local(): call(functools.partial(state_kernel, columns), (payload, shape((lines, gr...]
where the time goes in v5:
time: 28.3 us; the launch traced here: 28.2 us
  starting transfers between devices  16.6 us (59%)
  Pallas kernels  8.89 us (31%)
  waiting for transfers between devices  1.88 us (7%)
  between operations  0.77 us (3%)
    ppermute x10, starting transfers between devices, send(): return lax.ppermute(x, axis, pairs)  16.6 us
    ppermute x10, waiting for transfers between devices, send(): return lax.ppermute(x, axis, pairs)  1.88 us
    pallas_call x1, Pallas kernels, local(): call(functools.partial(queries_kernel, levels, count, columns, dp // 2),...  1.74 us
    pallas_call x1, Pallas kernels, local(): call(keys_kernel, (wide, wide, wide), 'keys')  1.71 us
    pallas_call x1, Pallas kernels, local(): call(forward_kernel, (wide, wide, shape((5 * n, C), F32), shape((C, token...  1.71 us
    pallas_call x1, Pallas kernels, local(): call(functools.partial(state_kernel, columns), (payload, shape((lines, gr...  1.45 us
    pallas_call x1, Pallas kernels, local(): call(functools.partial(last_kernel, levels), (narrow, narrow), 'last', sc...  1.12 us
    pallas_call x1, Pallas kernels, local(): call(functools.partial(norm_kernel, levels), (narrow, wide, square, shape...  0.72 us
  transfers between devices with their start and end apart: 10, of which 4 were waited for; matrix products, arithmetic and copies ran while one was open for 0% of the time, Pallas kernels for 22%

profile of v5, /device:TPU:0, one launch (start us, length us, event | category | flops | bytes accessed | tf_op | source)
XLA Modules:
  0.0 28.2 jit_solution(7076875265890701002)
XLA Ops:
  0.6 0.0 copy-start.3
  0.6 1.5 %state.1 = (bf16[144,128]{1,0:T(8,128)(2,1)S(1)}, bf16[32,3072]{1,0:T(8,128)(2,1)S(1)}) custom-call(bf16[1024,128]{1,0:T(8,128)(2,1)} %bitcast.10, bf16[1024,128]{1,0:T(8,128)(2,1)} %bitcast.16, f32[8,128]{1,0:T(8,128)} %bitcast.29, bf16[32,6144]{1,0:T(8,128)(2,1)} %bitcast.25), custom_call_target="tpu_custom_call" | custom-call | bytes 1024 | tf_op jit(solution)/shard_map/state/pallas_call | solution.py:410
  2.1 0.5 %collective-permute-start.1 = (bf16[32,3072]{1,0:T(8,128)(2,1)S(1)}, bf16[32,3072]{1,0:T(8,128)(2,1)S(1)}, u32[]{:S(2)}, u32[]{:S(2)}) collective-permute-start(bf16[32,3072]{1,0:T(8,128)(2,1)S(1)} %get-tuple-element.32), channel_id=1, source_target_pairs={{0,8},{8,0},{16,24},{24,16},{1,9},{9,1},{17,25},{25,17},{2,10},{10... | collective-permute-start | bytes 589832 | tf_op jit(solution)/shard_map/ppermute | solution.py:389
  2.6 2.6 %collective-permute-start = (bf16[144,128]{1,0:T(8,128)(2,1)S(1)}, bf16[144,128]{1,0:T(8,128)(2,1)S(1)}, u32[]{:S(2)}, u32[]{:S(2)}) collective-permute-start(bf16[144,128]{1,0:T(8,128)(2,1)S(1)} %get-tuple-element.31.own_ref.refs_0_.refs_3_), channel_id=1, source_target_pairs={{0,1},{1,0},{2,3},{3,2},{4,5},{5,4},{6,7},{7,6},{8,9},{9,8},{10,11... | collective-permute-start | bytes 110600 | tf_op jit(solution)/shard_map/ppermute | solution.py:389
  5.2 0.0 collective-permute-done.1.came_ref
  5.2 0.0 copy-done.3
  5.2 0.0 copy-start.1
  5.2 0.0 copy-start.2
  5.2 0.0 copy-start.4
  5.2 0.1 add.1
  5.3 0.0 copy-start
  5.3 1.6 %collective-permute-start.5 = (bf16[32,1536]{1,0:T(8,128)(2,1)S(1)}, bf16[32,1536]{1,0:T(8,128)(2,1)S(1)}, u32[]{:S(2)}, u32[]{:S(2)}) collective-permute-start(bf16[32,1536]{1,0:T(8,128)(2,1)S(1)} %get-tuple-element.46), channel_id=1, source_target_pairs={{0,16},{8,24},{16,0},{24,8},{1,17},{9,25},{17,1},{25,9},{2,18},{10... | collective-permute-start | bytes 294920 | tf_op jit(solution)/shard_map/ppermute | solution.py:389
  6.9 0.4 %collective-permute-done.refs_0_.refs_2_.refs_5_ = bf16[144,128]{1,0:T(8,128)(2,1)S(1)} collective-permute-done((bf16[144,128]{1,0:T(8,128)(2,1)S(1)}, bf16[144,128]{1,0:T(8,128)(2,1)S(1)}, u32[]{:S(2)}, u32[]{:S(2)}) %collective-permute-start) | collective-permute-done | bytes 36896 | tf_op jit(solution)/shard_map/ppermute | solution.py:389
  7.3 0.0 copy-start.5
  7.3 2.0 %collective-permute-start.4 = (bf16[144,128]{1,0:T(8,128)(2,1)S(1)}, bf16[144,128]{1,0:T(8,128)(2,1)S(1)}, u32[]{:S(2)}, u32[]{:S(2)}) collective-permute-start(bf16[144,128]{1,0:T(8,128)(2,1)S(1)} %fold.1.order_ref.refs_1_.refs_4_), channel_id=1, source_target_pairs={{0,2},{1,3},{2,4},{3,5},{4,6},{5,7},{6,0},{7,1},{8,10},{9,11},{10,... | collective-permute-start | bytes 110600 | tf_op jit(solution)/shard_map/ppermute | solution.py:389
  9.3 2.6 %collective-permute-start.3 = (bf16[144,128]{1,0:T(8,128)(2,1)S(1)}, bf16[144,128]{1,0:T(8,128)(2,1)S(1)}, u32[]{:S(2)}, u32[]{:S(2)}) collective-permute-start(bf16[144,128]{1,0:T(8,128)(2,1)S(1)} %fold.1.order_ref.refs_1_.refs_4_), channel_id=1, source_target_pairs={{0,4},{1,5},{2,6},{3,7},{4,0},{5,1},{6,2},{7,3},{8,12},{9,13},{10,... | collective-permute-start | bytes 110600 | tf_op jit(solution)/shard_map/ppermute | solution.py:389
  11.9 1.3 %collective-permute-start.2 = (bf16[144,128]{1,0:T(8,128)(2,1)S(1)}, bf16[144,128]{1,0:T(8,128)(2,1)S(1)}, u32[]{:S(2)}, u32[]{:S(2)}) collective-permute-start(bf16[144,128]{1,0:T(8,128)(2,1)S(1)} %fold.1.order_ref.refs_1_.refs_4_), channel_id=1, source_target_pairs={{0,6},{1,7},{2,0},{3,1},{4,2},{5,3},{6,4},{7,5},{8,14},{9,15},{10,... | collective-permute-start | bytes 110600 | tf_op jit(solution)/shard_map/ppermute | solution.py:389
  13.3 0.0 copy-done.1
  13.3 0.0 copy-done.2
  13.3 0.0 copy-done.4
  13.3 0.0 copy-done
  13.3 0.0 copy-done.5
  13.3 1.7 %forward.1 = (f32[1024,128]{1,0:T(8,128)S(1)}, f32[1024,128]{1,0:T(8,128)S(1)}, f32[40,128]{1,0:T(8,128)S(1)}, bf16[128,1024]{1,0:T(8,128)(2,1)S(1)}, f32[1024,1...) custom-call(bf16[1024,128]{1,0:T(8,128)(2,1)S(1)} %bitcast.21, bf16[1024,128]{1,0:T(8,128)(2,1)S(1)} %bitcast.11, ...), custom_call_target="tpu_custom_call" | custom-call | bytes 1024 | tf_op jit(solution)/shard_map/forward/pallas_call | solution.py:433
  15.0 0.3 %turned.1 = (bf16[1024,256]{1,0:T(8,128)(2,1)S(1)}, f32[1024,128]{1,0:T(8,128)S(1)}) custom-call(bf16[1024,128]{1,0:T(8,128)(2,1)S(1)} %bitcast.22, bf16[1024,128]{1,0:T(8,128)(2,1)S(1)} %bitcast.12, f32[1024,128]{1,0:T(8,128)S(1)} %get-tuple-element.34.downs_ref, f32[40,128]{1,0:T(8,128)S(1)} %get-tuple-element.35.rows_ref, ...), custom_call_target="tpu_custom_call" | custom-call | bytes 1024 | tf_op jit(solution)/shard_map/turned/pallas_call | solution.py:436
  15.3 0.0 collective-permute-done.4.refs_5_.refs_8_
  15.3 0.0 collective-permute-done.3.refs_4_.refs_7_
  15.3 0.5 %collective-permute-done.2.refs_3_.refs_6_ = bf16[144,128]{1,0:T(8,128)(2,1)S(1)} collective-permute-done((bf16[144,128]{1,0:T(8,128)(2,1)S(1)}, bf16[144,128]{1,0:T(8,128)(2,1)S(1)}, u32[]{:S(2)}, u32[]{:S(2)}) %collective-permute-start.2) | collective-permute-done | bytes 36896 | tf_op jit(solution)/shard_map/ppermute | solution.py:389
  15.9 0.7 %norm.1 = (bf16[1024,128]{1,0:T(8,128)(2,1)S(1)}, f32[1024,128]{1,0:T(8,128)S(1)}, f32[128,128]{1,0:T(8,128)S(1)}, bf16[128,128]{1,0:T(8,128)(2,1)S(1)}) custom-call(f32[1024,128]{1,0:T(8,128)S(1)} %get-tuple-element.38.local_ref, bf16[1024,128]{1,0:T(8,128)(2,1)S(1)} %bitcast.23, bf16[128,1024]{1,0:T(8,128)(2,1)S(1)} %get-tuple-element.39.qt_ref, ...), custom_call_target="tpu_custom_call" | custom-call | bytes 1024 | tf_op jit(solution)/shard_map/norm/pallas_call | solution.py:439
  16.6 1.6 %collective-permute-start.6 = (bf16[128,128]{1,0:T(8,128)(2,1)S(1)}, bf16[128,128]{1,0:T(8,128)(2,1)S(1)}, u32[]{:S(2)}, u32[]{:S(2)}) collective-permute-start(bf16[128,128]{1,0:T(8,128)(2,1)S(1)} %get-tuple-element.44.order_ref.own_ref), channel_id=1, source_target_pairs={{0,1},{1,0},{2,3},{3,2},{4,5},{5,4},{6,7},{7,6},{8,9},{9,8},{10,11... | collective-permute-start | bytes 98312 | tf_op jit(solution)/shard_map/ppermute | solution.py:389
  18.2 0.0 collective-permute-done.5.refs_2_
  18.2 1.7 %queries.1 = (bf16[1024,128]{1,0:T(8,128)(2,1)}, bf16[1024,128]{1,0:T(8,128)(2,1)}, f32[32,1536]{1,0:T(8,128)}, f32[16,128]{1,0:T(8,128)S(1)}) custom-call(bf16[1024,128]{1,0:T(8,128)(2,1)S(1)} %bitcast.13, bf16[1024,128]{1,0:T(8,128)(2,1)S(1)} %bitcast.18, f32[1024,128]{1,0:T(8,128)S(1)} %get-tuple-element.34.downs_ref, ...), custom_call_target="tpu_custom_call" | custom-call | bytes 1024 | tf_op jit(solution)/shard_map/queries/pallas_call | solution.py:443
  19.9 0.7 %collective-permute-done.6.refs_0_ = bf16[128,128]{1,0:T(8,128)(2,1)S(1)} collective-permute-done((bf16[128,128]{1,0:T(8,128)(2,1)S(1)}, bf16[128,128]{1,0:T(8,128)(2,1)S(1)}, u32[]{:S(2)}, u32[]{:S(2)}) %collective-permute-start.6) | collective-permute-done | bytes 32800 | tf_op jit(solution)/shard_map/ppermute | solution.py:389
  20.6 1.0 %collective-permute-start.9 = (bf16[128,128]{1,0:T(8,128)(2,1)S(1)}, bf16[128,128]{1,0:T(8,128)(2,1)S(1)}, u32[]{:S(2)}, u32[]{:S(2)}) collective-permute-start(bf16[128,128]{1,0:T(8,128)(2,1)S(1)} %fold_back.1.order_ref), channel_id=1, source_target_pairs={{0,4},{1,5},{2,6},{3,7},{4,2},{5,3},{6,0},{7,1},{8,12},{9,13},{10,... | collective-permute-start | bytes 98312 | tf_op jit(solution)/shard_map/ppermute | solution.py:389
  21.6 0.8 %collective-permute-start.8 = (bf16[128,128]{1,0:T(8,128)(2,1)S(1)}, bf16[128,128]{1,0:T(8,128)(2,1)S(1)}, u32[]{:S(2)}, u32[]{:S(2)}) collective-permute-start(bf16[128,128]{1,0:T(8,128)(2,1)S(1)} %fold_back.1.order_ref), channel_id=1, source_target_pairs={{0,4},{1,5},{2,6},{3,7},{4,0},{5,1},{6,2},{7,3},{8,12},{9,13},{10,... | collective-permute-start | bytes 98312 | tf_op jit(solution)/shard_map/ppermute | solution.py:389
  22.4 2.6 %collective-permute-start.7 = (bf16[128,128]{1,0:T(8,128)(2,1)S(1)}, bf16[128,128]{1,0:T(8,128)(2,1)S(1)}, u32[]{:S(2)}, u32[]{:S(2)}) collective-permute-start(bf16[128,128]{1,0:T(8,128)(2,1)S(1)} %fold_back.1.order_ref), channel_id=1, source_target_pairs={{0,2},{1,3},{2,0},{3,1},{4,6},{5,7},{6,4},{7,5},{8,10},{9,11},{10,... | collective-permute-start | bytes 98312 | tf_op jit(solution)/shard_map/ppermute | solution.py:389
  25.0 1.7 %keys.1 = (f32[1024,128]{1,0:T(8,128)S(1)}, f32[1024,128]{1,0:T(8,128)S(1)}, f32[1024,128]{1,0:T(8,128)S(1)}) custom-call(bf16[1024,128]{1,0:T(8,128)(2,1)S(1)} %bitcast.24, bf16[1024,128]{1,0:T(8,128)(2,1)S(1)} %bitcast.14, bf16[1024,128]{1,0:T(8,128)(2,1)S(1)} %bitcast.19, bf16[128,1024]{1,0:T(8,128)(2,1)S(1)} %get-tuple-element.39.qt_ref, ...), custom_call_target="tpu_custom_call" | custom-call | bytes 1024 | tf_op jit(solution)/shard_map/keys/pallas_call | solution.py:460
  26.8 0.0 collective-permute-done.9.refs_3_
  26.8 0.0 collective-permute-done.8.refs_2_
  26.8 0.3 %collective-permute-done.7.refs_1_ = bf16[128,128]{1,0:T(8,128)(2,1)S(1)} collective-permute-done((bf16[128,128]{1,0:T(8,128)(2,1)S(1)}, bf16[128,128]{1,0:T(8,128)(2,1)S(1)}, u32[]{:S(2)}, u32[]{:S(2)}) %collective-permute-start.7) | collective-permute-done | bytes 32800 | tf_op jit(solution)/shard_map/ppermute | solution.py:389
  27.1 1.1 %last.1 = (bf16[1024,128]{1,0:T(8,128)(2,1)}, bf16[1024,128]{1,0:T(8,128)(2,1)}) custom-call(f32[1024,128]{1,0:T(8,128)S(1)} %get-tuple-element.51.dk_ref, f32[1024,128]{1,0:T(8,128)S(1)} %get-tuple-element.52.dv_ref, bf16[1024,128]{1,0:T(8,128)(2,1)S(1)} %bitcast.15, bf16[1024,128]{1,0:T(8,128)(2,1)S(1)} %bitcast.20, ...), custom_call_target="tpu_custom_call" | custom-call | bytes 1024 | tf_op jit(solution)/shard_map/last/pallas_call | solution.py:461
  (2 shorter events, 0.0 us)
Async XLA Ops:
  0.6 4.6 %copy-start.3 = (bf16[1,32,6144]{2,1,0:T(8,128)(2,1)S(1)}, bf16[1,32,6144]{2,1,0:T(8,128)(2,1)}, u32[]{:S(2)}) copy-start(bf16[1,32,6144]{2,1,0:T(8,128)(2,1)} %param.11) | copy-start | bytes 1179652
  2.1 3.1 %collective-permute-start.1 = (bf16[32,3072]{1,0:T(8,128)(2,1)S(1)}, bf16[32,3072]{1,0:T(8,128)(2,1)S(1)}, u32[]{:S(2)}, u32[]{:S(2)}) collective-permute-start(bf16[32,3072]{1,0:T(8,128)(2,1)S(1)} %get-tuple-element.32), channel_id=1, source_target_pairs={{0,8},{8,0},{16,24},{24,16},{1,9},{9,1},{17,25},{25,17},{2,10},{10... | collective-permute-start | bytes 589832 | tf_op jit(solution)/shard_map/ppermute | solution.py:389
  2.6 4.6 %collective-permute-start = (bf16[144,128]{1,0:T(8,128)(2,1)S(1)}, bf16[144,128]{1,0:T(8,128)(2,1)S(1)}, u32[]{:S(2)}, u32[]{:S(2)}) collective-permute-start(bf16[144,128]{1,0:T(8,128)(2,1)S(1)} %get-tuple-element.31.own_ref.refs_0_.refs_3_), channel_id=1, source_target_pairs={{0,1},{1,0},{2,3},{3,2},{4,5},{5,4},{6,7},{7,6},{8,9},{9,8},{10,11... | collective-permute-start | bytes 110600 | tf_op jit(solution)/shard_map/ppermute | solution.py:389
  5.2 8.1 %copy-start.1 = (bf16[1,1024,128]{2,1,0:T(8,128)(2,1)S(1)}, bf16[1,1024,128]{2,1,0:T(8,128)(2,1)}, u32[]{:S(2)}) copy-start(bf16[1,1024,128]{2,1,0:T(8,128)(2,1)} %param.8) | copy-start | bytes 786436
  5.2 8.1 %copy-start.2 = (bf16[1,1024,128]{2,1,0:T(8,128)(2,1)S(1)}, bf16[1,1024,128]{2,1,0:T(8,128)(2,1)}, u32[]{:S(2)}) copy-start(bf16[1,1024,128]{2,1,0:T(8,128)(2,1)} %param.6) | copy-start | bytes 786436
  5.2 8.1 %copy-start.4 = (bf16[1,1024,128]{2,1,0:T(8,128)(2,1)S(1)}, bf16[1,1024,128]{2,1,0:T(8,128)(2,1)}, u32[]{:S(2)}) copy-start(bf16[1,1024,128]{2,1,0:T(8,128)(2,1)} %param.9) | copy-start | bytes 786436
  5.3 8.0 %copy-start = (bf16[1,1024,128]{2,1,0:T(8,128)(2,1)S(1)}, bf16[1,1024,128]{2,1,0:T(8,128)(2,1)}, u32[]{:S(2)}) copy-start(bf16[1,1024,128]{2,1,0:T(8,128)(2,1)} %param.7) | copy-start | bytes 786436
  5.3 12.9 %collective-permute-start.5 = (bf16[32,1536]{1,0:T(8,128)(2,1)S(1)}, bf16[32,1536]{1,0:T(8,128)(2,1)S(1)}, u32[]{:S(2)}, u32[]{:S(2)}) collective-permute-start(bf16[32,1536]{1,0:T(8,128)(2,1)S(1)} %get-tuple-element.46), channel_id=1, source_target_pairs={{0,16},{8,24},{16,0},{24,8},{1,17},{9,25},{17,1},{25,9},{2,18},{10... | collective-permute-start | bytes 294920 | tf_op jit(solution)/shard_map/ppermute | solution.py:389
  7.3 6.0 %copy-start.5 = (f32[1,1,1024]{2,1,0:T(1,128)S(1)}, f32[1,1,1024]{2,1,0:T(1,128)}, u32[]{:S(2)}) copy-start(f32[1,1,1024]{2,1,0:T(1,128)} %param.10) | copy-start | bytes 12292
  7.3 8.0 %collective-permute-start.4 = (bf16[144,128]{1,0:T(8,128)(2,1)S(1)}, bf16[144,128]{1,0:T(8,128)(2,1)S(1)}, u32[]{:S(2)}, u32[]{:S(2)}) collective-permute-start(bf16[144,128]{1,0:T(8,128)(2,1)S(1)} %fold.1.order_ref.refs_1_.refs_4_), channel_id=1, source_target_pairs={{0,2},{1,3},{2,4},{3,5},{4,6},{5,7},{6,0},{7,1},{8,10},{9,11},{10,... | collective-permute-start | bytes 110600 | tf_op jit(solution)/shard_map/ppermute | solution.py:389
  9.3 6.0 %collective-permute-start.3 = (bf16[144,128]{1,0:T(8,128)(2,1)S(1)}, bf16[144,128]{1,0:T(8,128)(2,1)S(1)}, u32[]{:S(2)}, u32[]{:S(2)}) collective-permute-start(bf16[144,128]{1,0:T(8,128)(2,1)S(1)} %fold.1.order_ref.refs_1_.refs_4_), channel_id=1, source_target_pairs={{0,4},{1,5},{2,6},{3,7},{4,0},{5,1},{6,2},{7,3},{8,12},{9,13},{10,... | collective-permute-start | bytes 110600 | tf_op jit(solution)/shard_map/ppermute | solution.py:389
  11.9 4.0 %collective-permute-start.2 = (bf16[144,128]{1,0:T(8,128)(2,1)S(1)}, bf16[144,128]{1,0:T(8,128)(2,1)S(1)}, u32[]{:S(2)}, u32[]{:S(2)}) collective-permute-start(bf16[144,128]{1,0:T(8,128)(2,1)S(1)} %fold.1.order_ref.refs_1_.refs_4_), channel_id=1, source_target_pairs={{0,6},{1,7},{2,0},{3,1},{4,2},{5,3},{6,4},{7,5},{8,14},{9,15},{10,... | collective-permute-start | bytes 110600 | tf_op jit(solution)/shard_map/ppermute | solution.py:389
  16.6 4.0 %collective-permute-start.6 = (bf16[128,128]{1,0:T(8,128)(2,1)S(1)}, bf16[128,128]{1,0:T(8,128)(2,1)S(1)}, u32[]{:S(2)}, u32[]{:S(2)}) collective-permute-start(bf16[128,128]{1,0:T(8,128)(2,1)S(1)} %get-tuple-element.44.order_ref.own_ref), channel_id=1, source_target_pairs={{0,1},{1,0},{2,3},{3,2},{4,5},{5,4},{6,7},{7,6},{8,9},{9,8},{10,11... | collective-permute-start | bytes 98312 | tf_op jit(solution)/shard_map/ppermute | solution.py:389
  20.6 6.2 %collective-permute-start.9 = (bf16[128,128]{1,0:T(8,128)(2,1)S(1)}, bf16[128,128]{1,0:T(8,128)(2,1)S(1)}, u32[]{:S(2)}, u32[]{:S(2)}) collective-permute-start(bf16[128,128]{1,0:T(8,128)(2,1)S(1)} %fold_back.1.order_ref), channel_id=1, source_target_pairs={{0,4},{1,5},{2,6},{3,7},{4,2},{5,3},{6,0},{7,1},{8,12},{9,13},{10,... | collective-permute-start | bytes 98312 | tf_op jit(solution)/shard_map/ppermute | solution.py:389
  21.6 5.2 %collective-permute-start.8 = (bf16[128,128]{1,0:T(8,128)(2,1)S(1)}, bf16[128,128]{1,0:T(8,128)(2,1)S(1)}, u32[]{:S(2)}, u32[]{:S(2)}) collective-permute-start(bf16[128,128]{1,0:T(8,128)(2,1)S(1)} %fold_back.1.order_ref), channel_id=1, source_target_pairs={{0,4},{1,5},{2,6},{3,7},{4,0},{5,1},{6,2},{7,3},{8,12},{9,13},{10,... | collective-permute-start | bytes 98312 | tf_op jit(solution)/shard_map/ppermute | solution.py:389
  22.4 4.7 %collective-permute-start.7 = (bf16[128,128]{1,0:T(8,128)(2,1)S(1)}, bf16[128,128]{1,0:T(8,128)(2,1)S(1)}, u32[]{:S(2)}, u32[]{:S(2)}) collective-permute-start(bf16[128,128]{1,0:T(8,128)(2,1)S(1)} %fold_back.1.order_ref), channel_id=1, source_target_pairs={{0,2},{1,3},{2,0},{3,1},{4,6},{5,7},{6,4},{7,5},{8,10},{9,11},{10,... | collective-permute-start | bytes 98312 | tf_op jit(solution)/shard_map/ppermute | solution.py:389

commit v6 on v5

--- a/solution.py
+++ b/solution.py
@@ -106,9 +106,9 @@
     copies[1].wait()
     copies[2].wait()
     state = jnp.zeros((C, C), F32)
-    for r, weight in enumerate(weights):
-        kw = flipped(chunk(k_ref, r)) * weight
-        state = state + mm(kw.astype(BF16), chunk(v_ref, r))
+    for r in range(0, len(weights), 2):
+        kw = [(flipped(chunk(k_ref, i)) * weights[i]).astype(BF16) for i in (r, r + 1)]
+        state = state + mm(jnp.concatenate(kw, axis=1), v_ref[r * C : (r + 2) * C, :])
     out_ref[:C, :] = state.astype(BF16)
     out_ref[C:, :] = log_rows(sum(tot))
     for copy in copies[3:]:
@@ -318,16 +318,16 @@
         taken += radix - 1
     future = future.astype(BF16)
     copies = []
-    for r in range(n):
-        tail = chunk(tail_ref, r)
-        dk = chunk(dk_ref, r) + tail * mm_nt(chunk(v_ref, r), future)
-        out_k_ref[r * C : (r + 1) * C, :] = dk.astype(BF16)
-        dv = chunk(dv_ref, r) + tail * mm(chunk(k_ref, r), future)
-        out_v_ref[r * C : (r + 1) * C, :] = dv.astype(BF16)
-        if (r + 1) % (n // 2) == 0:
-            rows = pl.ds((r + 1 - n // 2) * C, n // 2 * C)
+    step = 2 * C
+    for r in range(n // 2):
+        rows = slice(r * step, (r + 1) * step)
+        tail = tail_ref[rows, :]
+        out_k_ref[rows, :] = (dk_ref[rows, :] + tail * mm_nt(v_ref[rows, :], future)).astype(BF16)
+        out_v_ref[rows, :] = (dv_ref[rows, :] + tail * mm(k_ref[rows, :], future)).astype(BF16)
+        if (r + 1) % (n // 4) == 0:
+            part = pl.ds((r + 1 - n // 4) * step, n // 4 * step)
             for source, target in ((out_k_ref, k_hbm), (out_v_ref, v_hbm)):
-                copies.append(pltpu.make_async_copy(source.at[rows], target.at[rows], sems.at[len(copies)]))
+                copies.append(pltpu.make_async_copy(source.at[part], target.at[part], sems.at[len(copies)]))
                 copies[-1].start()
     for copy in copies:
         copy.wait()

time: 28.3 us -> 28.3 us (level)
  no operation moved by 1% of the time
where the time goes in v6:
time: 28.3 us; the launch traced here: 28.1 us
  starting transfers between devices  16.6 us (59%)
  Pallas kernels  8.8 us (31%)
  waiting for transfers between devices  1.88 us (7%)
  between operations  0.77 us (3%)
    ppermute x10, starting transfers between devices, send(): return lax.ppermute(x, axis, pairs)  16.6 us
    ppermute x10, waiting for transfers between devices, send(): return lax.ppermute(x, axis, pairs)  1.88 us
    pallas_call x1, Pallas kernels, local(): call(functools.partial(queries_kernel, levels, count, columns, dp // 2),...  1.74 us
    pallas_call x1, Pallas kernels, local(): call(keys_kernel, (wide, wide, wide), 'keys')  1.71 us
    pallas_call x1, Pallas kernels, local(): call(forward_kernel, (wide, wide, shape((5 * n, C), F32), shape((C, token...  1.7 us
    pallas_call x1, Pallas kernels, local(): call(functools.partial(state_kernel, columns), (payload, shape((lines, gr...  1.44 us
    pallas_call x1, Pallas kernels, local(): call(functools.partial(last_kernel, levels), (narrow, narrow), 'last', sc...  1.05 us
    pallas_call x1, Pallas kernels, local(): call(functools.partial(norm_kernel, levels), (narrow, wide, square, shape...  0.72 us
  transfers between devices with their start and end apart: 10, of which 4 were waited for; matrix products, arithmetic and copies ran while one was open for 0% of the time, Pallas kernels for 22%

profile of v6, /device:TPU:0, one launch (start us, length us, event | category | flops | bytes accessed | tf_op | source)
XLA Modules:
  0.0 28.1 jit_solution(816122149330735161)
XLA Ops:
  0.6 0.0 copy-start.3
  0.6 1.4 %state.1 = (bf16[144,128]{1,0:T(8,128)(2,1)S(1)}, bf16[32,3072]{1,0:T(8,128)(2,1)S(1)}) custom-call(bf16[1024,128]{1,0:T(8,128)(2,1)} %bitcast.10, bf16[1024,128]{1,0:T(8,128)(2,1)} %bitcast.16, f32[8,128]{1,0:T(8,128)} %bitcast.29, bf16[32,6144]{1,0:T(8,128)(2,1)} %bitcast.25), custom_call_target="tpu_custom_call" | custom-call | bytes 1024 | tf_op jit(solution)/shard_map/state/pallas_call | solution.py:410
  2.1 0.5 %collective-permute-start.1 = (bf16[32,3072]{1,0:T(8,128)(2,1)S(1)}, bf16[32,3072]{1,0:T(8,128)(2,1)S(1)}, u32[]{:S(2)}, u32[]{:S(2)}) collective-permute-start(bf16[32,3072]{1,0:T(8,128)(2,1)S(1)} %get-tuple-element.32), channel_id=1, source_target_pairs={{0,8},{8,0},{16,24},{24,16},{1,9},{9,1},{17,25},{25,17},{2,10},{10... | collective-permute-start | bytes 589832 | tf_op jit(solution)/shard_map/ppermute | solution.py:389
  2.6 2.6 %collective-permute-start = (bf16[144,128]{1,0:T(8,128)(2,1)S(1)}, bf16[144,128]{1,0:T(8,128)(2,1)S(1)}, u32[]{:S(2)}, u32[]{:S(2)}) collective-permute-start(bf16[144,128]{1,0:T(8,128)(2,1)S(1)} %get-tuple-element.31.own_ref.refs_0_.refs_3_), channel_id=1, source_target_pairs={{0,1},{1,0},{2,3},{3,2},{4,5},{5,4},{6,7},{7,6},{8,9},{9,8},{10,11... | collective-permute-start | bytes 110600 | tf_op jit(solution)/shard_map/ppermute | solution.py:389
  5.2 0.0 collective-permute-done.1.came_ref
  5.2 0.0 copy-done.3
  5.2 0.0 copy-start.1
  5.2 0.0 copy-start.2
  5.2 0.0 copy-start.4
  5.2 0.1 add.1
  5.3 0.0 copy-start
  5.3 1.6 %collective-permute-start.5 = (bf16[32,1536]{1,0:T(8,128)(2,1)S(1)}, bf16[32,1536]{1,0:T(8,128)(2,1)S(1)}, u32[]{:S(2)}, u32[]{:S(2)}) collective-permute-start(bf16[32,1536]{1,0:T(8,128)(2,1)S(1)} %get-tuple-element.46), channel_id=1, source_target_pairs={{0,16},{8,24},{16,0},{24,8},{1,17},{9,25},{17,1},{25,9},{2,18},{10... | collective-permute-start | bytes 294920 | tf_op jit(solution)/shard_map/ppermute | solution.py:389
  6.9 0.4 %collective-permute-done.refs_0_.refs_2_.refs_5_ = bf16[144,128]{1,0:T(8,128)(2,1)S(1)} collective-permute-done((bf16[144,128]{1,0:T(8,128)(2,1)S(1)}, bf16[144,128]{1,0:T(8,128)(2,1)S(1)}, u32[]{:S(2)}, u32[]{:S(2)}) %collective-permute-start) | collective-permute-done | bytes 36896 | tf_op jit(solution)/shard_map/ppermute | solution.py:389
  7.2 0.0 copy-start.5
  7.3 2.0 %collective-permute-start.4 = (bf16[144,128]{1,0:T(8,128)(2,1)S(1)}, bf16[144,128]{1,0:T(8,128)(2,1)S(1)}, u32[]{:S(2)}, u32[]{:S(2)}) collective-permute-start(bf16[144,128]{1,0:T(8,128)(2,1)S(1)} %fold.1.order_ref.refs_1_.refs_4_), channel_id=1, source_target_pairs={{0,2},{1,3},{2,4},{3,5},{4,6},{5,7},{6,0},{7,1},{8,10},{9,11},{10,... | collective-permute-start | bytes 110600 | tf_op jit(solution)/shard_map/ppermute | solution.py:389
  9.3 2.6 %collective-permute-start.3 = (bf16[144,128]{1,0:T(8,128)(2,1)S(1)}, bf16[144,128]{1,0:T(8,128)(2,1)S(1)}, u32[]{:S(2)}, u32[]{:S(2)}) collective-permute-start(bf16[144,128]{1,0:T(8,128)(2,1)S(1)} %fold.1.order_ref.refs_1_.refs_4_), channel_id=1, source_target_pairs={{0,4},{1,5},{2,6},{3,7},{4,0},{5,1},{6,2},{7,3},{8,12},{9,13},{10,... | collective-permute-start | bytes 110600 | tf_op jit(solution)/shard_map/ppermute | solution.py:389
  11.9 1.3 %collective-permute-start.2 = (bf16[144,128]{1,0:T(8,128)(2,1)S(1)}, bf16[144,128]{1,0:T(8,128)(2,1)S(1)}, u32[]{:S(2)}, u32[]{:S(2)}) collective-permute-start(bf16[144,128]{1,0:T(8,128)(2,1)S(1)} %fold.1.order_ref.refs_1_.refs_4_), channel_id=1, source_target_pairs={{0,6},{1,7},{2,0},{3,1},{4,2},{5,3},{6,4},{7,5},{8,14},{9,15},{10,... | collective-permute-start | bytes 110600 | tf_op jit(solution)/shard_map/ppermute | solution.py:389
  13.2 0.0 copy-done.1
  13.2 0.0 copy-done.2
  13.2 0.0 copy-done.4
  13.2 0.0 copy-done
  13.2 0.0 copy-done.5
  13.3 1.7 %forward.1 = (f32[1024,128]{1,0:T(8,128)S(1)}, f32[1024,128]{1,0:T(8,128)S(1)}, f32[40,128]{1,0:T(8,128)S(1)}, bf16[128,1024]{1,0:T(8,128)(2,1)S(1)}, f32[1024,1...) custom-call(bf16[1024,128]{1,0:T(8,128)(2,1)S(1)} %bitcast.21, bf16[1024,128]{1,0:T(8,128)(2,1)S(1)} %bitcast.11, ...), custom_call_target="tpu_custom_call" | custom-call | bytes 1024 | tf_op jit(solution)/shard_map/forward/pallas_call | solution.py:433
  15.0 0.3 %turned.1 = (bf16[1024,256]{1,0:T(8,128)(2,1)S(1)}, f32[1024,128]{1,0:T(8,128)S(1)}) custom-call(bf16[1024,128]{1,0:T(8,128)(2,1)S(1)} %bitcast.22, bf16[1024,128]{1,0:T(8,128)(2,1)S(1)} %bitcast.12, f32[1024,128]{1,0:T(8,128)S(1)} %get-tuple-element.34.downs_ref, f32[40,128]{1,0:T(8,128)S(1)} %get-tuple-element.35.rows_ref, ...), custom_call_target="tpu_custom_call" | custom-call | bytes 1024 | tf_op jit(solution)/shard_map/turned/pallas_call | solution.py:436
  15.3 0.0 collective-permute-done.4.refs_5_.refs_8_
  15.3 0.0 collective-permute-done.3.refs_4_.refs_7_
  15.3 0.5 %collective-permute-done.2.refs_3_.refs_6_ = bf16[144,128]{1,0:T(8,128)(2,1)S(1)} collective-permute-done((bf16[144,128]{1,0:T(8,128)(2,1)S(1)}, bf16[144,128]{1,0:T(8,128)(2,1)S(1)}, u32[]{:S(2)}, u32[]{:S(2)}) %collective-permute-start.2) | collective-permute-done | bytes 36896 | tf_op jit(solution)/shard_map/ppermute | solution.py:389
  15.8 0.7 %norm.1 = (bf16[1024,128]{1,0:T(8,128)(2,1)S(1)}, f32[1024,128]{1,0:T(8,128)S(1)}, f32[128,128]{1,0:T(8,128)S(1)}, bf16[128,128]{1,0:T(8,128)(2,1)S(1)}) custom-call(f32[1024,128]{1,0:T(8,128)S(1)} %get-tuple-element.38.local_ref, bf16[1024,128]{1,0:T(8,128)(2,1)S(1)} %bitcast.23, bf16[128,1024]{1,0:T(8,128)(2,1)S(1)} %get-tuple-element.39.qt_ref, ...), custom_call_target="tpu_custom_call" | custom-call | bytes 1024 | tf_op jit(solution)/shard_map/norm/pallas_call | solution.py:439
  16.6 1.6 %collective-permute-start.6 = (bf16[128,128]{1,0:T(8,128)(2,1)S(1)}, bf16[128,128]{1,0:T(8,128)(2,1)S(1)}, u32[]{:S(2)}, u32[]{:S(2)}) collective-permute-start(bf16[128,128]{1,0:T(8,128)(2,1)S(1)} %get-tuple-element.44.order_ref.own_ref), channel_id=1, source_target_pairs={{0,1},{1,0},{2,3},{3,2},{4,5},{5,4},{6,7},{7,6},{8,9},{9,8},{10,11... | collective-permute-start | bytes 98312 | tf_op jit(solution)/shard_map/ppermute | solution.py:389
  18.1 0.0 collective-permute-done.5.refs_2_
  18.1 1.7 %queries.1 = (bf16[1024,128]{1,0:T(8,128)(2,1)}, bf16[1024,128]{1,0:T(8,128)(2,1)}, f32[32,1536]{1,0:T(8,128)}, f32[16,128]{1,0:T(8,128)S(1)}) custom-call(bf16[1024,128]{1,0:T(8,128)(2,1)S(1)} %bitcast.13, bf16[1024,128]{1,0:T(8,128)(2,1)S(1)} %bitcast.18, f32[1024,128]{1,0:T(8,128)S(1)} %get-tuple-element.34.downs_ref, ...), custom_call_target="tpu_custom_call" | custom-call | bytes 1024 | tf_op jit(solution)/shard_map/queries/pallas_call | solution.py:443
  19.9 0.7 %collective-permute-done.6.refs_0_ = bf16[128,128]{1,0:T(8,128)(2,1)S(1)} collective-permute-done((bf16[128,128]{1,0:T(8,128)(2,1)S(1)}, bf16[128,128]{1,0:T(8,128)(2,1)S(1)}, u32[]{:S(2)}, u32[]{:S(2)}) %collective-permute-start.6) | collective-permute-done | bytes 32800 | tf_op jit(solution)/shard_map/ppermute | solution.py:389
  20.6 1.0 %collective-permute-start.9 = (bf16[128,128]{1,0:T(8,128)(2,1)S(1)}, bf16[128,128]{1,0:T(8,128)(2,1)S(1)}, u32[]{:S(2)}, u32[]{:S(2)}) collective-permute-start(bf16[128,128]{1,0:T(8,128)(2,1)S(1)} %fold_back.1.order_ref), channel_id=1, source_target_pairs={{0,4},{1,5},{2,6},{3,7},{4,2},{5,3},{6,0},{7,1},{8,12},{9,13},{10,... | collective-permute-start | bytes 98312 | tf_op jit(solution)/shard_map/ppermute | solution.py:389
  21.5 0.8 %collective-permute-start.8 = (bf16[128,128]{1,0:T(8,128)(2,1)S(1)}, bf16[128,128]{1,0:T(8,128)(2,1)S(1)}, u32[]{:S(2)}, u32[]{:S(2)}) collective-permute-start(bf16[128,128]{1,0:T(8,128)(2,1)S(1)} %fold_back.1.order_ref), channel_id=1, source_target_pairs={{0,4},{1,5},{2,6},{3,7},{4,0},{5,1},{6,2},{7,3},{8,12},{9,13},{10,... | collective-permute-start | bytes 98312 | tf_op jit(solution)/shard_map/ppermute | solution.py:389
  22.4 2.6 %collective-permute-start.7 = (bf16[128,128]{1,0:T(8,128)(2,1)S(1)}, bf16[128,128]{1,0:T(8,128)(2,1)S(1)}, u32[]{:S(2)}, u32[]{:S(2)}) collective-permute-start(bf16[128,128]{1,0:T(8,128)(2,1)S(1)} %fold_back.1.order_ref), channel_id=1, source_target_pairs={{0,2},{1,3},{2,0},{3,1},{4,6},{5,7},{6,4},{7,5},{8,10},{9,11},{10,... | collective-permute-start | bytes 98312 | tf_op jit(solution)/shard_map/ppermute | solution.py:389
  25.0 1.7 %keys.1 = (f32[1024,128]{1,0:T(8,128)S(1)}, f32[1024,128]{1,0:T(8,128)S(1)}, f32[1024,128]{1,0:T(8,128)S(1)}) custom-call(bf16[1024,128]{1,0:T(8,128)(2,1)S(1)} %bitcast.24, bf16[1024,128]{1,0:T(8,128)(2,1)S(1)} %bitcast.14, bf16[1024,128]{1,0:T(8,128)(2,1)S(1)} %bitcast.19, bf16[128,1024]{1,0:T(8,128)(2,1)S(1)} %get-tuple-element.39.qt_ref, ...), custom_call_target="tpu_custom_call" | custom-call | bytes 1024 | tf_op jit(solution)/shard_map/keys/pallas_call | solution.py:460
  26.7 0.0 collective-permute-done.9.refs_3_
  26.8 0.0 collective-permute-done.8.refs_2_
  26.8 0.3 %collective-permute-done.7.refs_1_ = bf16[128,128]{1,0:T(8,128)(2,1)S(1)} collective-permute-done((bf16[128,128]{1,0:T(8,128)(2,1)S(1)}, bf16[128,128]{1,0:T(8,128)(2,1)S(1)}, u32[]{:S(2)}, u32[]{:S(2)}) %collective-permute-start.7) | collective-permute-done | bytes 32800 | tf_op jit(solution)/shard_map/ppermute | solution.py:389
  27.1 1.0 %last.1 = (bf16[1024,128]{1,0:T(8,128)(2,1)}, bf16[1024,128]{1,0:T(8,128)(2,1)}) custom-call(f32[1024,128]{1,0:T(8,128)S(1)} %get-tuple-element.51.dk_ref, f32[1024,128]{1,0:T(8,128)S(1)} %get-tuple-element.52.dv_ref, bf16[1024,128]{1,0:T(8,128)(2,1)S(1)} %bitcast.15, bf16[1024,128]{1,0:T(8,128)(2,1)S(1)} %bitcast.20, ...), custom_call_target="tpu_custom_call" | custom-call | bytes 1024 | tf_op jit(solution)/shard_map/last/pallas_call | solution.py:461
  (2 shorter events, 0.0 us)
Async XLA Ops:
  0.6 4.5 %copy-start.3 = (bf16[1,32,6144]{2,1,0:T(8,128)(2,1)S(1)}, bf16[1,32,6144]{2,1,0:T(8,128)(2,1)}, u32[]{:S(2)}) copy-start(bf16[1,32,6144]{2,1,0:T(8,128)(2,1)} %param.11) | copy-start | bytes 1179652
  2.1 3.1 %collective-permute-start.1 = (bf16[32,3072]{1,0:T(8,128)(2,1)S(1)}, bf16[32,3072]{1,0:T(8,128)(2,1)S(1)}, u32[]{:S(2)}, u32[]{:S(2)}) collective-permute-start(bf16[32,3072]{1,0:T(8,128)(2,1)S(1)} %get-tuple-element.32), channel_id=1, source_target_pairs={{0,8},{8,0},{16,24},{24,16},{1,9},{9,1},{17,25},{25,17},{2,10},{10... | collective-permute-start | bytes 589832 | tf_op jit(solution)/shard_map/ppermute | solution.py:389
  2.6 4.6 %collective-permute-start = (bf16[144,128]{1,0:T(8,128)(2,1)S(1)}, bf16[144,128]{1,0:T(8,128)(2,1)S(1)}, u32[]{:S(2)}, u32[]{:S(2)}) collective-permute-start(bf16[144,128]{1,0:T(8,128)(2,1)S(1)} %get-tuple-element.31.own_ref.refs_0_.refs_3_), channel_id=1, source_target_pairs={{0,1},{1,0},{2,3},{3,2},{4,5},{5,4},{6,7},{7,6},{8,9},{9,8},{10,11... | collective-permute-start | bytes 110600 | tf_op jit(solution)/shard_map/ppermute | solution.py:389
  5.2 8.1 %copy-start.1 = (bf16[1,1024,128]{2,1,0:T(8,128)(2,1)S(1)}, bf16[1,1024,128]{2,1,0:T(8,128)(2,1)}, u32[]{:S(2)}) copy-start(bf16[1,1024,128]{2,1,0:T(8,128)(2,1)} %param.8) | copy-start | bytes 786436
  5.2 8.1 %copy-start.2 = (bf16[1,1024,128]{2,1,0:T(8,128)(2,1)S(1)}, bf16[1,1024,128]{2,1,0:T(8,128)(2,1)}, u32[]{:S(2)}) copy-start(bf16[1,1024,128]{2,1,0:T(8,128)(2,1)} %param.6) | copy-start | bytes 786436
  5.2 8.1 %copy-start.4 = (bf16[1,1024,128]{2,1,0:T(8,128)(2,1)S(1)}, bf16[1,1024,128]{2,1,0:T(8,128)(2,1)}, u32[]{:S(2)}) copy-start(bf16[1,1024,128]{2,1,0:T(8,128)(2,1)} %param.9) | copy-start | bytes 786436
  5.3 8.0 %copy-start = (bf16[1,1024,128]{2,1,0:T(8,128)(2,1)S(1)}, bf16[1,1024,128]{2,1,0:T(8,128)(2,1)}, u32[]{:S(2)}) copy-start(bf16[1,1024,128]{2,1,0:T(8,128)(2,1)} %param.7) | copy-start | bytes 786436
  5.3 12.9 %collective-permute-start.5 = (bf16[32,1536]{1,0:T(8,128)(2,1)S(1)}, bf16[32,1536]{1,0:T(8,128)(2,1)S(1)}, u32[]{:S(2)}, u32[]{:S(2)}) collective-permute-start(bf16[32,1536]{1,0:T(8,128)(2,1)S(1)} %get-tuple-element.46), channel_id=1, source_target_pairs={{0,16},{8,24},{16,0},{24,8},{1,17},{9,25},{17,1},{25,9},{2,18},{10... | collective-permute-start | bytes 294920 | tf_op jit(solution)/shard_map/ppermute | solution.py:389
  7.2 6.0 %copy-start.5 = (f32[1,1,1024]{2,1,0:T(1,128)S(1)}, f32[1,1,1024]{2,1,0:T(1,128)}, u32[]{:S(2)}) copy-start(f32[1,1,1024]{2,1,0:T(1,128)} %param.10) | copy-start | bytes 12292
  7.3 8.0 %collective-permute-start.4 = (bf16[144,128]{1,0:T(8,128)(2,1)S(1)}, bf16[144,128]{1,0:T(8,128)(2,1)S(1)}, u32[]{:S(2)}, u32[]{:S(2)}) collective-permute-start(bf16[144,128]{1,0:T(8,128)(2,1)S(1)} %fold.1.order_ref.refs_1_.refs_4_), channel_id=1, source_target_pairs={{0,2},{1,3},{2,4},{3,5},{4,6},{5,7},{6,0},{7,1},{8,10},{9,11},{10,... | collective-permute-start | bytes 110600 | tf_op jit(solution)/shard_map/ppermute | solution.py:389
  9.3 6.0 %collective-permute-start.3 = (bf16[144,128]{1,0:T(8,128)(2,1)S(1)}, bf16[144,128]{1,0:T(8,128)(2,1)S(1)}, u32[]{:S(2)}, u32[]{:S(2)}) collective-permute-start(bf16[144,128]{1,0:T(8,128)(2,1)S(1)} %fold.1.order_ref.refs_1_.refs_4_), channel_id=1, source_target_pairs={{0,4},{1,5},{2,6},{3,7},{4,0},{5,1},{6,2},{7,3},{8,12},{9,13},{10,... | collective-permute-start | bytes 110600 | tf_op jit(solution)/shard_map/ppermute | solution.py:389
  11.9 4.0 %collective-permute-start.2 = (bf16[144,128]{1,0:T(8,128)(2,1)S(1)}, bf16[144,128]{1,0:T(8,128)(2,1)S(1)}, u32[]{:S(2)}, u32[]{:S(2)}) collective-permute-start(bf16[144,128]{1,0:T(8,128)(2,1)S(1)} %fold.1.order_ref.refs_1_.refs_4_), channel_id=1, source_target_pairs={{0,6},{1,7},{2,0},{3,1},{4,2},{5,3},{6,4},{7,5},{8,14},{9,15},{10,... | collective-permute-start | bytes 110600 | tf_op jit(solution)/shard_map/ppermute | solution.py:389
  16.6 4.0 %collective-permute-start.6 = (bf16[128,128]{1,0:T(8,128)(2,1)S(1)}, bf16[128,128]{1,0:T(8,128)(2,1)S(1)}, u32[]{:S(2)}, u32[]{:S(2)}) collective-permute-start(bf16[128,128]{1,0:T(8,128)(2,1)S(1)} %get-tuple-element.44.order_ref.own_ref), channel_id=1, source_target_pairs={{0,1},{1,0},{2,3},{3,2},{4,5},{5,4},{6,7},{7,6},{8,9},{9,8},{10,11... | collective-permute-start | bytes 98312 | tf_op jit(solution)/shard_map/ppermute | solution.py:389
  20.6 6.2 %collective-permute-start.9 = (bf16[128,128]{1,0:T(8,128)(2,1)S(1)}, bf16[128,128]{1,0:T(8,128)(2,1)S(1)}, u32[]{:S(2)}, u32[]{:S(2)}) collective-permute-start(bf16[128,128]{1,0:T(8,128)(2,1)S(1)} %fold_back.1.order_ref), channel_id=1, source_target_pairs={{0,4},{1,5},{2,6},{3,7},{4,2},{5,3},{6,0},{7,1},{8,12},{9,13},{10,... | collective-permute-start | bytes 98312 | tf_op jit(solution)/shard_map/ppermute | solution.py:389
  21.5 5.2 %collective-permute-start.8 = (bf16[128,128]{1,0:T(8,128)(2,1)S(1)}, bf16[128,128]{1,0:T(8,128)(2,1)S(1)}, u32[]{:S(2)}, u32[]{:S(2)}) collective-permute-start(bf16[128,128]{1,0:T(8,128)(2,1)S(1)} %fold_back.1.order_ref), channel_id=1, source_target_pairs={{0,4},{1,5},{2,6},{3,7},{4,0},{5,1},{6,2},{7,3},{8,12},{9,13},{10,... | collective-permute-start | bytes 98312 | tf_op jit(solution)/shard_map/ppermute | solution.py:389
  22.4 4.7 %collective-permute-start.7 = (bf16[128,128]{1,0:T(8,128)(2,1)S(1)}, bf16[128,128]{1,0:T(8,128)(2,1)S(1)}, u32[]{:S(2)}, u32[]{:S(2)}) collective-permute-start(bf16[128,128]{1,0:T(8,128)(2,1)S(1)} %fold_back.1.order_ref), channel_id=1, source_target_pairs={{0,2},{1,3},{2,0},{3,1},{4,6},{5,7},{6,4},{7,5},{8,10},{9,11},{10,... | collective-permute-start | bytes 98312 | tf_op jit(solution)/shard_map/ppermute | solution.py:389

commit v7 on v6

--- a/solution.py
+++ b/solution.py
@@ -280,7 +280,7 @@
 
 
 def keys_kernel(
-    q_ref, k_ref, v_ref, qt_ref, downs_ref, rows_ref, scores_ref, upper_ref, dattn_ref, order_ref, dk_ref, dv_ref, tail_ref
+    q_ref, k_ref, v_ref, qt_ref, downs_ref, rows_ref, scores_ref, upper_ref, dattn_ref, order_ref, dk_ref, dv_ref, kt_ref, vt_ref
 ):
     n = rows_ref.shape[0] // 5
     future = jnp.zeros((C, C), F32)
@@ -290,7 +290,9 @@
         pair = parts(dattn, 1)
         down = chunk(downs_ref, r)
         left = jnp.minimum(rows_ref[3 * n + r : 3 * n + r + 1, :] - down, 0.0)
-        tail_ref[r * C : (r + 1) * C, :] = jnp.exp(left + rows_ref[4 * n + r : 4 * n + r + 1, :])
+        whole_tail = jnp.exp(left + rows_ref[4 * n + r : 4 * n + r + 1, :])
+        kt_ref[r * C : (r + 1) * C, :] = (whole_tail * k.astype(F32)).astype(BF16)
+        vt_ref[r * C : (r + 1) * C, :] = (whole_tail * v.astype(F32)).astype(BF16)
         dscores_t = mm_nt(twice(v, 1), pair) * chunk(upper_ref, r)
         scores = chunk(scores_ref, r)
         dk = mm(parts(dscores_t, 1), twice(chunk(q_ref, r), 0))
@@ -306,7 +308,7 @@
             future = rows_ref[n + r : n + r + 1, :] * future + both[:, :C] + both[:, C:]
 
 
-def last_kernel(levels, dk_ref, dv_ref, k_ref, v_ref, tail_ref, weights_ref, *refs):
+def last_kernel(levels, dk_ref, dv_ref, kt_ref, vt_ref, weights_ref, *refs):
     received, (k_hbm, v_hbm, out_k_ref, out_v_ref, sems) = refs[:-5], refs[-5:]
     n = dk_ref.shape[0] // C
     future = jnp.zeros((C, C), F32)
@@ -321,9 +323,8 @@
     step = 2 * C
     for r in range(n // 2):
         rows = slice(r * step, (r + 1) * step)
-        tail = tail_ref[rows, :]
-        out_k_ref[rows, :] = (dk_ref[rows, :] + tail * mm_nt(v_ref[rows, :], future)).astype(BF16)
-        out_v_ref[rows, :] = (dv_ref[rows, :] + tail * mm(k_ref[rows, :], future)).astype(BF16)
+        out_k_ref[rows, :] = (dk_ref[rows, :] + mm_nt(vt_ref[rows, :], future)).astype(BF16)
+        out_v_ref[rows, :] = (dv_ref[rows, :] + mm(kt_ref[rows, :], future)).astype(BF16)
         if (r + 1) % (n // 4) == 0:
             part = pl.ds((r + 1 - n // 4) * step, n // 4 * step)
             for source, target in ((out_k_ref, k_hbm), (out_v_ref, v_hbm)):
@@ -457,15 +458,15 @@
             fold = functools.partial(fold_back_kernel, at + radix - 1, radix)
             state = call(fold, shape((C, C), BF16), "fold_back")(state, *got, weights)
         at += 2 * radix - 1
-    dk, dv, tail = call(keys_kernel, (wide, wide, wide), "keys")(q, k, v, qt, downs, rows, scores_t, upper, dattn, state)
+    dk, dv, kt, vt = call(keys_kernel, (wide, wide, narrow, narrow), "keys")(q, k, v, qt, downs, rows, scores_t, upper, dattn, state)
     grad_key, grad_value = call(
         functools.partial(last_kernel, levels),
         (narrow, narrow),
         "last",
         scratch=[whole, whole, dma((4,))],
-        in_specs=[here] * (6 + len(received)),
+        in_specs=[here] * (5 + len(received)),
         out_specs=(away, away),
-    )(dk, dv, k, v, tail, weights, *received)
+    )(dk, dv, kt, vt, weights, *received)
     return attn_out[None], grad_query[None], grad_key[None], grad_value[None], grad_shard
 
 

time: 28.3 us -> 28.2 us (level)
  no operation moved by 1% of the time
where the time goes in v7:
time: 28.2 us; the launch traced here: 28.1 us
  starting transfers between devices  16.6 us (59%)
  Pallas kernels  8.8 us (31%)
  waiting for transfers between devices  1.87 us (7%)
  between operations  0.77 us (3%)
    ppermute x10, starting transfers between devices, send(): return lax.ppermute(x, axis, pairs)  16.6 us
    ppermute x10, waiting for transfers between devices, send(): return lax.ppermute(x, axis, pairs)  1.87 us
    pallas_call x1, Pallas kernels, local(): call(functools.partial(queries_kernel, levels, count, columns, dp // 2),...  1.74 us
    pallas_call x1, Pallas kernels, local(): call(keys_kernel, (wide, wide, narrow, narrow), 'keys')  1.72 us
    pallas_call x1, Pallas kernels, local(): call(forward_kernel, (wide, wide, shape((5 * n, C), F32), shape((C, token...  1.7 us
    pallas_call x1, Pallas kernels, local(): call(functools.partial(state_kernel, columns), (payload, shape((lines, gr...  1.44 us
    pallas_call x1, Pallas kernels, local(): call(functools.partial(last_kernel, levels), (narrow, narrow), 'last', sc...  1.04 us
    pallas_call x1, Pallas kernels, local(): call(functools.partial(norm_kernel, levels), (narrow, wide, square, shape...  0.72 us
  transfers between devices with their start and end apart: 10, of which 4 were waited for; matrix products, arithmetic and copies ran while one was open for 0% of the time, Pallas kernels for 22%

profile of v7, /device:TPU:0, one launch (start us, length us, event | category | flops | bytes accessed | tf_op | source)
XLA Modules:
  0.0 28.1 jit_solution(1564491532334825823)
XLA Ops:
  0.6 0.0 copy-start.3
  0.6 1.4 %state.1 = (bf16[144,128]{1,0:T(8,128)(2,1)S(1)}, bf16[32,3072]{1,0:T(8,128)(2,1)S(1)}) custom-call(bf16[1024,128]{1,0:T(8,128)(2,1)} %bitcast.10, bf16[1024,128]{1,0:T(8,128)(2,1)} %bitcast.15, f32[8,128]{1,0:T(8,128)} %bitcast.27, bf16[32,6144]{1,0:T(8,128)(2,1)} %bitcast.23), custom_call_target="tpu_custom_call" | custom-call | bytes 1024 | tf_op jit(solution)/shard_map/state/pallas_call | solution.py:411
  2.1 0.5 %collective-permute-start.1 = (bf16[32,3072]{1,0:T(8,128)(2,1)S(1)}, bf16[32,3072]{1,0:T(8,128)(2,1)S(1)}, u32[]{:S(2)}, u32[]{:S(2)}) collective-permute-start(bf16[32,3072]{1,0:T(8,128)(2,1)S(1)} %get-tuple-element.33), channel_id=1, source_target_pairs={{0,8},{8,0},{16,24},{24,16},{1,9},{9,1},{17,25},{25,17},{2,10},{10... | collective-permute-start | bytes 589832 | tf_op jit(solution)/shard_map/ppermute | solution.py:390
  2.6 2.6 %collective-permute-start = (bf16[144,128]{1,0:T(8,128)(2,1)S(1)}, bf16[144,128]{1,0:T(8,128)(2,1)S(1)}, u32[]{:S(2)}, u32[]{:S(2)}) collective-permute-start(bf16[144,128]{1,0:T(8,128)(2,1)S(1)} %get-tuple-element.32.own_ref.refs_0_.refs_3_), channel_id=1, source_target_pairs={{0,1},{1,0},{2,3},{3,2},{4,5},{5,4},{6,7},{7,6},{8,9},{9,8},{10,11... | collective-permute-start | bytes 110600 | tf_op jit(solution)/shard_map/ppermute | solution.py:390
  5.2 0.0 collective-permute-done.1.came_ref
  5.2 0.0 copy-done.3
  5.2 0.0 copy-start.1
  5.2 0.0 copy-start.2
  5.2 0.0 copy-start.4
  5.2 0.1 add.1
  5.3 0.0 copy-start
  5.3 1.6 %collective-permute-start.5 = (bf16[32,1536]{1,0:T(8,128)(2,1)S(1)}, bf16[32,1536]{1,0:T(8,128)(2,1)S(1)}, u32[]{:S(2)}, u32[]{:S(2)}) collective-permute-start(bf16[32,1536]{1,0:T(8,128)(2,1)S(1)} %get-tuple-element.47), channel_id=1, source_target_pairs={{0,16},{8,24},{16,0},{24,8},{1,17},{9,25},{17,1},{25,9},{2,18},{10... | collective-permute-start | bytes 294920 | tf_op jit(solution)/shard_map/ppermute | solution.py:390
  6.9 0.4 %collective-permute-done.refs_0_.refs_2_.refs_5_ = bf16[144,128]{1,0:T(8,128)(2,1)S(1)} collective-permute-done((bf16[144,128]{1,0:T(8,128)(2,1)S(1)}, bf16[144,128]{1,0:T(8,128)(2,1)S(1)}, u32[]{:S(2)}, u32[]{:S(2)}) %collective-permute-start) | collective-permute-done | bytes 36896 | tf_op jit(solution)/shard_map/ppermute | solution.py:390
  7.2 0.0 copy-start.5
  7.3 2.0 %collective-permute-start.4 = (bf16[144,128]{1,0:T(8,128)(2,1)S(1)}, bf16[144,128]{1,0:T(8,128)(2,1)S(1)}, u32[]{:S(2)}, u32[]{:S(2)}) collective-permute-start(bf16[144,128]{1,0:T(8,128)(2,1)S(1)} %fold.1.order_ref.refs_1_.refs_4_), channel_id=1, source_target_pairs={{0,2},{1,3},{2,4},{3,5},{4,6},{5,7},{6,0},{7,1},{8,10},{9,11},{10,... | collective-permute-start | bytes 110600 | tf_op jit(solution)/shard_map/ppermute | solution.py:390
  9.3 2.6 %collective-permute-start.3 = (bf16[144,128]{1,0:T(8,128)(2,1)S(1)}, bf16[144,128]{1,0:T(8,128)(2,1)S(1)}, u32[]{:S(2)}, u32[]{:S(2)}) collective-permute-start(bf16[144,128]{1,0:T(8,128)(2,1)S(1)} %fold.1.order_ref.refs_1_.refs_4_), channel_id=1, source_target_pairs={{0,4},{1,5},{2,6},{3,7},{4,0},{5,1},{6,2},{7,3},{8,12},{9,13},{10,... | collective-permute-start | bytes 110600 | tf_op jit(solution)/shard_map/ppermute | solution.py:390
  11.9 1.3 %collective-permute-start.2 = (bf16[144,128]{1,0:T(8,128)(2,1)S(1)}, bf16[144,128]{1,0:T(8,128)(2,1)S(1)}, u32[]{:S(2)}, u32[]{:S(2)}) collective-permute-start(bf16[144,128]{1,0:T(8,128)(2,1)S(1)} %fold.1.order_ref.refs_1_.refs_4_), channel_id=1, source_target_pairs={{0,6},{1,7},{2,0},{3,1},{4,2},{5,3},{6,4},{7,5},{8,14},{9,15},{10,... | collective-permute-start | bytes 110600 | tf_op jit(solution)/shard_map/ppermute | solution.py:390
  13.2 0.0 copy-done.1
  13.2 0.0 copy-done.2
  13.2 0.0 copy-done.4
  13.2 0.0 copy-done
  13.2 0.0 copy-done.5
  13.3 1.7 %forward.1 = (f32[1024,128]{1,0:T(8,128)S(1)}, f32[1024,128]{1,0:T(8,128)S(1)}, f32[40,128]{1,0:T(8,128)S(1)}, bf16[128,1024]{1,0:T(8,128)(2,1)S(1)}, f32[1024,1...) custom-call(bf16[1024,128]{1,0:T(8,128)(2,1)S(1)} %bitcast.19, bf16[1024,128]{1,0:T(8,128)(2,1)S(1)} %bitcast.11, ...), custom_call_target="tpu_custom_call" | custom-call | bytes 1024 | tf_op jit(solution)/shard_map/forward/pallas_call | solution.py:434
  15.0 0.3 %turned.1 = (bf16[1024,256]{1,0:T(8,128)(2,1)S(1)}, f32[1024,128]{1,0:T(8,128)S(1)}) custom-call(bf16[1024,128]{1,0:T(8,128)(2,1)S(1)} %bitcast.20, bf16[1024,128]{1,0:T(8,128)(2,1)S(1)} %bitcast.12, f32[1024,128]{1,0:T(8,128)S(1)} %get-tuple-element.35.downs_ref, f32[40,128]{1,0:T(8,128)S(1)} %get-tuple-element.36.rows_ref, ...), custom_call_target="tpu_custom_call" | custom-call | bytes 1024 | tf_op jit(solution)/shard_map/turned/pallas_call | solution.py:437
  15.3 0.0 collective-permute-done.4.refs_5_.refs_8_
  15.3 0.0 collective-permute-done.3.refs_4_.refs_7_
  15.3 0.5 %collective-permute-done.2.refs_3_.refs_6_ = bf16[144,128]{1,0:T(8,128)(2,1)S(1)} collective-permute-done((bf16[144,128]{1,0:T(8,128)(2,1)S(1)}, bf16[144,128]{1,0:T(8,128)(2,1)S(1)}, u32[]{:S(2)}, u32[]{:S(2)}) %collective-permute-start.2) | collective-permute-done | bytes 36896 | tf_op jit(solution)/shard_map/ppermute | solution.py:390
  15.8 0.7 %norm.1 = (bf16[1024,128]{1,0:T(8,128)(2,1)S(1)}, f32[1024,128]{1,0:T(8,128)S(1)}, f32[128,128]{1,0:T(8,128)S(1)}, bf16[128,128]{1,0:T(8,128)(2,1)S(1)}) custom-call(f32[1024,128]{1,0:T(8,128)S(1)} %get-tuple-element.39.local_ref, bf16[1024,128]{1,0:T(8,128)(2,1)S(1)} %bitcast.21, bf16[128,1024]{1,0:T(8,128)(2,1)S(1)} %get-tuple-element.40.qt_ref, ...), custom_call_target="tpu_custom_call" | custom-call | bytes 1024 | tf_op jit(solution)/shard_map/norm/pallas_call | solution.py:440
  16.6 1.6 %collective-permute-start.6 = (bf16[128,128]{1,0:T(8,128)(2,1)S(1)}, bf16[128,128]{1,0:T(8,128)(2,1)S(1)}, u32[]{:S(2)}, u32[]{:S(2)}) collective-permute-start(bf16[128,128]{1,0:T(8,128)(2,1)S(1)} %get-tuple-element.45.order_ref.own_ref), channel_id=1, source_target_pairs={{0,1},{1,0},{2,3},{3,2},{4,5},{5,4},{6,7},{7,6},{8,9},{9,8},{10,11... | collective-permute-start | bytes 98312 | tf_op jit(solution)/shard_map/ppermute | solution.py:390
  18.1 0.0 collective-permute-done.5.refs_2_
  18.1 1.7 %queries.1 = (bf16[1024,128]{1,0:T(8,128)(2,1)}, bf16[1024,128]{1,0:T(8,128)(2,1)}, f32[32,1536]{1,0:T(8,128)}, f32[16,128]{1,0:T(8,128)S(1)}) custom-call(bf16[1024,128]{1,0:T(8,128)(2,1)S(1)} %bitcast.13, bf16[1024,128]{1,0:T(8,128)(2,1)S(1)} %bitcast.17, f32[1024,128]{1,0:T(8,128)S(1)} %get-tuple-element.35.downs_ref, ...), custom_call_target="tpu_custom_call" | custom-call | bytes 1024 | tf_op jit(solution)/shard_map/queries/pallas_call | solution.py:444
  19.9 0.7 %collective-permute-done.6.refs_0_ = bf16[128,128]{1,0:T(8,128)(2,1)S(1)} collective-permute-done((bf16[128,128]{1,0:T(8,128)(2,1)S(1)}, bf16[128,128]{1,0:T(8,128)(2,1)S(1)}, u32[]{:S(2)}, u32[]{:S(2)}) %collective-permute-start.6) | collective-permute-done | bytes 32800 | tf_op jit(solution)/shard_map/ppermute | solution.py:390
  20.6 1.0 %collective-permute-start.9 = (bf16[128,128]{1,0:T(8,128)(2,1)S(1)}, bf16[128,128]{1,0:T(8,128)(2,1)S(1)}, u32[]{:S(2)}, u32[]{:S(2)}) collective-permute-start(bf16[128,128]{1,0:T(8,128)(2,1)S(1)} %fold_back.1.order_ref), channel_id=1, source_target_pairs={{0,4},{1,5},{2,6},{3,7},{4,2},{5,3},{6,0},{7,1},{8,12},{9,13},{10,... | collective-permute-start | bytes 98312 | tf_op jit(solution)/shard_map/ppermute | solution.py:390
  21.5 0.8 %collective-permute-start.8 = (bf16[128,128]{1,0:T(8,128)(2,1)S(1)}, bf16[128,128]{1,0:T(8,128)(2,1)S(1)}, u32[]{:S(2)}, u32[]{:S(2)}) collective-permute-start(bf16[128,128]{1,0:T(8,128)(2,1)S(1)} %fold_back.1.order_ref), channel_id=1, source_target_pairs={{0,4},{1,5},{2,6},{3,7},{4,0},{5,1},{6,2},{7,3},{8,12},{9,13},{10,... | collective-permute-start | bytes 98312 | tf_op jit(solution)/shard_map/ppermute | solution.py:390
  22.4 2.6 %collective-permute-start.7 = (bf16[128,128]{1,0:T(8,128)(2,1)S(1)}, bf16[128,128]{1,0:T(8,128)(2,1)S(1)}, u32[]{:S(2)}, u32[]{:S(2)}) collective-permute-start(bf16[128,128]{1,0:T(8,128)(2,1)S(1)} %fold_back.1.order_ref), channel_id=1, source_target_pairs={{0,2},{1,3},{2,0},{3,1},{4,6},{5,7},{6,4},{7,5},{8,10},{9,11},{10,... | collective-permute-start | bytes 98312 | tf_op jit(solution)/shard_map/ppermute | solution.py:390
  25.0 1.7 %keys.1 = (f32[1024,128]{1,0:T(8,128)S(1)}, f32[1024,128]{1,0:T(8,128)S(1)}, bf16[1024,128]{1,0:T(8,128)(2,1)S(1)}, bf16[1024,128]{1,0:T(8,128)(2,1)S(1)}) custom-call(bf16[1024,128]{1,0:T(8,128)(2,1)S(1)} %bitcast.22, bf16[1024,128]{1,0:T(8,128)(2,1)S(1)} %bitcast.14, bf16[1024,128]{1,0:T(8,128)(2,1)S(1)} %bitcast.18, ...), custom_call_target="tpu_custom_call" | custom-call | bytes 1024 | tf_op jit(solution)/shard_map/keys/pallas_call | solution.py:461
  26.7 0.0 collective-permute-done.9.refs_3_
  26.8 0.0 collective-permute-done.8.refs_2_
  26.8 0.3 %collective-permute-done.7.refs_1_ = bf16[128,128]{1,0:T(8,128)(2,1)S(1)} collective-permute-done((bf16[128,128]{1,0:T(8,128)(2,1)S(1)}, bf16[128,128]{1,0:T(8,128)(2,1)S(1)}, u32[]{:S(2)}, u32[]{:S(2)}) %collective-permute-start.7) | collective-permute-done | bytes 32800 | tf_op jit(solution)/shard_map/ppermute | solution.py:390
  27.1 1.0 %last.1 = (bf16[1024,128]{1,0:T(8,128)(2,1)}, bf16[1024,128]{1,0:T(8,128)(2,1)}) custom-call(f32[1024,128]{1,0:T(8,128)S(1)} %get-tuple-element.52.dk_ref, f32[1024,128]{1,0:T(8,128)S(1)} %get-tuple-element.53.dv_ref, bf16[1024,128]{1,0:T(8,128)(2,1)S(1)} %get-tuple-element.54.kt_ref, bf16[1024,128]{1,0:T(8,128)(2,1)S(1)} %get-tuple-element.55.vt_ref, ...), custom_call_target="tpu_custom_call" | custom-call | bytes 1024 | tf_op jit(solution)/shard_map/last/pallas_call | solution.py:462
  (2 shorter events, 0.0 us)
Async XLA Ops:
  0.6 4.5 %copy-start.3 = (bf16[1,32,6144]{2,1,0:T(8,128)(2,1)S(1)}, bf16[1,32,6144]{2,1,0:T(8,128)(2,1)}, u32[]{:S(2)}) copy-start(bf16[1,32,6144]{2,1,0:T(8,128)(2,1)} %param.11) | copy-start | bytes 1179652
  2.1 3.1 %collective-permute-start.1 = (bf16[32,3072]{1,0:T(8,128)(2,1)S(1)}, bf16[32,3072]{1,0:T(8,128)(2,1)S(1)}, u32[]{:S(2)}, u32[]{:S(2)}) collective-permute-start(bf16[32,3072]{1,0:T(8,128)(2,1)S(1)} %get-tuple-element.33), channel_id=1, source_target_pairs={{0,8},{8,0},{16,24},{24,16},{1,9},{9,1},{17,25},{25,17},{2,10},{10... | collective-permute-start | bytes 589832 | tf_op jit(solution)/shard_map/ppermute | solution.py:390
  2.6 4.6 %collective-permute-start = (bf16[144,128]{1,0:T(8,128)(2,1)S(1)}, bf16[144,128]{1,0:T(8,128)(2,1)S(1)}, u32[]{:S(2)}, u32[]{:S(2)}) collective-permute-start(bf16[144,128]{1,0:T(8,128)(2,1)S(1)} %get-tuple-element.32.own_ref.refs_0_.refs_3_), channel_id=1, source_target_pairs={{0,1},{1,0},{2,3},{3,2},{4,5},{5,4},{6,7},{7,6},{8,9},{9,8},{10,11... | collective-permute-start | bytes 110600 | tf_op jit(solution)/shard_map/ppermute | solution.py:390
  5.2 8.1 %copy-start.1 = (bf16[1,1024,128]{2,1,0:T(8,128)(2,1)S(1)}, bf16[1,1024,128]{2,1,0:T(8,128)(2,1)}, u32[]{:S(2)}) copy-start(bf16[1,1024,128]{2,1,0:T(8,128)(2,1)} %param.8) | copy-start | bytes 786436
  5.2 8.1 %copy-start.2 = (bf16[1,1024,128]{2,1,0:T(8,128)(2,1)S(1)}, bf16[1,1024,128]{2,1,0:T(8,128)(2,1)}, u32[]{:S(2)}) copy-start(bf16[1,1024,128]{2,1,0:T(8,128)(2,1)} %param.6) | copy-start | bytes 786436
  5.2 8.1 %copy-start.4 = (bf16[1,1024,128]{2,1,0:T(8,128)(2,1)S(1)}, bf16[1,1024,128]{2,1,0:T(8,128)(2,1)}, u32[]{:S(2)}) copy-start(bf16[1,1024,128]{2,1,0:T(8,128)(2,1)} %param.9) | copy-start | bytes 786436
  5.3 8.0 %copy-start = (bf16[1,1024,128]{2,1,0:T(8,128)(2,1)S(1)}, bf16[1,1024,128]{2,1,0:T(8,128)(2,1)}, u32[]{:S(2)}) copy-start(bf16[1,1024,128]{2,1,0:T(8,128)(2,1)} %param.7) | copy-start | bytes 786436
  5.3 12.9 %collective-permute-start.5 = (bf16[32,1536]{1,0:T(8,128)(2,1)S(1)}, bf16[32,1536]{1,0:T(8,128)(2,1)S(1)}, u32[]{:S(2)}, u32[]{:S(2)}) collective-permute-start(bf16[32,1536]{1,0:T(8,128)(2,1)S(1)} %get-tuple-element.47), channel_id=1, source_target_pairs={{0,16},{8,24},{16,0},{24,8},{1,17},{9,25},{17,1},{25,9},{2,18},{10... | collective-permute-start | bytes 294920 | tf_op jit(solution)/shard_map/ppermute | solution.py:390
  7.2 6.0 %copy-start.5 = (f32[1,1,1024]{2,1,0:T(1,128)S(1)}, f32[1,1,1024]{2,1,0:T(1,128)}, u32[]{:S(2)}) copy-start(f32[1,1,1024]{2,1,0:T(1,128)} %param.10) | copy-start | bytes 12292
  7.3 8.0 %collective-permute-start.4 = (bf16[144,128]{1,0:T(8,128)(2,1)S(1)}, bf16[144,128]{1,0:T(8,128)(2,1)S(1)}, u32[]{:S(2)}, u32[]{:S(2)}) collective-permute-start(bf16[144,128]{1,0:T(8,128)(2,1)S(1)} %fold.1.order_ref.refs_1_.refs_4_), channel_id=1, source_target_pairs={{0,2},{1,3},{2,4},{3,5},{4,6},{5,7},{6,0},{7,1},{8,10},{9,11},{10,... | collective-permute-start | bytes 110600 | tf_op jit(solution)/shard_map/ppermute | solution.py:390
  9.3 6.0 %collective-permute-start.3 = (bf16[144,128]{1,0:T(8,128)(2,1)S(1)}, bf16[144,128]{1,0:T(8,128)(2,1)S(1)}, u32[]{:S(2)}, u32[]{:S(2)}) collective-permute-start(bf16[144,128]{1,0:T(8,128)(2,1)S(1)} %fold.1.order_ref.refs_1_.refs_4_), channel_id=1, source_target_pairs={{0,4},{1,5},{2,6},{3,7},{4,0},{5,1},{6,2},{7,3},{8,12},{9,13},{10,... | collective-permute-start | bytes 110600 | tf_op jit(solution)/shard_map/ppermute | solution.py:390
  11.9 4.0 %collective-permute-start.2 = (bf16[144,128]{1,0:T(8,128)(2,1)S(1)}, bf16[144,128]{1,0:T(8,128)(2,1)S(1)}, u32[]{:S(2)}, u32[]{:S(2)}) collective-permute-start(bf16[144,128]{1,0:T(8,128)(2,1)S(1)} %fold.1.order_ref.refs_1_.refs_4_), channel_id=1, source_target_pairs={{0,6},{1,7},{2,0},{3,1},{4,2},{5,3},{6,4},{7,5},{8,14},{9,15},{10,... | collective-permute-start | bytes 110600 | tf_op jit(solution)/shard_map/ppermute | solution.py:390
  16.6 4.0 %collective-permute-start.6 = (bf16[128,128]{1,0:T(8,128)(2,1)S(1)}, bf16[128,128]{1,0:T(8,128)(2,1)S(1)}, u32[]{:S(2)}, u32[]{:S(2)}) collective-permute-start(bf16[128,128]{1,0:T(8,128)(2,1)S(1)} %get-tuple-element.45.order_ref.own_ref), channel_id=1, source_target_pairs={{0,1},{1,0},{2,3},{3,2},{4,5},{5,4},{6,7},{7,6},{8,9},{9,8},{10,11... | collective-permute-start | bytes 98312 | tf_op jit(solution)/shard_map/ppermute | solution.py:390
  20.6 6.2 %collective-permute-start.9 = (bf16[128,128]{1,0:T(8,128)(2,1)S(1)}, bf16[128,128]{1,0:T(8,128)(2,1)S(1)}, u32[]{:S(2)}, u32[]{:S(2)}) collective-permute-start(bf16[128,128]{1,0:T(8,128)(2,1)S(1)} %fold_back.1.order_ref), channel_id=1, source_target_pairs={{0,4},{1,5},{2,6},{3,7},{4,2},{5,3},{6,0},{7,1},{8,12},{9,13},{10,... | collective-permute-start | bytes 98312 | tf_op jit(solution)/shard_map/ppermute | solution.py:390
  21.5 5.2 %collective-permute-start.8 = (bf16[128,128]{1,0:T(8,128)(2,1)S(1)}, bf16[128,128]{1,0:T(8,128)(2,1)S(1)}, u32[]{:S(2)}, u32[]{:S(2)}) collective-permute-start(bf16[128,128]{1,0:T(8,128)(2,1)S(1)} %fold_back.1.order_ref), channel_id=1, source_target_pairs={{0,4},{1,5},{2,6},{3,7},{4,0},{5,1},{6,2},{7,3},{8,12},{9,13},{10,... | collective-permute-start | bytes 98312 | tf_op jit(solution)/shard_map/ppermute | solution.py:390
  22.4 4.7 %collective-permute-start.7 = (bf16[128,128]{1,0:T(8,128)(2,1)S(1)}, bf16[128,128]{1,0:T(8,128)(2,1)S(1)}, u32[]{:S(2)}, u32[]{:S(2)}) collective-permute-start(bf16[128,128]{1,0:T(8,128)(2,1)S(1)} %fold_back.1.order_ref), channel_id=1, source_target_pairs={{0,2},{1,3},{2,0},{3,1},{4,6},{5,7},{6,4},{7,5},{8,10},{9,11},{10,... | collective-permute-start | bytes 98312 | tf_op jit(solution)/shard_map/ppermute | solution.py:390
